TPU v7x, 128 devices: a whole 4x4x4 slice. The times are simulated.
128 devices in a mesh: wrap: 8 (over z_lo, y), span: 16 (over x, z_hi, core).
Axes of the slice: x: 4, y: 4, z: 4 (z_hi: 2, z_lo: 2; z = z_hi * 2 + z_lo), core: 2. Of those that a mesh axis runs over, the one named last changes fastest.
Arguments:
- cgrid_state: float32 [5, 256, 256, 256], P(None, 'span', 'wrap'), as said below
- cgrid_metric: float32 [3, 256, 256, 256], P(None, 'span', 'wrap'), may hold values from 0.5 to 2
- flap_state: float32 [5, 256, 96, 512], P(None, 'span', 'wrap'), as said below
- flap_metric: float32 [3, 256, 96, 512], P(None, 'span', 'wrap'), may hold values from 0.5 to 2
- iblank: int32 [256, 96, 512], P('span', 'wrap'), may hold values from 0 to 1
- fringe_from: int32 [256, 96, 512], P('span', 'wrap'), may hold values from 0 to 8191
- donor_cell: int32 [128, 8, 1024], P(('wrap', 'span')), may hold values from 0 to 118574
- donor_frac: float32 [128, 8, 3, 1024], P(('wrap', 'span')), may hold values from 0 to 1
Outputs:
- cgrid_rate: float32 [5, 256, 256, 256], P(None, 'span', 'wrap')
- flap_rate: float32 [5, 256, 96, 512], P(None, 'span', 'wrap')
Inputs may be any that keep to these rules, and one draw needn't show every extreme that they name: `cgrid_state`: component 0 (density) lies between 0.5 and 2. `flap_state`: component 0 (density) lies between 0.5 and 2.
All inputs are finite; a program needn't handle non-finite values.
Results may differ from a plain program's by a relative error of at most 0.0003.
Values sent between devices are 32-bit elements; how exact they have to be, the bound alone decides.
No kernel may reach another device: no remote copies, remote signals or barrier semaphores. Data moves between devices by JAX's collectives and lax.ppermute only.
A program may use at most 256 MiB of HBM per device.

v0:
```python
import jax
import jax.numpy as jnp
from jax import lax
from jax.sharding import PartitionSpec as P

heat_ratio = 1.4
viscosity = 0.05
conduction = 0.07
damping = 1.0 / 32.0


def extended(value, sides, width):
    for axis, dim in sides:
        size, length = (lax.axis_size(axis), value.shape[dim])
        up = [(i, (i + 1) % size) for i in range(size)]
        down = [(j, i) for i, j in up]
        last = lax.slice_in_dim(value, length - width, length, axis=dim)
        leading = lax.slice_in_dim(value, 0, width, axis=dim)
        before = lax.ppermute(last, axis, up)
        after = lax.ppermute(leading, axis, down)
        value = jnp.concatenate([before, value, after], axis=dim)
    return value


def swapped(value, axis, distance):
    mask = 2**distance
    pairs = [(source, source ^ mask) for source in range(lax.axis_size(axis))]
    return lax.ppermute(value, axis, pairs)


def primitives(state):
    density = state[0]
    velocity = state[1:4] / density
    kinetic = 0.5 * jnp.sum(velocity * velocity, axis=0)
    pressure = (heat_ratio - 1.0) * (state[4] - density * kinetic)
    return (velocity, kinetic, pressure, pressure / density)


def flux_along(state, prims, component):
    velocity, kinetic, pressure, heat = prims
    normal_speed = velocity[component - 1]
    pieces = [state[0] * normal_speed]
    for member in range(1, 4):
        flowing = state[member] * normal_speed
        if member == component:
            flowing = flowing + pressure
        pieces.append(flowing)
    pieces.append((state[4] + pressure) * normal_speed)
    return jnp.stack(pieces)


def smooth_terms(prior_one, center_prims, next_one, factor, component):
    prior_prims = primitives(prior_one)
    next_prims = primitives(next_one)
    inviscid = (
        -0.5
        * factor
        * (
            flux_along(next_one, next_prims, component)
            - flux_along(prior_one, prior_prims, component)
        )
    )
    square = factor * factor
    bend_velocity = next_prims[0] - 2.0 * center_prims[0] + prior_prims[0]
    bend_kinetic = next_prims[1] - 2.0 * center_prims[1] + prior_prims[1]
    bend_heat = next_prims[3] - 2.0 * center_prims[3] + prior_prims[3]
    viscous = jnp.concatenate(
        [
            jnp.zeros_like(factor)[None],
            viscosity * square * bend_velocity,
            (square * (viscosity * bend_kinetic + conduction * bend_heat))[None],
        ],
        axis=0,
    )
    return inviscid + viscous


def fourth_difference(prior_two, prior_one, center, next_one, next_two, factor):
    return (
        -damping * factor * (next_two - 4.0 * next_one + 6.0 * center - 4.0 * prior_one + prior_two)
    )


def rate_of(state, metric, neighbours, components):
    center_prims = primitives(state)
    total = jnp.zeros_like(state)
    for direction in range(3):
        prior_one, next_one, damp_term = neighbours[direction]
        total = total + (
            smooth_terms(
                prior_one, center_prims, next_one, metric[direction], components[direction]
            )
            + damp_term
        )
    return total


def five_point(full, center, factor, axis, count):
    prior_two = lax.slice_in_dim(full, 0, count, axis=axis)
    prior_one = lax.slice_in_dim(full, 1, count + 1, axis=axis)
    next_one = lax.slice_in_dim(full, 3, count + 3, axis=axis)
    next_two = lax.slice_in_dim(full, 4, count + 4, axis=axis)
    return (
        prior_one,
        next_one,
        fourth_difference(prior_two, prior_one, center, next_one, next_two, factor),
    )


def linear_weights(lower_pos, frac, count):
    cells = jnp.arange(count, dtype=jnp.int32)[None, :]
    low_part = jnp.where(cells == lower_pos[:, None], (1.0 - frac)[:, None], 0.0)
    high_part = jnp.where(cells == lower_pos[:, None] + 1, frac[:, None], 0.0)
    return low_part + high_part


def body(
    cgrid_state, cgrid_metric, flap_state, flap_metric, iblank, fringe_from, donor_cell, donor_frac
):
    wrap_count = lax.axis_size("wrap")
    wrap_place = lax.axis_index("wrap")
    span_cells, wrap_cells, normal_cells = cgrid_state.shape[1:]
    slot_count = donor_cell.shape[2]
    at_start = wrap_place == 0
    at_end = wrap_place == wrap_count - 1
    sign = jnp.array([1.0, -1.0, -1.0, -1.0, 1.0], jnp.float32).reshape(5, 1, 1, 1)
    corner = donor_cell.reshape(-1)
    normal_pos = corner % (normal_cells - 1)
    remainder = corner // (normal_cells - 1)
    wrap_pos = remainder % (wrap_cells - 1)
    span_pos = remainder // (wrap_cells - 1)
    fractions = donor_frac[0]
    frac_span = fractions[:, 0].reshape(-1)
    frac_wrap = fractions[:, 1].reshape(-1)
    frac_normal = fractions[:, 2].reshape(-1)
    slot_total = corner.shape[0]
    span_table = linear_weights(span_pos, frac_span, span_cells)
    wrap_table = linear_weights(wrap_pos, frac_wrap, wrap_cells)
    normal_table = linear_weights(normal_pos, frac_normal, normal_cells)
    plane_table = (span_table[:, :, None] * wrap_table[:, None, :]).reshape(
        slot_total, span_cells * wrap_cells
    )
    state_rows = jnp.transpose(cgrid_state, (1, 2, 0, 3)).reshape(
        span_cells * wrap_cells, 5 * normal_cells
    )
    plane_mixed = jnp.dot(
        plane_table, state_rows, precision=lax.Precision.HIGHEST, preferred_element_type=jnp.float32
    )
    donor_total = jnp.sum(
        plane_mixed.reshape(slot_total, 5, normal_cells) * normal_table[:, None, :], axis=2
    )
    donor_total = jnp.transpose(donor_total)
    outgoing = jnp.transpose(donor_total.reshape(5, wrap_count, slot_count), (1, 0, 2))
    incoming = lax.all_to_all(outgoing, "wrap", split_axis=0, concat_axis=0, tiled=True)
    buffer = jnp.transpose(incoming, (1, 0, 2)).reshape(5, -1)
    fringe_values = buffer[:, fringe_from]
    filled = jnp.where(iblank[None] == 1, flap_state, fringe_values)
    first = cgrid_state[:, :, 0:1]
    last = cgrid_state[:, :, -1:]
    padded = extended(cgrid_state, (("wrap", 2), ("span", 1)), 2)
    span_full = padded[:, :, 2:-2]
    wrap_mid = padded[:, 2:-2]
    low_side = jnp.where(at_start, jnp.concatenate([first, first], axis=2), wrap_mid[:, :, 0:2])
    high_side = jnp.where(at_end, jnp.concatenate([last, last], axis=2), wrap_mid[:, :, -2:])
    wrap_full = jnp.concatenate([low_side, cgrid_state, high_side], axis=2)
    span_terms = five_point(span_full, cgrid_state, cgrid_metric[0], 1, span_cells)
    wrap_terms = five_point(wrap_full, cgrid_state, cgrid_metric[1], 2, wrap_cells)
    wake_rows = jnp.transpose(cgrid_state[:, :, :, 0:2], (0, 1, 3, 2))
    partner = wake_rows[:, :, :, ::-1]
    for bit_number in range(wrap_count.bit_length() - 1):
        partner = swapped(partner, "wrap", bit_number)
    partner_cells = jnp.transpose(partner, (0, 1, 3, 2))[:, :, :, ::-1]
    wall = cgrid_state[:, :, :, 1::-1] * sign
    global_wrap = wrap_place * wrap_cells + jnp.arange(wrap_cells, dtype=jnp.int32)
    total_wrap = wrap_cells * wrap_count
    in_wake = (global_wrap < total_wrap // 4) | (global_wrap >= total_wrap - total_wrap // 4)
    lower = jnp.where(in_wake[None, None, :, None], partner_cells, wall)
    top = cgrid_state[:, :, :, -1:]
    normal_full = jnp.concatenate([lower, cgrid_state, top, top], axis=3)
    normal_terms = five_point(normal_full, cgrid_state, cgrid_metric[2], 3, normal_cells)
    cgrid_rate = rate_of(
        cgrid_state, cgrid_metric, (span_terms, wrap_terms, normal_terms), (3, 1, 2)
    )
    flap_span_cells, flap_normal_cells, flap_around_cells = filled.shape[1:]
    flap_padded = extended(filled, (("wrap", 2), ("span", 1)), 2)
    flap_span_full = flap_padded[:, :, 2:-2]
    flap_mid = flap_padded[:, 2:-2]
    flap_wall = filled[:, :, 1::-1] * sign
    flap_top = filled[:, :, -1:]
    flap_low = jnp.where(at_start, flap_wall, flap_mid[:, :, 0:2])
    flap_high = jnp.where(
        at_end, jnp.concatenate([flap_top, flap_top], axis=2), flap_mid[:, :, -2:]
    )
    flap_normal_full = jnp.concatenate([flap_low, filled, flap_high], axis=2)
    flap_span_terms = five_point(flap_span_full, filled, flap_metric[0], 1, flap_span_cells)
    flap_normal_terms = five_point(flap_normal_full, filled, flap_metric[1], 2, flap_normal_cells)
    around_prior_two = jnp.roll(filled, 2, axis=3)
    around_prior = jnp.roll(filled, 1, axis=3)
    around_next = jnp.roll(filled, -1, axis=3)
    around_next_two = jnp.roll(filled, -2, axis=3)
    flap_around_terms = (
        around_prior,
        around_next,
        fourth_difference(
            around_prior_two, around_prior, filled, around_next, around_next_two, flap_metric[2]
        ),
    )
    flap_rate = rate_of(
        filled, flap_metric, (flap_span_terms, flap_normal_terms, flap_around_terms), (3, 2, 1)
    )
    flap_rate = jnp.where(iblank[None] == 1, flap_rate, jnp.zeros_like(flap_rate))
    return (cgrid_rate, flap_rate)


def solution(mesh):
    return jax.shard_map(
        body,
        mesh=mesh,
        in_specs=(
            P(None, "span", "wrap", None),
            P(None, "span", "wrap", None),
            P(None, "span", "wrap", None),
            P(None, "span", "wrap", None),
            P("span", "wrap", None),
            P("span", "wrap", None),
            P(("wrap", "span"), None, None),
            P(("wrap", "span"), None, None, None),
        ),
        out_specs=(P(None, "span", "wrap", None), P(None, "span", "wrap", None)),
        check_vma=False,
    )
```

profile of v0, /device:TPU:0, one launch (start us, length us, event | category | flops | bytes accessed | tf_op | source)
XLA Modules:
  0.0 597.0 jit_solution(666890322197085396)
XLA Ops:
  3.1 3.5 copy.28
  7.8 2.1 copy.29
  10.2 7.8 %broadcast_multiply_fusion = f32[8192,16,32]{0,2,1:T(8,128)} fusion(f32[8192,32]{0,1:T(8,128)S(1)} %select_add_fusion.1, f32[8192,16]{0,1:T(8,128)S(1)} %select_add_fusion.2), kind=kLoop, calls=%fused_computation.26 | loop fusion | flops 4194304 | bytes 18350080 | tf_op jit(solution)/shard_map/mul | solution.py:140
  19.7 71.9 %multiply_reduce_fusion = f32[8192,5]{0,1:T(8,128)} fusion(f32[8192,256]{0,1:T(8,128)S(1)} %select_add_fusion, f32[8192,512,1]{0,1,2:T(8,128)} %bitcast.397, f32[5,256,512]{2,1,0:T(8,128)S(1)} %bitcast.406), kind=kOutput, calls=%fused_computation.1 | convolution fusion | flops 64445440000 | bytes 27951104 | tf_op jit(solution)/shard_map/dot_general | solution.py:146
  91.7 5.9 all-to-all-start
  98.3 4.1 collective-permute-start.1
  104.3 1.8 copy.39
  107.4 2.4 multiply_bitcast_fusion.10
  111.7 4.7 collective-permute-start.5
  116.5 2.7 collective-permute-done.5
  122.1 1.7 collective-permute-done.6
  125.5 3.6 copy.32
  129.2 327.4 %gather_fusion = f32[98304,5]{1,0:T(8,128)} fusion(f32[5,8192]{0,1:T(8,128)} %bitcast.396, s32[98304]{0:T(1024)S(1)} %broadcast_clamp_fusion), kind=kCustom, calls=%fused_computation | custom fusion | bytes 4325376 | tf_op jit(solution)/shard_map/gather | solution.py:156
  456.6 30.0 %copy.34 = f32[16,12,512,5]{2,0,1,3:T(8,128)} copy(f32[16,12,512,5]{3,2,1,0:T(8,128)} %bitcast.398) | data formatting | bytes 3932160 | tf_op jit(solution)/shard_map/gather | solution.py:156
  486.5 2.6 bitcast_select_fusion
  490.2 2.6 fusion.259
  494.0 3.0 collective-permute-start.8
  501.3 3.6 add_multiply_fusion
  511.8 1.8 multiply_dynamic-update-slice_fusion.6
  518.8 2.1 multiply_dynamic-update-slice_fusion.4
  522.2 1.9 multiply_dynamic-update-slice_fusion
  525.2 2.3 collective-permute-start.10
  527.5 3.1 collective-permute-start.9
  530.8 2.3 pad_maximum_fusion.3
  533.2 2.1 add_multiply_fusion.2
  538.4 2.2 multiply_dynamic-update-slice_fusion.8
  542.1 13.9 %fusion.6 = f32[5,16,32,256]{3,2,1,0:T(8,128)} fusion(f32[5,16,32,1]{3,2,1,0:T(8,128)S(1)} %copy-done.1, f32[5,16,32,256]{3,2,1,0:T(8,128)S(1)} %copy-done, f32[5,16,32,2]{3,2,1,0:T(8,128)S(1)} %copy-done.2, f32[5,16,2,256]{3,2,1,0:T(2,128)} %copy-done.7, f32[5,16,2,256]{3,2,1,0:T(2,128)S(1)} %maximum_select_fusion.1, f32[5,18,36,256]{3,2,1,0:T(8,128)} %copy-done.3, ...), kind=kLoop, calls=%fused_computation.98 | loop fusion | flops 33423360 | bytes 41252884 | tf_op jit(solution)/shard_map/add | solution.py:89
  557.2 2.4 add_multiply_fusion.3
  561.0 2.4 pad_maximum_fusion.2
  563.5 1.9 add_multiply_fusion.5
  570.7 1.7 multiply_dynamic-update-slice_fusion.12
  586.0 10.8 %fusion.34 = f32[5,16,12,512]{3,1,2,0:T(8,128)} fusion(f32[5,16,12,512]{3,1,2,0:T(8,128)S(1)} %bitcast_select_fusion, f32[5,16,12,1]{3,1,2,0:T(8,128)S(1)} %get-tuple-element.100, f32[5,16,12,1]{3,1,2,0:T(8,128)S(1)} %get-tuple-element.99, f32[5,16,2,512]{3,1,2,0:T(8,128)S(1)} %multiply_select_fusion, f32[5,16,2,512]{3,1,2,0:T(8,128)S(1)} %maximum_select_fusion, ...), kind=kLoop, calls=%fused_computation.150 | loop fusion | flops 25067520 | bytes 39288852 | tf_op jit(solution)/shard_map/jit(_where)/select_n | solution.py:211
  (202 shorter events, 62.8 us)
Async XLA Ops:
  19.7 77.8 %copy-start = (f32[5,16,32,256]{3,2,1,0:T(8,128)S(1)}, f32[5,16,32,256]{3,2,1,0:T(8,128)}, u32[]{:S(2)}) copy-start(f32[5,16,32,256]{3,2,1,0:T(8,128)} %param.9) | copy-start | bytes 7864324
  91.7 33.9 %all-to-all-start = ((f32[8,5,1024]{2,1,0:T(8,128)}), f32[8,5,1024]{2,1,0:T(8,128)}, u32[]{:S(2)}, u32[]{:S(2)}) async-start(f32[8,5,1024]{2,1,0:T(8,128)} %bitcast.34), calls=%async_computation | async-start | bytes 524288 | tf_op jit(solution)/shard_map/all_to_all | solution.py:154
  98.3 400.6 %collective-permute-start.1 = (f32[5,16,2,256]{3,2,1,0:T(2,128)}, f32[5,16,2,256]{3,2,1,0:T(2,128)}, u32[]{:S(2)}, u32[]{:S(2)}) collective-permute-start(f32[5,16,2,256]{3,2,1,0:T(2,128)} %get-tuple-element.74), channel_id=1, source_target_pairs={{16,0},{32,16},{48,32},{64,48},{80,64},{96,80},{112,96},{0,112},{1... | collective-permute-start | bytes 491528 | tf_op jit(solution)/shard_map/ppermute | solution.py:20
  103.1 3.8 copy-start.39
  103.1 395.6 %collective-permute-start = (f32[5,16,2,256]{3,1,2,0:T(8,128)}, f32[5,16,2,256]{3,1,2,0:T(8,128)}, u32[]{:S(2)}, u32[]{:S(2)}) collective-permute-start(f32[5,16,2,256]{3,1,2,0:T(8,128)} %copy.37), channel_id=1, source_target_pairs={{0,16},{16,32},{32,48},{48,64},{64,80},{80,96},{96,112},{112,0},{1... | collective-permute-start | bytes 491528 | tf_op jit(solution)/shard_map/ppermute | solution.py:19
  106.9 4.8 collective-permute-start.4
  107.3 2.5 copy-start.4
  107.4 9.1 %copy-start.40 = (s32[16,12,512]{2,0,1:T(8,128)S(1)}, s32[16,12,512]{2,0,1:T(8,128)}, u32[]{:S(2)}) copy-start(s32[16,12,512]{2,0,1:T(8,128)} %param.13) | copy-start | bytes 1179652
  111.0 12.8 %copy-start.37 = (f32[5,16,32,2]{2,1,3,0:T(8,128)S(1)}, f32[5,16,32,2]{2,1,3,0:T(8,128)}, u32[]{:S(2)}) copy-start(f32[5,16,32,2]{2,1,3,0:T(8,128)} %copy-done.36) | copy-start | bytes 61444
  111.0 12.8 %copy-start.42 = (f32[5]{0:T(128)S(1)}, f32[5]{0:T(128)}, u32[]{:S(2)}) copy-start(f32[5]{0:T(128)} %constant.92.clone) | copy-start | bytes 64
  111.7 7.4 %collective-permute-start.5 = (f32[5,16,2,32]{3,1,2,0:T(8,128)}, f32[5,16,2,32]{3,1,2,0:T(8,128)}, u32[]{:S(2)}, u32[]{:S(2)}) collective-permute-start(f32[5,16,2,32]{3,1,2,0:T(8,128)} %collective-permute-done.4), channel_id=1, source_target_pairs={{0,32},{16,48},{32,0},{48,16},{64,96},{80,112},{96,64},{112,80},{1... | collective-permute-start | bytes 61448 | tf_op jit(solution)/shard_map/ppermute | solution.py:28
  116.5 370.0 %copy-start.34 = (pred[16,12,512]{2,0,1:T(8,128)(4,1)}, pred[16,12,512]{2,0,1:T(8,128)(4,1)S(1)}, u32[]{:S(2)}) copy-start(pred[16,12,512]{2,0,1:T(8,128)(4,1)S(1)} %broadcast_compare_fusion) | copy-start | bytes 294916
  119.2 4.7 collective-permute-start.6
  494.0 30.0 %collective-permute-start.8 = (f32[5,16,2,512]{3,1,2,0:T(8,128)S(1)}, f32[5,16,2,512]{3,1,2,0:T(8,128)S(1)}, u32[]{:S(2)}, u32[]{:S(2)}) collective-permute-start(f32[5,16,2,512]{3,1,2,0:T(8,128)S(1)} %get-tuple-element.97), channel_id=1, source_target_pairs={{16,0},{32,16},{48,32},{64,48},{80,64},{96,80},{112,96},{0,112},{1... | collective-permute-start | bytes 983048 | tf_op jit(solution)/shard_map/ppermute | solution.py:20
  497.8 26.3 %collective-permute-start.7 = (f32[5,16,2,512]{3,1,2,0:T(8,128)S(1)}, f32[5,16,2,512]{3,1,2,0:T(8,128)S(1)}, u32[]{:S(2)}, u32[]{:S(2)}) collective-permute-start(f32[5,16,2,512]{3,1,2,0:T(8,128)S(1)} %get-tuple-element.98), channel_id=1, source_target_pairs={{0,16},{16,32},{32,48},{48,64},{64,80},{80,96},{96,112},{112,0},{1... | collective-permute-start | bytes 983048 | tf_op jit(solution)/shard_map/ppermute | solution.py:19
  498.9 19.9 %copy-start.7 = (f32[5,16,2,256]{3,2,1,0:T(2,128)}, f32[5,16,2,256]{3,2,1,0:T(2,128)S(1)}, u32[]{:S(2)}) copy-start(f32[5,16,2,256]{3,2,1,0:T(2,128)S(1)} %copy.25) | copy-start | bytes 491524
  516.2 2.6 copy-start.5
  517.2 13.6 %collective-permute-start.2 = (f32[5,2,36,256]{3,2,1,0:T(8,128)S(1)}, f32[5,2,36,256]{3,2,1,0:T(8,128)S(1)}, u32[]{:S(2)}, u32[]{:S(2)}) collective-permute-start(f32[5,2,36,256]{3,2,1,0:T(8,128)S(1)} %get-tuple-element.49), channel_id=1, source_target_pairs={{1,0},{2,1},{3,2},{4,3},{5,4},{6,5},{7,6},{8,7},{9,8},{10,9},{11,1... | collective-permute-start | bytes 1105928 | tf_op jit(solution)/shard_map/ppermute | solution.py:20
  518.8 12.0 %collective-permute-start.3 = (f32[5,2,36,256]{3,2,1,0:T(8,128)S(1)}, f32[5,2,36,256]{3,2,1,0:T(8,128)S(1)}, u32[]{:S(2)}, u32[]{:S(2)}) collective-permute-start(f32[5,2,36,256]{3,2,1,0:T(8,128)S(1)} %get-tuple-element.50), channel_id=1, source_target_pairs={{0,1},{1,2},{2,3},{3,4},{4,5},{5,6},{6,7},{7,8},{8,9},{9,10},{10,1... | collective-permute-start | bytes 1105928 | tf_op jit(solution)/shard_map/ppermute | solution.py:19
  524.1 6.5 %copy-start.38 = (f32[5,16,1,512]{3,1,2,0:T(8,128)S(1)}, f32[5,16,1,512]{3,1,2,0:T(8,128)}, u32[]{:S(2)}) copy-start(f32[5,16,1,512]{3,1,2,0:T(8,128)} %slice.786) | copy-start | bytes 491524
  525.2 30.7 %collective-permute-start.10 = (f32[5,2,16,512]{3,1,2,0:T(2,128)}, f32[5,2,16,512]{3,1,2,0:T(2,128)}, u32[]{:S(2)}, u32[]{:S(2)}) collective-permute-start(f32[5,2,16,512]{3,1,2,0:T(2,128)} %get-tuple-element.57), channel_id=1, source_target_pairs={{0,1},{1,2},{2,3},{3,4},{4,5},{5,6},{6,7},{7,8},{8,9},{9,10},{10,1... | collective-permute-start | bytes 983048 | tf_op jit(solution)/shard_map/ppermute | solution.py:19
  527.5 28.5 %collective-permute-start.9 = (f32[5,2,16,512]{3,1,2,0:T(2,128)}, f32[5,2,16,512]{3,1,2,0:T(2,128)}, u32[]{:S(2)}, u32[]{:S(2)}) collective-permute-start(f32[5,2,16,512]{3,1,2,0:T(2,128)} %get-tuple-element.56), channel_id=1, source_target_pairs={{1,0},{2,1},{3,2},{4,3},{5,4},{6,5},{7,6},{8,7},{9,8},{10,9},{11,1... | collective-permute-start | bytes 983048 | tf_op jit(solution)/shard_map/ppermute | solution.py:20
  533.1 5.3 copy-start.3
  561.0 2.5 copy-start.31
  581.2 3.4 copy-start.10
  581.2 3.6 copy-start.11
  581.2 4.1 copy-start.26
  581.2 4.4 copy-start.27
  581.2 4.5 copy-start.28
  581.2 4.6 copy-start.29
  581.3 4.7 copy-start.30
  581.3 4.7 copy-start.35
  (23 other events, 34.0 us)
where the time goes:
time: 608 us; the launch traced here: 597 us
  local copies, waits for them, and re-layouts  399 us (66%)
  other arithmetic  93.5 us (15%)
  matrix products  71.9 us (12%)
  starting transfers between devices  26.1 us (4%)
    gather x2, local copies, waits for them, and re-layouts, body(): fringe_values = buffer[:, fringe_from]  357 us
    dot_general x1, matrix products, body(): jnp.dot(plane_table, state_rows, precision=lax.Precision.HIGHEST, preferr...  71.9 us
    unnamed x92, local copies, waits for them, and re-layouts  19.2 us
    unnamed x39, other arithmetic  17.1 us
    add x1, other arithmetic, rate_of(): total + (smooth_terms(prior_one, center_prims, next_one, metric[direction...  13.9 us
    mul x6, other arithmetic, smooth_terms(): viscosity * square * bend_velocity  13.7 us
    another operation x8, other arithmetic, flux_along(): return jnp.stack(pieces)  12.8 us
  transfers between devices with their start and end apart: 12, of which 2 were waited for; matrix products, arithmetic and copies ran while one was open for 72% of the time, Pallas kernels for 0%

commit v1 on v0

v1 whole, which is shorter than its diff:
```python
import functools

import jax
import jax.numpy as jnp
from jax import lax
from jax.experimental import pallas as pl
from jax.experimental.pallas import tpu as pltpu
from jax.sharding import PartitionSpec as P

viscosity = 0.05
conduction = 0.07
damping = 1.0 / 32.0
VMEM_LIMIT = 56 * 1024 * 1024

f32, bf16, i32 = jnp.float32, jnp.bfloat16, jnp.int32


def whole(shape):
    return pl.BlockSpec(shape, lambda *_: (0,) * len(shape))


def params():
    return pltpu.CompilerParams(vmem_limit_bytes=VMEM_LIMIT)


def primitives(q):
    inverse = 1.0 / q[0]
    v = [q[m] * inverse for m in (1, 2, 3)]
    kinetic = 0.5 * (v[0] * v[0] + v[1] * v[1] + v[2] * v[2])
    pressure = 0.4 * (q[4] - q[0] * kinetic)
    return v + [pressure, viscosity * kinetic + conduction * (pressure * inverse)]


def flux(q, prims, m):
    u = prims[m - 1]
    f = [q[0] * u]
    for c in (1, 2, 3):
        f.append(q[c] * u + prims[3] if c == m else q[c] * u)
    f.append((q[4] + prims[3]) * u)
    return f


def pack_kernel(q_ref, wrap_lo, wrap_hi, span_lo, span_hi, wall):
    spans, rows = q_ref.shape[1], q_ref.shape[2]
    lane = lax.broadcasted_iota(i32, (rows, 128), 1)
    for c in range(5):
        for l in range(2):
            span_lo[c, l] = q_ref[c, l]
            span_hi[c, l] = q_ref[c, spans - 2 + l]
        cells = jnp.zeros((rows, 128), f32)
        for k in range(spans):
            for l in range(2):
                wrap_lo[c, l, k : k + 1, :] = q_ref[c, k, l : l + 1, :]
                wrap_hi[c, l, k : k + 1, :] = q_ref[c, k, rows - 2 + l : rows - 1 + l, :]
            near = q_ref[c, k, :, 0:128]
            if k:
                near = pltpu.roll(near, 2 * k, 1)
            cells = jnp.where(lane // 2 == k, near, cells)
        wall[c] = cells


def pack(state):
    _, spans, rows, lanes = state.shape
    shapes = [(5, 2, spans, lanes)] * 2 + [(5, 2, rows, lanes)] * 2 + [(5, rows, 128)]
    return pl.pallas_call(
        pack_kernel,
        in_specs=[whole(state.shape)],
        out_specs=[whole(s) for s in shapes],
        out_shape=[jax.ShapeDtypeStruct(s, f32) for s in shapes],
        grid=(1,),
        compiler_params=params(),
        name="cgrid_pack",
    )(state)


def rate_kernel(
    place_ref,
    q_hbm,
    major_lo,
    major_hi,
    sub_lo,
    sub_hi,
    own_lo,
    own_hi,
    wall_own,
    wall_far,
    metric_ref,
    mask_ref,
    out_ref,
    qe,
    prim,
    sub_edge,
    lane_edge,
    sems,
    *,
    cgrid,
    step_planes,
    components,
    metric_rows,
):
    planes, rows, lanes = qe.shape[1] - 4, qe.shape[2], qe.shape[3]
    step = pl.program_id(0)
    at_start = place_ref[0] == 0
    at_end = place_ref[0] == place_ref[1] - 1
    major_m, sub_m, lane_m = components

    def edge_fields(q1, q2, m, side):
        prims = primitives(q1)
        fl = flux(q1, prims, m)
        lead = [(-0.5 * side) * fl[c] + 0.125 * q1[c] - damping * q2[c] for c in range(5)]
        return lead + q1 + prims[:3] + prims[4:]

    def store_prims(k, slot):
        for i, x in enumerate(primitives([qe[c, k] for c in range(5)])):
            prim[slot, i] = x

    @pl.when(step == 0)
    def _():
        copies = [
            pltpu.make_async_copy(q_hbm, qe.at[:, pl.ds(2, planes)], sems.at[0]),
            pltpu.make_async_copy(major_lo, qe.at[:, pl.ds(0, 2)], sems.at[1]),
            pltpu.make_async_copy(major_hi, qe.at[:, pl.ds(planes + 2, 2)], sems.at[2]),
        ]
        for copy in copies:
            copy.start()
        for side, ref, own in ((-1, sub_lo, own_lo), (1, sub_hi, own_hi)):
            near, far = (1, 0) if side < 0 else (0, 1)
            q1 = [ref[c, near] for c in range(5)]
            q2 = [ref[c, far] for c in range(5)]
            if cgrid:
                edge = at_start if side < 0 else at_end
                clamp = 0 if side < 0 else 1
                q1 = [jnp.where(edge, own[c, clamp], q1[c]) for c in range(5)]
                q2 = [jnp.where(edge, own[c, clamp], q2[c]) for c in range(5)]
            for i, x in enumerate(edge_fields(q1, q2, sub_m, side)):
                sub_edge[(side + 1) // 2, i] = x
        if cgrid:
            place, count = place_ref[0], place_ref[1]
            in_wake = (place < count // 4) | (place >= count - count // 4)
            turn = 7 - lax.broadcasted_iota(i32, (8, 128), 0)
            ghosts = []
            for c in range(5):
                sign = -1.0 if c in (1, 2, 3) else 1.0
                parts = []
                for r in range(rows // 8):
                    far = wall_far[c, rows - 8 - 8 * r : rows - 8 * r, :]
                    far = jnp.take_along_axis(far, turn, axis=0, mode="promise_in_bounds")
                    parts.append(jnp.where(in_wake, far, sign * wall_own[c, 8 * r : 8 * r + 8, :]))
                ghosts.append(jnp.concatenate(parts, axis=0))
            second = [pltpu.roll(x, 127, 1) for x in ghosts]
            for i, x in enumerate(edge_fields(ghosts, second, lane_m, -1)):
                lane_edge[i] = x
        for copy in copies:
            copy.wait()
        if not cgrid:

            @pl.when(at_start)
            def _():
                for c in range(5):
                    sign = -1.0 if c in (1, 2, 3) else 1.0
                    qe[c, 1] = sign * qe[c, 2]
                    qe[c, 0] = sign * qe[c, 3]

            @pl.when(at_end)
            def _():
                for c in range(5):
                    qe[c, planes + 2] = qe[c, planes + 1]
                    qe[c, planes + 3] = qe[c, planes + 1]

        store_prims(1, 0)
        store_prims(2, 1)

    row_at = lax.broadcasted_iota(i32, (rows, lanes), 0)
    lane_at = lax.broadcasted_iota(i32, (rows, lanes), 1)
    row_first, row_last = row_at == 0, row_at == rows - 1
    lane_first, lane_last = lane_at == 0, lane_at == lanes - 1

    def one(b, _):
        k = step * step_planes + b
        here, below, above = lax.rem(k + 1, 3), lax.rem(k, 3), lax.rem(k + 2, 3)
        store_prims(k + 3, above)

        def sub_next(x, i):
            return jnp.where(row_last, sub_edge[1, i, pl.ds(k, 1), :], pltpu.roll(x, rows - 1, 0))

        def sub_prior(x, i):
            return jnp.where(row_first, sub_edge[0, i, pl.ds(k, 1), :], pltpu.roll(x, 1, 0))

        def lane_next(x):
            moved = pltpu.roll(x, lanes - 1, 1)
            return jnp.where(lane_last, x, moved) if cgrid else moved

        def lane_prior(x, i):
            moved = pltpu.roll(x, 1, 1)
            if not cgrid:
                return moved
            ghost = pltpu.roll(lane_edge[i], lax.rem(128 - 2 * k, 128), 1)
            ghost = jnp.concatenate([ghost] * (lanes // 128), axis=1)
            return jnp.where(lane_first, ghost, moved)

        gm = metric_ref[metric_rows[0], b]
        gs = metric_ref[metric_rows[1], b]
        gl = metric_ref[metric_rows[2], b]
        gm2, gs2, gl2 = gm * gm, gs * gs, gl * gl
        mine = [prim[here, i] for i in range(5)]
        viscous = {}
        for i, field, c, e in ((0, 0, 1, 10), (1, 1, 2, 11), (2, 2, 3, 12), (4, 4, 4, 13)):
            x = mine[field]
            twice = 2.0 * x
            total = gm2 * (prim[above, i] + prim[below, i] - twice)
            total += gs2 * (sub_next(x, e) + sub_prior(x, e) - twice)
            total += gl2 * (lane_next(x) + lane_prior(x, e) - twice)
            viscous[c] = total if c == 4 else viscosity * total
        q = [qe[c, k + 2] for c in range(5)]
        sub_flux = flux(q, mine, sub_m)
        lane_flux = flux(q, mine, lane_m)
        next_flux = flux([qe[c, k + 3] for c in range(5)], [prim[above, i] for i in range(5)], major_m)
        prior_flux = flux([qe[c, k + 1] for c in range(5)], [prim[below, i] for i in range(5)], major_m)
        for c in range(5):
            x = q[c]
            middle = (6.0 * damping) * x
            eighth = 0.125 * x
            bend = (
                0.125 * (qe[c, k + 3] + qe[c, k + 1])
                - damping * (qe[c, k + 4] + qe[c, k])
                - 0.5 * (next_flux[c] - prior_flux[c])
                - middle
            )
            total = gm * bend
            half = 0.5 * sub_flux[c]
            up = eighth - half - damping * sub_next(x, 5 + c)
            down = eighth + half - damping * sub_prior(x, 5 + c)
            total += gs * (sub_next(up, c) + sub_prior(down, c) - middle)
            half = 0.5 * lane_flux[c]
            up = eighth - half - damping * lane_next(x)
            down = eighth + half - damping * lane_prior(x, 5 + c)
            total += gl * (lane_next(up) + lane_prior(down, c) - middle)
            if c:
                total += viscous[c]
            if not cgrid:
                total = jnp.where(mask_ref[b] == 1, total, 0.0)
            out_ref[c, b] = total
        return 0

    lax.fori_loop(0, step_planes, one, 0)


def rate(place, q, majors, subs, owns, walls, metric, mask, *, cgrid, step_planes, components, metric_rows):
    _, planes, rows, lanes = q.shape
    anywhere = pl.BlockSpec(memory_space=pl.ANY)
    block = lambda n: pl.BlockSpec((n, step_planes, rows, lanes), lambda i: (0, i, 0, 0))
    if mask is None:
        mask = jnp.zeros((1, 8, 128), i32)
        mask_spec = whole(mask.shape)
    else:
        mask_spec = pl.BlockSpec((step_planes, rows, lanes), lambda i: (i, 0, 0))
    return pl.pallas_call(
        functools.partial(
            rate_kernel,
            cgrid=cgrid,
            step_planes=step_planes,
            components=components,
            metric_rows=metric_rows,
        ),
        grid=(planes // step_planes,),
        in_specs=[pl.BlockSpec(memory_space=pltpu.SMEM), anywhere, anywhere, anywhere]
        + [whole(x.shape) for x in (*subs, *owns, *walls)]
        + [block(3), mask_spec],
        out_specs=block(5),
        out_shape=jax.ShapeDtypeStruct(q.shape, f32),
        scratch_shapes=[
            pltpu.VMEM((5, planes + 4, rows, lanes), f32),
            pltpu.VMEM((3, 5, rows, lanes), f32),
            pltpu.VMEM((2, 14, planes, lanes), f32),
            pltpu.VMEM((14, rows, 128), f32),
            pltpu.SemaphoreType.DMA((3,)),
        ],
        compiler_params=params(),
        cost_estimate=pl.CostEstimate(
            flops=300 * planes * rows * lanes, bytes_accessed=60 * planes * rows * lanes, transcendentals=0
        ),
        name="cgrid_rate" if cgrid else "flap_rate",
    )(place, q, *majors, *subs, *owns, *walls, metric, mask)


def split_two(x):
    high = x.astype(bf16)
    return high, (x - high.astype(f32)).astype(bf16)


def donor_kernel(cell_ref, frac_ref, q_ref, out_ref, table, *, tile):
    spans, rows, lanes = q_ref.shape[1:]
    slots = cell_ref.shape[1]

    @pl.when(pl.program_id(0) == 0)
    def _():
        def prepare(k, _):
            for c in range(5):
                high, low = split_two(q_ref[c, k])
                here = slice(c * rows, (c + 1) * rows)
                table[k, here, 0:lanes] = high
                table[k, here, lanes : 2 * lanes] = low
                table[k, here, 2 * lanes : 3 * lanes] = high
            return 0

        lax.fori_loop(0, spans, prepare, 0)

    part = pl.program_id(0)
    per = slots // tile
    w = part // per
    t0 = pl.multiple_of((part % per) * tile, 128)
    cell = cell_ref[pl.ds(w, 1), pl.ds(t0, tile)]
    f0, f1, f2 = [frac_ref[d, pl.ds(w, 1), pl.ds(t0, tile)] for d in range(3)]
    upper = jnp.floor((cell.astype(f32) + 0.5) * (1.0 / (lanes - 1)))
    span = jnp.floor((upper + 0.5) * (1.0 / (rows - 1)))
    wrap = (upper - span * (rows - 1)).astype(i32)
    normal = cell - upper.astype(i32) * (lanes - 1)
    span = span.astype(i32)

    def weights(count, at, frac):
        cells = lax.broadcasted_iota(i32, (count, tile), 0)
        return jnp.where(cells == at, 1.0 - frac, jnp.where(cells == at + 1, frac, 0.0))

    high, low = split_two(weights(lanes, normal, f2))
    along = jnp.concatenate([high, high, low], axis=0)
    across = weights(rows, wrap, f1)

    def plane(k, sums):
        mixed = jnp.dot(table[k], along, preferred_element_type=f32)
        ws = jnp.where(span == k, 1.0 - f0, jnp.where(span + 1 == k, f0, 0.0))
        new = []
        for c in range(5):
            total = mixed[c * rows : c * rows + 8] * across[0:8]
            for r in range(8, rows, 8):
                total += mixed[c * rows + r : c * rows + r + 8] * across[r : r + 8]
            new.append(sums[c] + ws * total)
        return tuple(new)

    sums = lax.fori_loop(0, spans, plane, tuple(jnp.zeros((8, tile), f32) for _ in range(5)), unroll=4)
    for c in range(5):
        out_ref[w, c : c + 1, pl.ds(t0, tile)] = jnp.sum(sums[c], axis=0, keepdims=True)


def donors(cell, frac, state, tile=256):
    _, spans, rows, lanes = state.shape
    count, slots = cell.shape
    return pl.pallas_call(
        functools.partial(donor_kernel, tile=tile),
        grid=(count * slots // tile,),
        in_specs=[whole(cell.shape), whole(frac.shape), whole(state.shape)],
        out_specs=whole((count, 5, slots)),
        out_shape=jax.ShapeDtypeStruct((count, 5, slots), f32),
        scratch_shapes=[pltpu.VMEM((spans, 5 * rows, 3 * lanes), bf16)],
        compiler_params=params(),
        name="donors",
    )(cell, frac, state)


def fill_kernel(from_ref, mask_ref, q_ref, slot_ref, out_ref, norm_lo, norm_hi, span_lo, span_hi, table):
    planes = pl.num_programs(0)
    rows, lanes = from_ref.shape[1:]
    low = 256
    highs = table.shape[0] // 10
    j = pl.program_id(0)

    @pl.when(j == 0)
    def _():
        per = slot_ref.shape[2] // low
        for c in range(5):
            for w in range(slot_ref.shape[0]):
                for r in range(per):
                    value = slot_ref[w, c : c + 1, r * low : (r + 1) * low]
                    table[c * highs + w * per + r : c * highs + w * per + r + 1, :] = value
        for r in range(0, 5 * highs, 8):
            value = table[r : r + 8, :]
            table[5 * highs + r : 5 * highs + r + 8, :] = value - value.astype(bf16).astype(f32)

    both = table[...].astype(bf16)
    sub = lax.broadcasted_iota(i32, (8, lanes), 0)
    cells = lax.broadcasted_iota(i32, (low, lanes), 0).astype(f32).astype(bf16)
    one, zero = jnp.ones((), bf16), jnp.zeros((), bf16)

    def row(s, _):
        at = from_ref[0, pl.ds(s, 1), :]
        pick = jnp.where(cells == (at & (low - 1)).astype(f32).astype(bf16), one, zero)
        high = at // low
        found = jnp.dot(both, pick, preferred_element_type=f32)
        masks = [sub + 8 * g == high for g in range(highs // 8)]
        keep = mask_ref[0, pl.ds(s, 1), :] == 1
        for c in range(5):
            value = None
            for g, mask in enumerate(masks):
                r = c * highs + 8 * g
                piece = found[r : r + 8] + found[5 * highs + r : 5 * highs + r + 8]
                value = jnp.where(mask, piece, 0.0 if value is None else value)
            value = jnp.sum(value, axis=0, keepdims=True)
            out_ref[c, 0, pl.ds(s, 1), :] = jnp.where(keep, q_ref[c, 0, pl.ds(s, 1), :], value)
        return 0

    lax.fori_loop(0, rows, row, 0, unroll=16)

    for c in range(5):
        for l in range(2):
            span_lo[c, l, pl.ds(j, 1), :] = out_ref[c, 0, l : l + 1, :]
            span_hi[c, l, pl.ds(j, 1), :] = out_ref[c, 0, rows - 2 + l : rows - 1 + l, :]

    @pl.when(j < 2)
    def _():
        for c in range(5):
            norm_lo[c, j] = out_ref[c, 0]

    @pl.when(j >= planes - 2)
    def _():
        for c in range(5):
            norm_hi[c, j - (planes - 2)] = out_ref[c, 0]


def fill(source, mask, state, slot):
    _, planes, rows, lanes = state.shape
    count, _, slots = slot.shape
    plane = pl.BlockSpec((1, rows, lanes), lambda j: (j, 0, 0))
    state_plane = pl.BlockSpec((5, 1, rows, lanes), lambda j: (0, j, 0, 0))
    edges = [(5, 2, rows, lanes)] * 2 + [(5, 2, planes, lanes)] * 2
    return pl.pallas_call(
        fill_kernel,
        grid=(planes,),
        in_specs=[plane, plane, state_plane, whole(slot.shape)],
        out_specs=[state_plane] + [whole(s) for s in edges],
        out_shape=[jax.ShapeDtypeStruct(s, f32) for s in [state.shape] + edges],
        scratch_shapes=[pltpu.VMEM((10 * count * slots // 256, 256), f32)],
        compiler_params=params(),
        cost_estimate=pl.CostEstimate(flops=24 * 10**9, bytes_accessed=6 * 10**6, transcendentals=0),
        name="fill",
    )(source, mask, state, slot)


def body(
    cgrid_state, cgrid_metric, flap_state, flap_metric, iblank, fringe_from, donor_cell, donor_frac
):
    wrap_count, span_count = lax.axis_size("wrap"), lax.axis_size("span")
    place = jnp.stack([lax.axis_index("wrap"), jnp.int32(wrap_count)]).astype(i32)

    def onward(value, axis):
        size = lax.axis_size(axis)
        return lax.ppermute(value, axis, [(i, (i + 1) % size) for i in range(size)])

    def back(value, axis):
        size = lax.axis_size(axis)
        return lax.ppermute(value, axis, [((i + 1) % size, i) for i in range(size)])

    wrap_lo, wrap_hi, span_lo, span_hi, wall = pack(cgrid_state)
    far = lax.ppermute(
        wall[:, :, 0:32], "wrap", [(i, wrap_count - 1 - i) for i in range(wrap_count)]
    )
    far = jnp.pad(far, ((0, 0), (0, 0), (0, 96)))
    majors = (onward(span_hi, "span"), back(span_lo, "span"))
    subs = (onward(wrap_hi, "wrap"), back(wrap_lo, "wrap"))

    slot = donors(donor_cell[0], jnp.transpose(donor_frac[0], (1, 0, 2)), cgrid_state)
    slot = lax.all_to_all(slot, "wrap", split_axis=0, concat_axis=0, tiled=True)

    turned = lambda x: jnp.swapaxes(x, -3, -2)
    mask = turned(iblank)
    filled, norm_lo, norm_hi, edge_lo, edge_hi = fill(turned(fringe_from), mask, turned(flap_state), slot)
    flap_majors = (onward(norm_hi, "wrap"), back(norm_lo, "wrap"))
    flap_subs = (onward(edge_hi, "span"), back(edge_lo, "span"))

    cgrid_rate = rate(
        place,
        cgrid_state,
        majors,
        subs,
        (wrap_lo, wrap_hi),
        (wall, far),
        cgrid_metric,
        None,
        cgrid=True,
        step_planes=4,
        components=(3, 1, 2),
        metric_rows=(0, 1, 2),
    )
    none = jnp.zeros((5, 8, 128), f32)
    flap_rate = rate(
        place,
        filled,
        flap_majors,
        flap_subs,
        (none, none),
        (none, none),
        turned(flap_metric),
        mask,
        cgrid=False,
        step_planes=3,
        components=(2, 3, 1),
        metric_rows=(1, 0, 2),
    )
    return (cgrid_rate, turned(flap_rate))


def solution(mesh):
    return jax.shard_map(
        body,
        mesh=mesh,
        in_specs=(
            P(None, "span", "wrap", None),
            P(None, "span", "wrap", None),
            P(None, "span", "wrap", None),
            P(None, "span", "wrap", None),
            P("span", "wrap", None),
            P("span", "wrap", None),
            P(("wrap", "span"), None, None),
            P(("wrap", "span"), None, None, None),
        ),
        out_specs=(P(None, "span", "wrap", None), P(None, "span", "wrap", None)),
        check_vma=False,
    )
```

time: 608 us -> 149 us (0.25); the launches traced: 597 us -> 149 us
  local copies, waits for them, and re-layouts: 399 us -> 3.08 us
  Pallas kernels: 0 us -> 115 us
  other arithmetic: 93.5 us -> 0.59 us
  matrix products: 71.9 us -> 0 us
    gather x2 -> x0, local copies, waits for them, and re-layouts: 357 us -> none  [body(): fringe_values = buffer[:, fringe_from]]
    pallas_call x0 -> x5, Pallas kernels: none -> 115 us  [the longest x1 64.6 us: donors(): pl.pallas_call(functools.partial(donor_kernel, tile=tile), grid=(count *...]
    dot_general x1 -> x0, matrix products: 71.9 us -> none  [body(): jnp.dot(plane_table, state_rows, precision=lax.Precision.HIGHEST, preferr...]
    mul x7 -> x0, other arithmetic: 21.5 us -> none  [the longest x6 13.7 us: smooth_terms(): viscosity * square * bend_velocity]
    unnamed x92 -> x18, local copies, waits for them, and re-layouts: 19.2 us -> 1.12 us
    unnamed x39 -> x0, other arithmetic: 17.1 us -> none
    add x5 -> x0, other arithmetic: 15.6 us -> none  [the longest x1 13.9 us: rate_of(): total + (smooth_terms(prior_one, center_prims, next_one, metric[direction...]
    select_n x8 -> x0, other arithmetic: 14.8 us -> none  [the longest x1 10.8 us: body(): jnp.where(iblank[None] == 1, flap_rate, jnp.zeros_like(flap_rate))]
  transfers between devices with their start and end apart: 12 -> 10, of which waited for: 2 -> 0; matrix products, arithmetic and copies ran while one was open for 72% -> 1% of each run, Pallas kernels for 0% -> 27%
where the time goes in v1:
time: 149 us
  Pallas kernels  115 us (77%)
  starting transfers between devices  29.1 us (20%)
  local copies, waits for them, and re-layouts  3.08 us (2%)
    pallas_call x1, Pallas kernels, donors(): pl.pallas_call(functools.partial(donor_kernel, tile=tile), grid=(count *...  64.6 us
    pallas_call x2, Pallas kernels, rate(): pl.pallas_call(functools.partial(rate_kernel, cgrid=cgrid, step_planes=st...  25.4 us
    pallas_call x1, Pallas kernels, fill(): pl.pallas_call(fill_kernel, grid=(planes,), in_specs=[plane, plane, state...  22.1 us
    ppermute x4, starting transfers between devices, back(): return lax.ppermute(value, axis, [((i + 1) % size, i) for i in range(size)])  18.7 us
    all_to_all x1, starting transfers between devices, body(): slot = lax.all_to_all(slot, 'wrap', split_axis=0, concat_axis=0, tiled=True)  5.91 us
    ppermute x1, starting transfers between devices, body(): lax.ppermute(wall[:, :, 0:32], 'wrap', [(i, wrap_count - 1 - i) for i in...  4.13 us
    pallas_call x1, Pallas kernels, pack(): pl.pallas_call(pack_kernel, in_specs=[whole(state.shape)], out_specs=[who...  3.1 us
  transfers between devices with their start and end apart: 10, of which 0 were waited for; matrix products, arithmetic and copies ran while one was open for 1% of the time, Pallas kernels for 27%

profile of v1, /device:TPU:0, one launch (start us, length us, event | category | flops | bytes accessed | tf_op | source)
XLA Modules:
  0.0 148.8 jit_solution(7107448274604404632)
XLA Ops:
  0.6 64.6 %donors.1 = f32[8,5,1024]{2,1,0:T(8,128)} custom-call(s32[8,1024]{1,0:T(8,128)} %bitcast.17, f32[3,8,1024]{2,1,0:T(8,128)} %bitcast.15, f32[5,16,32,256]{3,2,1,0:T(8,128)} %q_ref.3), custom_call_target="tpu_custom_call" | custom-call | tf_op jit(solution)/shard_map/donors/pallas_call | solution.py:347
  65.2 5.9 %all-to-all-start = ((f32[8,5,1024]{2,1,0:T(8,128)}), f32[8,5,1024]{2,1,0:T(8,128)S(1)}, u32[]{:S(2)}, u32[]{:S(2)}) async-start(f32[8,5,1024]{2,1,0:T(8,128)} %donors.1), calls=%async_computation | async-start | bytes 524288 | tf_op jit(solution)/shard_map/all_to_all | solution.py:460
  71.1 3.1 %cgrid_pack.1 = (f32[5,2,16,256]{3,2,1,0:T(8,128)}, f32[5,2,16,256]{3,2,1,0:T(8,128)}, f32[5,2,32,256]{3,2,1,0:T(8,128)}, f32[5,2,32,256]{3,2,1,0:T(8,128)}, f32[5,32,128]{2,1,0:T(8,128)}) custom-call(f32[5,16,32,256]{3,2,1,0:T(8,128)} %q_ref.3), custom_call_target="tpu_custom_call" | custom-call | tf_op jit(solution)/shard_map/cgrid_pack/pallas_call | solution.py:65
  74.2 4.1 %collective-permute-start.4 = (f32[5,32,32]{2,1,0:T(8,128)}, f32[5,32,32]{2,1,0:T(8,128)S(1)}, u32[]{:S(2)}, u32[]{:S(2)}) collective-permute-start(f32[5,32,32]{2,1,0:T(8,128)} %bitcast.16), channel_id=1, source_target_pairs={{0,112},{16,96},{32,80},{48,64},{64,48},{80,32},{96,16},{112,0},{1... | collective-permute-start | bytes 61448 | tf_op jit(solution)/shard_map/ppermute | solution.py:452
  78.4 0.3 collective-permute-start.2
  78.6 3.9 %collective-permute-start.3 = (f32[5,2,16,256]{3,2,1,0:T(8,128)}, f32[5,2,16,256]{3,2,1,0:T(8,128)S(1)}, u32[]{:S(2)}, u32[]{:S(2)}) collective-permute-start(f32[5,2,16,256]{3,2,1,0:T(8,128)} %get-tuple-element.15.own_lo), channel_id=1, source_target_pairs={{16,0},{32,16},{48,32},{64,48},{80,64},{96,80},{112,96},{0,112},{1... | collective-permute-start | bytes 491528 | tf_op jit(solution)/shard_map/ppermute | solution.py:449
  82.5 0.0 collective-permute-start
  82.5 5.4 %collective-permute-start.1 = (f32[5,2,32,256]{3,2,1,0:T(8,128)}, f32[5,2,32,256]{3,2,1,0:T(8,128)S(1)}, u32[]{:S(2)}, u32[]{:S(2)}) collective-permute-start(f32[5,2,32,256]{3,2,1,0:T(8,128)} %get-tuple-element.13), channel_id=1, source_target_pairs={{1,0},{2,1},{3,2},{4,3},{5,4},{6,5},{7,6},{8,7},{9,8},{10,9},{11,1... | collective-permute-start | bytes 983048 | tf_op jit(solution)/shard_map/ppermute | solution.py:449
  87.9 0.0 all-to-all-done.slot_ref
  87.9 0.7 copy-done.6
  88.6 22.1 %fill.1 = (f32[5,12,16,512]{3,2,1,0:T(8,128)}, f32[5,2,16,512]{3,2,1,0:T(8,128)}, f32[5,2,16,512]{3,2,1,0:T(8,128)}, f32[5,2,12,512]{3,2,1,0:T(8,128)}, f32[5,2,12,512]{3,2,1,0:T(8,128)}) custom-call(s32[12,16,512]{2,1,0:T(8,128)} %bitcast.19, s32[12,16,512]{2,1,0:T(8,128)} %bitcast.13, f32[5,12,16,512]{3,2,1,0:T(8,128)} %bitcast.18, f32[8,5,1024]{2,1,0:T(8,128)} %copy-done.6), custom_call_target="tpu_custom_call" | custom-call | flops 24000000000 | bytes 6000000 | tf_op jit(solution)/shard_map/fill/pallas_call | solution.py:424
  110.7 0.0 collective-permute-done.4
  110.7 0.1 collective-permute-start.5
  110.8 0.0 collective-permute-done.2.sub_lo
  110.8 4.1 %collective-permute-start.6 = (f32[5,2,16,512]{3,2,1,0:T(8,128)}, f32[5,2,16,512]{3,2,1,0:T(8,128)S(1)}, u32[]{:S(2)}, u32[]{:S(2)}) collective-permute-start(f32[5,2,16,512]{3,2,1,0:T(8,128)} %get-tuple-element.19), channel_id=1, source_target_pairs={{16,0},{32,16},{48,32},{64,48},{80,64},{96,80},{112,96},{0,112},{1... | collective-permute-start | bytes 983048 | tf_op jit(solution)/shard_map/ppermute | solution.py:449
  114.9 0.0 collective-permute-done.3.sub_hi
  115.0 0.0 collective-permute-start.7
  115.0 0.0 collective-permute-done.major_lo
  115.0 5.3 %collective-permute-start.8 = (f32[5,2,12,512]{3,2,1,0:T(8,128)}, f32[5,2,12,512]{3,2,1,0:T(8,128)S(1)}, u32[]{:S(2)}, u32[]{:S(2)}) collective-permute-start(f32[5,2,12,512]{3,2,1,0:T(8,128)} %get-tuple-element.21), channel_id=1, source_target_pairs={{1,0},{2,1},{3,2},{4,3},{5,4},{6,5},{7,6},{8,7},{9,8},{10,9},{11,1... | collective-permute-start | bytes 737288 | tf_op jit(solution)/shard_map/ppermute | solution.py:449
  120.3 0.6 pad_add_fusion.place_ref
  120.9 0.6 pad.4.wall_far
  121.6 0.0 collective-permute-done.1.major_hi
  121.6 0.6 broadcast_in_dim.6.mask_ref
  122.2 0.1 copy-done.5
  122.3 14.6 %cgrid_rate.1 = f32[5,16,32,256]{3,2,1,0:T(8,128)} custom-call(s32[2]{0:T(128)} %pad_add_fusion.place_ref, f32[5,16,32,256]{3,2,1,0:T(8,128)} %q_ref.3, f32[5,2,32,256]{3,2,1,0:T(8,128)} %copy-done.4, f32[5,2,32,256]{3,2,1,0:T(8,128)} %copy-done.5, f32[5,2,16,256]{3,2,1,0:T(8,128)} %copy-done.7, f32[5,2,16,256]{3,2,1,0:T(8,128)} %copy-done.8, ...), custom_call_target="tpu_custom_call" | custom-call | flops 39321600 | bytes 7864320 | tf_op jit(solution)/shard_map/cgrid_rate/pallas_call | solution.py:257
  136.9 0.0 collective-permute-done.7.sub_lo
  136.9 0.0 collective-permute-done.6.major_hi
  136.9 0.7 broadcast_in_dim.7.own_lo.own_hi.wall_own.wall_far
  137.6 0.1 copy-done.3
  137.7 0.1 copy-done
  137.8 0.1 copy-done.1
  137.9 10.9 %flap_rate.1 = f32[5,12,16,512]{3,2,1,0:T(8,128)} custom-call(s32[2]{0:T(128)} %pad_add_fusion.place_ref, f32[5,12,16,512]{3,2,1,0:T(8,128)} %get-tuple-element.17.q_hbm, f32[5,2,16,512]{3,2,1,0:T(8,128)} %copy-done, f32[5,2,16,512]{3,2,1,0:T(8,128)} %copy-done.1, f32[5,2,12,512]{3,2,1,0:T(8,128)} %copy-done.2, f32[5,2,12,512]{3,2,1,0:T(8,128)} %copy-done.3, ...), custom_call_target="tpu_custom_call" | custom-call | flops 29491200 | bytes 5898240 | tf_op jit(solution)/shard_map/flap_rate/pallas_call | solution.py:257
  (15 shorter events, 0.0 us)
Async XLA Ops:
  65.2 22.6 %all-to-all-start = ((f32[8,5,1024]{2,1,0:T(8,128)}), f32[8,5,1024]{2,1,0:T(8,128)S(1)}, u32[]{:S(2)}, u32[]{:S(2)}) async-start(f32[8,5,1024]{2,1,0:T(8,128)} %donors.1), calls=%async_computation | async-start | bytes 524288 | tf_op jit(solution)/shard_map/all_to_all | solution.py:460
  74.2 36.5 %collective-permute-start.4 = (f32[5,32,32]{2,1,0:T(8,128)}, f32[5,32,32]{2,1,0:T(8,128)S(1)}, u32[]{:S(2)}, u32[]{:S(2)}) collective-permute-start(f32[5,32,32]{2,1,0:T(8,128)} %bitcast.16), channel_id=1, source_target_pairs={{0,112},{16,96},{32,80},{48,64},{64,48},{80,32},{96,16},{112,0},{1... | collective-permute-start | bytes 61448 | tf_op jit(solution)/shard_map/ppermute | solution.py:452
  78.4 32.4 %collective-permute-start.2 = (f32[5,2,16,256]{3,2,1,0:T(8,128)}, f32[5,2,16,256]{3,2,1,0:T(8,128)S(1)}, u32[]{:S(2)}, u32[]{:S(2)}) collective-permute-start(f32[5,2,16,256]{3,2,1,0:T(8,128)} %get-tuple-element.14.own_hi), channel_id=1, source_target_pairs={{0,16},{16,32},{32,48},{48,64},{64,80},{80,96},{96,112},{112,0},{1... | collective-permute-start | bytes 491528 | tf_op jit(solution)/shard_map/ppermute | solution.py:445
  78.6 36.3 %collective-permute-start.3 = (f32[5,2,16,256]{3,2,1,0:T(8,128)}, f32[5,2,16,256]{3,2,1,0:T(8,128)S(1)}, u32[]{:S(2)}, u32[]{:S(2)}) collective-permute-start(f32[5,2,16,256]{3,2,1,0:T(8,128)} %get-tuple-element.15.own_lo), channel_id=1, source_target_pairs={{16,0},{32,16},{48,32},{64,48},{80,64},{96,80},{112,96},{0,112},{1... | collective-permute-start | bytes 491528 | tf_op jit(solution)/shard_map/ppermute | solution.py:449
  82.5 32.4 %collective-permute-start = (f32[5,2,32,256]{3,2,1,0:T(8,128)}, f32[5,2,32,256]{3,2,1,0:T(8,128)S(1)}, u32[]{:S(2)}, u32[]{:S(2)}) collective-permute-start(f32[5,2,32,256]{3,2,1,0:T(8,128)} %get-tuple-element.12), channel_id=1, source_target_pairs={{0,1},{1,2},{2,3},{3,4},{4,5},{5,6},{6,7},{7,8},{8,9},{9,10},{10,1... | collective-permute-start | bytes 983048 | tf_op jit(solution)/shard_map/ppermute | solution.py:445
  82.5 39.0 %collective-permute-start.1 = (f32[5,2,32,256]{3,2,1,0:T(8,128)}, f32[5,2,32,256]{3,2,1,0:T(8,128)S(1)}, u32[]{:S(2)}, u32[]{:S(2)}) collective-permute-start(f32[5,2,32,256]{3,2,1,0:T(8,128)} %get-tuple-element.13), channel_id=1, source_target_pairs={{1,0},{2,1},{3,2},{4,3},{5,4},{6,5},{7,6},{8,7},{9,8},{10,9},{11,1... | collective-permute-start | bytes 983048 | tf_op jit(solution)/shard_map/ppermute | solution.py:449
  87.9 0.7 copy-start.6
  110.7 26.2 %collective-permute-start.5 = (f32[5,2,16,512]{3,2,1,0:T(8,128)}, f32[5,2,16,512]{3,2,1,0:T(8,128)S(1)}, u32[]{:S(2)}, u32[]{:S(2)}) collective-permute-start(f32[5,2,16,512]{3,2,1,0:T(8,128)} %get-tuple-element.18), channel_id=1, source_target_pairs={{0,16},{16,32},{32,48},{48,64},{64,80},{80,96},{96,112},{112,0},{1... | collective-permute-start | bytes 983048 | tf_op jit(solution)/shard_map/ppermute | solution.py:445
  110.8 11.4 %copy-start.7 = (f32[5,2,16,256]{3,2,1,0:T(8,128)}, f32[5,2,16,256]{3,2,1,0:T(8,128)S(1)}, u32[]{:S(2)}) copy-start(f32[5,2,16,256]{3,2,1,0:T(8,128)S(1)} %collective-permute-done.2.sub_lo) | copy-start | bytes 491524
  110.8 26.1 %collective-permute-start.6 = (f32[5,2,16,512]{3,2,1,0:T(8,128)}, f32[5,2,16,512]{3,2,1,0:T(8,128)S(1)}, u32[]{:S(2)}, u32[]{:S(2)}) collective-permute-start(f32[5,2,16,512]{3,2,1,0:T(8,128)} %get-tuple-element.19), channel_id=1, source_target_pairs={{16,0},{32,16},{48,32},{64,48},{80,64},{96,80},{112,96},{0,112},{1... | collective-permute-start | bytes 983048 | tf_op jit(solution)/shard_map/ppermute | solution.py:449
  115.0 7.2 %copy-start.8 = (f32[5,2,16,256]{3,2,1,0:T(8,128)}, f32[5,2,16,256]{3,2,1,0:T(8,128)S(1)}, u32[]{:S(2)}) copy-start(f32[5,2,16,256]{3,2,1,0:T(8,128)S(1)} %collective-permute-done.3.sub_hi) | copy-start | bytes 491524
  115.0 21.9 %collective-permute-start.7 = (f32[5,2,12,512]{3,2,1,0:T(8,128)}, f32[5,2,12,512]{3,2,1,0:T(8,128)S(1)}, u32[]{:S(2)}, u32[]{:S(2)}) collective-permute-start(f32[5,2,12,512]{3,2,1,0:T(8,128)} %get-tuple-element.20), channel_id=1, source_target_pairs={{0,1},{1,2},{2,3},{3,4},{4,5},{5,6},{6,7},{7,8},{8,9},{9,10},{10,1... | collective-permute-start | bytes 737288 | tf_op jit(solution)/shard_map/ppermute | solution.py:445
  115.0 7.2 %copy-start.4 = (f32[5,2,32,256]{3,2,1,0:T(8,128)}, f32[5,2,32,256]{3,2,1,0:T(8,128)S(1)}, u32[]{:S(2)}) copy-start(f32[5,2,32,256]{3,2,1,0:T(8,128)S(1)} %collective-permute-done.major_lo) | copy-start | bytes 983044
  115.0 21.9 %collective-permute-start.8 = (f32[5,2,12,512]{3,2,1,0:T(8,128)}, f32[5,2,12,512]{3,2,1,0:T(8,128)S(1)}, u32[]{:S(2)}, u32[]{:S(2)}) collective-permute-start(f32[5,2,12,512]{3,2,1,0:T(8,128)} %get-tuple-element.21), channel_id=1, source_target_pairs={{1,0},{2,1},{3,2},{4,3},{5,4},{6,5},{7,6},{8,7},{9,8},{10,9},{11,1... | collective-permute-start | bytes 737288 | tf_op jit(solution)/shard_map/ppermute | solution.py:449
  121.6 0.7 copy-start.5
  136.9 0.8 copy-start.2
  136.9 0.8 copy-start.3
  136.9 0.9 copy-start
  136.9 1.0 copy-start.1

commit v2 on v1

--- a/solution.py
+++ b/solution.py
@@ -11,6 +11,7 @@
 conduction = 0.07
 damping = 1.0 / 32.0
 VMEM_LIMIT = 56 * 1024 * 1024
+GROUP = 8
 
 f32, bf16, i32 = jnp.float32, jnp.bfloat16, jnp.int32
 
@@ -56,12 +57,12 @@
             if k:
                 near = pltpu.roll(near, 2 * k, 1)
             cells = jnp.where(lane // 2 == k, near, cells)
-        wall[c] = cells
+        wall[c] = cells[:, 0 : 2 * spans]
 
 
 def pack(state):
     _, spans, rows, lanes = state.shape
-    shapes = [(5, 2, spans, lanes)] * 2 + [(5, 2, rows, lanes)] * 2 + [(5, rows, 128)]
+    shapes = [(5, 2, spans, lanes)] * 2 + [(5, 2, rows, lanes)] * 2 + [(5, rows, 2 * spans)]
     return pl.pallas_call(
         pack_kernel,
         in_specs=[whole(state.shape)],
@@ -74,34 +75,27 @@
 
 
 def rate_kernel(
-    place_ref,
     q_hbm,
     major_lo,
     major_hi,
     sub_lo,
     sub_hi,
-    own_lo,
-    own_hi,
-    wall_own,
-    wall_far,
-    metric_ref,
-    mask_ref,
-    out_ref,
-    qe,
-    prim,
-    sub_edge,
-    lane_edge,
-    sems,
-    *,
+    *refs,
     cgrid,
     step_planes,
     components,
     metric_rows,
 ):
+    if cgrid:
+        own_lo, own_hi, wall_own, wall_far, metric_ref, out_ref, qe, prim, sub_edge, lane_edge, sems = refs
+    else:
+        own_lo = own_hi = None
+        mask_ref, metric_ref, out_ref, qe, prim, sub_edge, sems = refs
     planes, rows, lanes = qe.shape[1] - 4, qe.shape[2], qe.shape[3]
     step = pl.program_id(0)
-    at_start = place_ref[0] == 0
-    at_end = place_ref[0] == place_ref[1] - 1
+    place, count = lax.axis_index("wrap"), lax.axis_size("wrap")
+    at_start = place == 0
+    at_end = place == count - 1
     major_m, sub_m, lane_m = components
 
     def edge_fields(q1, q2, m, side):
@@ -135,7 +129,6 @@
             for i, x in enumerate(edge_fields(q1, q2, sub_m, side)):
                 sub_edge[(side + 1) // 2, i] = x
         if cgrid:
-            place, count = place_ref[0], place_ref[1]
             in_wake = (place < count // 4) | (place >= count - count // 4)
             turn = 7 - lax.broadcasted_iota(i32, (8, 128), 0)
             ghosts = []
@@ -144,8 +137,11 @@
                 parts = []
                 for r in range(rows // 8):
                     far = wall_far[c, rows - 8 - 8 * r : rows - 8 * r, :]
+                    own = wall_own[c, 8 * r : 8 * r + 8, :]
+                    own = jnp.concatenate([own, jnp.zeros((8, 128 - own.shape[1]), f32)], axis=1)
+                    far = jnp.concatenate([far, jnp.zeros((8, 128 - far.shape[1]), f32)], axis=1)
                     far = jnp.take_along_axis(far, turn, axis=0, mode="promise_in_bounds")
-                    parts.append(jnp.where(in_wake, far, sign * wall_own[c, 8 * r : 8 * r + 8, :]))
+                    parts.append(jnp.where(in_wake, far, sign * own))
                 ghosts.append(jnp.concatenate(parts, axis=0))
             second = [pltpu.roll(x, 127, 1) for x in ghosts]
             for i, x in enumerate(edge_fields(ghosts, second, lane_m, -1)):
@@ -245,15 +241,15 @@
     lax.fori_loop(0, step_planes, one, 0)
 
 
-def rate(place, q, majors, subs, owns, walls, metric, mask, *, cgrid, step_planes, components, metric_rows):
+def rate(q, majors, subs, extras, metric, mask, *, cgrid, step_planes, components, metric_rows):
     _, planes, rows, lanes = q.shape
     anywhere = pl.BlockSpec(memory_space=pl.ANY)
     block = lambda n: pl.BlockSpec((n, step_planes, rows, lanes), lambda i: (0, i, 0, 0))
-    if mask is None:
-        mask = jnp.zeros((1, 8, 128), i32)
-        mask_spec = whole(mask.shape)
-    else:
-        mask_spec = pl.BlockSpec((step_planes, rows, lanes), lambda i: (i, 0, 0))
+    last_specs = [block(3)]
+    last = (metric,)
+    if mask is not None:
+        last_specs = [pl.BlockSpec((step_planes, rows, lanes), lambda i: (i, 0, 0))] + last_specs
+        last = (mask, metric)
     return pl.pallas_call(
         functools.partial(
             rate_kernel,
@@ -263,24 +259,22 @@
             metric_rows=metric_rows,
         ),
         grid=(planes // step_planes,),
-        in_specs=[pl.BlockSpec(memory_space=pltpu.SMEM), anywhere, anywhere, anywhere]
-        + [whole(x.shape) for x in (*subs, *owns, *walls)]
-        + [block(3), mask_spec],
+        in_specs=[anywhere] * 3 + [whole(x.shape) for x in (*subs, *extras)] + last_specs,
         out_specs=block(5),
         out_shape=jax.ShapeDtypeStruct(q.shape, f32),
         scratch_shapes=[
             pltpu.VMEM((5, planes + 4, rows, lanes), f32),
             pltpu.VMEM((3, 5, rows, lanes), f32),
             pltpu.VMEM((2, 14, planes, lanes), f32),
-            pltpu.VMEM((14, rows, 128), f32),
-            pltpu.SemaphoreType.DMA((3,)),
-        ],
+        ]
+        + [pltpu.VMEM((14, rows, 128), f32)] * cgrid
+        + [pltpu.SemaphoreType.DMA((3,))],
         compiler_params=params(),
         cost_estimate=pl.CostEstimate(
             flops=300 * planes * rows * lanes, bytes_accessed=60 * planes * rows * lanes, transcendentals=0
         ),
         name="cgrid_rate" if cgrid else "flap_rate",
-    )(place, q, *majors, *subs, *owns, *walls, metric, mask)
+    )(q, *majors, *subs, *extras, *last)
 
 
 def split_two(x):
@@ -288,69 +282,207 @@
     return high, (x - high.astype(f32)).astype(bf16)
 
 
-def donor_kernel(cell_ref, frac_ref, q_ref, out_ref, table, *, tile):
+def lookup(both, at):
+    width = at.shape[1]
+    highs = both.shape[0] // 10
+    cells = lax.broadcasted_iota(i32, (256, width), 0).astype(f32).astype(bf16)
+    sub = lax.broadcasted_iota(i32, (8, width), 0)
+    pick = jnp.where(
+        cells == (at & 255).astype(f32).astype(bf16), jnp.ones((), bf16), jnp.zeros((), bf16)
+    )
+    high = at // 256
+    found = jnp.dot(both, pick, preferred_element_type=f32)
+    masks = [sub + 8 * g == high for g in range(highs // 8)]
+    values = []
+    for c in range(5):
+        value = None
+        for g, mask in enumerate(masks):
+            r = c * highs + 8 * g
+            piece = found[r : r + 8] + found[5 * highs + r : 5 * highs + r + 8]
+            value = jnp.where(mask, piece, 0.0 if value is None else value)
+        values.append(jnp.sum(value, axis=0, keepdims=True))
+    return values
+
+
+def add_remainders(table):
+    half = table.shape[0] // 2
+    for r in range(0, half, 8):
+        value = table[r : r + 8, :]
+        table[half + r : half + r + 8, :] = value - value.astype(bf16).astype(f32)
+
+
+def donor_kernel(
+    cell_ref, frac_ref, q_ref, out_ref, planes, pieces, rank_ref, ordered, where_ref, first, partial, table, sem
+):
     spans, rows, lanes = q_ref.shape[1:]
-    slots = cell_ref.shape[1]
-
-    @pl.when(pl.program_id(0) == 0)
-    def _():
-        def prepare(k, _):
-            for c in range(5):
-                high, low = split_two(q_ref[c, k])
-                here = slice(c * rows, (c + 1) * rows)
-                table[k, here, 0:lanes] = high
-                table[k, here, lanes : 2 * lanes] = low
-                table[k, here, 2 * lanes : 3 * lanes] = high
-            return 0
-
-        lax.fori_loop(0, spans, prepare, 0)
-
-    part = pl.program_id(0)
-    per = slots // tile
-    w = part // per
-    t0 = pl.multiple_of((part % per) * tile, 128)
-    cell = cell_ref[pl.ds(w, 1), pl.ds(t0, tile)]
-    f0, f1, f2 = [frac_ref[d, pl.ds(w, 1), pl.ds(t0, tile)] for d in range(3)]
+    count, slots = cell_ref.shape
+    tile = 256
+    tiles = count * slots // tile
+    wide = slots // 128
+    one, zero = jnp.ones((), bf16), jnp.zeros((), bf16)
+
+    def prepare(k, _):
+        for c in range(5):
+            high, low = split_two(q_ref[c, k])
+            here = pl.ds(pl.multiple_of(k * 5 * rows + c * rows, 16), rows)
+            planes[here, 0:lanes] = high
+            planes[here, lanes : 2 * lanes] = low
+            planes[here, 2 * lanes : 3 * lanes] = high
+        return 0
+
+    lax.fori_loop(0, spans, prepare, 0)
+    planes[spans * 5 * rows :, :] = jnp.zeros((5 * rows, 3 * lanes), bf16)
+
+    cell = cell_ref[...]
     upper = jnp.floor((cell.astype(f32) + 0.5) * (1.0 / (lanes - 1)))
     span = jnp.floor((upper + 0.5) * (1.0 / (rows - 1)))
-    wrap = (upper - span * (rows - 1)).astype(i32)
-    normal = cell - upper.astype(i32) * (lanes - 1)
-    span = span.astype(i32)
-
-    def weights(count, at, frac):
-        cells = lax.broadcasted_iota(i32, (count, tile), 0)
-        return jnp.where(cells == at, 1.0 - frac, jnp.where(cells == at + 1, frac, 0.0))
-
-    high, low = split_two(weights(lanes, normal, f2))
-    along = jnp.concatenate([high, high, low], axis=0)
-    across = weights(rows, wrap, f1)
-
-    def plane(k, sums):
-        mixed = jnp.dot(table[k], along, preferred_element_type=f32)
-        ws = jnp.where(span == k, 1.0 - f0, jnp.where(span + 1 == k, f0, 0.0))
-        new = []
-        for c in range(5):
-            total = mixed[c * rows : c * rows + 8] * across[0:8]
-            for r in range(8, rows, 8):
-                total += mixed[c * rows + r : c * rows + r + 8] * across[r : r + 8]
-            new.append(sums[c] + ws * total)
+    pieces[0] = span
+    pieces[1] = upper - span * (rows - 1)
+    pieces[2] = cell.astype(f32) - upper * (lanes - 1)
+    for d in range(3):
+        f = frac_ref[d]
+        high = f.astype(bf16).astype(f32)
+        pieces[3 + 2 * d] = high
+        pieces[4 + 2 * d] = f - high
+
+    lines = jnp.concatenate([span[:, 128 * t : 128 * t + 128] for t in range(wide)], axis=0)
+    depth = lines.shape[0]
+    hits = [jnp.where(lines == b, 1.0, 0.0).astype(bf16) for b in range(spans)]
+    into = lax.broadcasted_iota(i32, (128, 256), 0)
+    onto = lax.broadcasted_iota(i32, (128, 256), 1)
+    before = jnp.where((into < onto) | (onto >= 128), 1.0, 0.0).astype(bf16)
+    inside = jnp.dot(jnp.concatenate(hits, axis=0), before, preferred_element_type=f32)
+    sums = [inside[b * depth : (b + 1) * depth, 128:256] for b in range(spans)]
+    lower = lax.broadcasted_iota(i32, (depth, depth), 1) < lax.broadcasted_iota(i32, (depth, depth), 0)
+    above = jnp.dot(
+        jnp.where(lower, 1.0, 0.0).astype(bf16),
+        jnp.concatenate([x.astype(bf16) for x in sums], axis=1),
+        preferred_element_type=f32,
+    )
+    start = jnp.zeros((1, 128), f32)
+    rank = jnp.zeros((depth, 128), f32)
+    for b in range(spans):
+        over = above[:, b * 128 : (b + 1) * 128]
+        rank = jnp.where(lines == b, inside[b * depth : (b + 1) * depth, 0:128] + over + start, rank)
+        start = start + over[depth - 1 :] + sums[b][depth - 1 :]
+    rank = rank.astype(i32)
+    for t in range(wide):
+        rank_ref[:, 128 * t : 128 * t + 128] = rank[8 * t : 8 * t + 8]
+
+    tile_at = lax.broadcasted_iota(i32, (tiles, slots), 0).astype(f32).astype(bf16)
+    place_at = lax.broadcasted_iota(i32, (tile, slots), 0).astype(f32).astype(bf16)
+    ordered[...] = jnp.zeros_like(ordered)
+
+    def order(w, _):
+        to = rank_ref[pl.ds(w, 1), :]
+        in_tile = jnp.where(tile_at == (to // tile).astype(f32).astype(bf16), one, zero)
+        at_place = jnp.where(place_at == (to & (tile - 1)).astype(f32).astype(bf16), one, zero)
+        parts = [in_tile * pieces[p, pl.ds(w, 1), :].astype(bf16) for p in range(9)]
+        ordered[...] += lax.dot_general(
+            jnp.concatenate(parts, axis=0),
+            at_place,
+            (((1,), (1,)), ((), ())),
+            preferred_element_type=f32,
+        )
+        return 0
+
+    lax.fori_loop(0, count, order, 0)
+    where_ref[...] = ordered[0:tiles, :].astype(i32)
+    copy = pltpu.make_async_copy(where_ref, first, sem)
+    copy.start()
+    copy.wait()
+
+    def weights(cells, at, frac):
+        here = lax.broadcasted_iota(i32, (cells, tile), 0)
+        return jnp.where(here == at, 1.0 - frac, jnp.where(here == at + 1, frac, 0.0))
+
+    def tile_of(i):
+        def piece(p):
+            return ordered[pl.ds(p * tiles + i, 1), :]
+
+        span, wrap, normal = piece(0).astype(i32), piece(1).astype(i32), piece(2).astype(i32)
+        f0, f1, f2 = [piece(3 + 2 * d) + piece(4 + 2 * d) for d in range(3)]
+        high, low = split_two(weights(lanes, normal, f2))
+        return span, f0, jnp.concatenate([high, high, low], axis=0), weights(rows, wrap, f1)
+
+    def pair(k, made, sums):
+        span, f0, along, across = made
+        from_row = pl.ds(pl.multiple_of(k * 5 * rows, 16), 10 * rows)
+        mixed = jnp.dot(planes[from_row, :], along, preferred_element_type=f32)
+        new = list(sums)
+        for n in range(2):
+            ws = jnp.where(span == k + n, 1.0 - f0, jnp.where(span + 1 == k + n, f0, 0.0))
+            for c in range(5):
+                r0 = (5 * n + c) * rows
+                total = mixed[r0 : r0 + 8] * across[0:8]
+                for r in range(8, rows, 8):
+                    total += mixed[r0 + r : r0 + r + 8] * across[r : r + 8]
+                new[c] = ws * total if new[c] is None else new[c] + ws * total
         return tuple(new)
 
-    sums = lax.fori_loop(0, spans, plane, tuple(jnp.zeros((8, tile), f32) for _ in range(5)), unroll=4)
-    for c in range(5):
-        out_ref[w, c : c + 1, pl.ds(t0, tile)] = jnp.sum(sums[c], axis=0, keepdims=True)
-
-
-def donors(cell, frac, state, tile=256):
+    def step(g, _):
+        for n in range(GROUP):
+            i = g * GROUP + n
+            for c, x in enumerate(pair(first[i, 0], tile_of(i), (None,) * 5)):
+                partial[n, c] = x
+        for n in range(GROUP):
+            i = g * GROUP + n
+            lowest = first[i, 0]
+            more = (first[i, tile - 1] + 1 - lowest) // 2
+
+            @pl.when(more > 0)
+            def _():
+                made = tile_of(i)
+
+                def again(m, _):
+                    sums = pair(lowest + 2 + 2 * m, made, tuple(partial[n, c] for c in range(5)))
+                    for c in range(5):
+                        partial[n, c] = sums[c]
+                    return 0
+
+                lax.fori_loop(0, more, again, 0)
+
+        for n in range(GROUP):
+            i = g * GROUP + n
+            for c in range(5):
+                table[pl.ds(c * tiles + i, 1), :] = jnp.sum(partial[n, c], axis=0, keepdims=True)
+        return 0
+
+    lax.fori_loop(0, tiles // GROUP, step, 0)
+
+    add_remainders(table)
+    both = table[...].astype(bf16)
+
+    def put_back(w, _):
+        for t in range(0, slots, 512):
+            for c, value in enumerate(lookup(both, rank_ref[pl.ds(w, 1), t : t + 512])):
+                out_ref[w, c : c + 1, t : t + 512] = value
+        return 0
+
+    lax.fori_loop(0, count, put_back, 0, unroll=8)
+
+
+def donors(cell, frac, state):
     _, spans, rows, lanes = state.shape
     count, slots = cell.shape
+    tiles = count * slots // 256
     return pl.pallas_call(
-        functools.partial(donor_kernel, tile=tile),
-        grid=(count * slots // tile,),
+        donor_kernel,
+        grid=(1,),
         in_specs=[whole(cell.shape), whole(frac.shape), whole(state.shape)],
         out_specs=whole((count, 5, slots)),
         out_shape=jax.ShapeDtypeStruct((count, 5, slots), f32),
-        scratch_shapes=[pltpu.VMEM((spans, 5 * rows, 3 * lanes), bf16)],
+        scratch_shapes=[
+            pltpu.VMEM(((spans + 1) * 5 * rows, 3 * lanes), bf16),
+            pltpu.VMEM((9, count, slots), f32),
+            pltpu.VMEM((count, slots), i32),
+            pltpu.VMEM((9 * tiles, 256), f32),
+            pltpu.VMEM((tiles, 256), i32),
+            pltpu.SMEM((tiles, 256), i32),
+            pltpu.VMEM((GROUP, 5, 8, 256), f32),
+            pltpu.VMEM((10 * tiles, 256), f32),
+            pltpu.SemaphoreType.DMA(()),
+        ],
         compiler_params=params(),
         name="donors",
     )(cell, frac, state)
@@ -371,29 +503,13 @@
                 for r in range(per):
                     value = slot_ref[w, c : c + 1, r * low : (r + 1) * low]
                     table[c * highs + w * per + r : c * highs + w * per + r + 1, :] = value
-        for r in range(0, 5 * highs, 8):
-            value = table[r : r + 8, :]
-            table[5 * highs + r : 5 * highs + r + 8, :] = value - value.astype(bf16).astype(f32)
+        add_remainders(table)
 
     both = table[...].astype(bf16)
-    sub = lax.broadcasted_iota(i32, (8, lanes), 0)
-    cells = lax.broadcasted_iota(i32, (low, lanes), 0).astype(f32).astype(bf16)
-    one, zero = jnp.ones((), bf16), jnp.zeros((), bf16)
 
     def row(s, _):
-        at = from_ref[0, pl.ds(s, 1), :]
-        pick = jnp.where(cells == (at & (low - 1)).astype(f32).astype(bf16), one, zero)
-        high = at // low
-        found = jnp.dot(both, pick, preferred_element_type=f32)
-        masks = [sub + 8 * g == high for g in range(highs // 8)]
         keep = mask_ref[0, pl.ds(s, 1), :] == 1
-        for c in range(5):
-            value = None
-            for g, mask in enumerate(masks):
-                r = c * highs + 8 * g
-                piece = found[r : r + 8] + found[5 * highs + r : 5 * highs + r + 8]
-                value = jnp.where(mask, piece, 0.0 if value is None else value)
-            value = jnp.sum(value, axis=0, keepdims=True)
+        for c, value in enumerate(lookup(both, from_ref[0, pl.ds(s, 1), :])):
             out_ref[c, 0, pl.ds(s, 1), :] = jnp.where(keep, q_ref[c, 0, pl.ds(s, 1), :], value)
         return 0
 
@@ -437,8 +553,7 @@
 def body(
     cgrid_state, cgrid_metric, flap_state, flap_metric, iblank, fringe_from, donor_cell, donor_frac
 ):
-    wrap_count, span_count = lax.axis_size("wrap"), lax.axis_size("span")
-    place = jnp.stack([lax.axis_index("wrap"), jnp.int32(wrap_count)]).astype(i32)
+    wrap_count = lax.axis_size("wrap")
 
     def onward(value, axis):
         size = lax.axis_size(axis)
@@ -450,9 +565,8 @@
 
     wrap_lo, wrap_hi, span_lo, span_hi, wall = pack(cgrid_state)
     far = lax.ppermute(
-        wall[:, :, 0:32], "wrap", [(i, wrap_count - 1 - i) for i in range(wrap_count)]
+        wall, "wrap", [(i, wrap_count - 1 - i) for i in range(wrap_count)]
     )
-    far = jnp.pad(far, ((0, 0), (0, 0), (0, 96)))
     majors = (onward(span_hi, "span"), back(span_lo, "span"))
     subs = (onward(wrap_hi, "wrap"), back(wrap_lo, "wrap"))
 
@@ -466,12 +580,10 @@
     flap_subs = (onward(edge_hi, "span"), back(edge_lo, "span"))
 
     cgrid_rate = rate(
-        place,
         cgrid_state,
         majors,
         subs,
-        (wrap_lo, wrap_hi),
-        (wall, far),
+        (wrap_lo, wrap_hi, wall, far),
         cgrid_metric,
         None,
         cgrid=True,
@@ -479,14 +591,11 @@
         components=(3, 1, 2),
         metric_rows=(0, 1, 2),
     )
-    none = jnp.zeros((5, 8, 128), f32)
     flap_rate = rate(
-        place,
         filled,
         flap_majors,
         flap_subs,
-        (none, none),
-        (none, none),
+        (),
         turned(flap_metric),
         mask,
         cgrid=False,

time: 149 us -> 105 us (0.70)
  Pallas kernels: 115 us -> 71.9 us
    pallas_call x1, Pallas kernels: 64.6 us -> 21.4 us  [donors(): pl.pallas_call(donor_kernel, grid=(1,), in_specs=[whole(cell.shape), whol...]
  transfers between devices with their start and end apart: 10 -> 10, of which waited for: 0 -> 0; matrix products, arithmetic and copies ran while one was open for 1% -> 0% of each run, Pallas kernels for 27% -> 38%
where the time goes in v2:
time: 105 us; the launch traced here: 104 us
  Pallas kernels  71.9 us (68%)
  starting transfers between devices  29.1 us (28%)
  local copies, waits for them, and re-layouts  2.46 us (2%)
    pallas_call x2, Pallas kernels, rate(): pl.pallas_call(functools.partial(rate_kernel, cgrid=cgrid, step_planes=st...  25.3 us
    pallas_call x1, Pallas kernels, fill(): pl.pallas_call(fill_kernel, grid=(planes,), in_specs=[plane, plane, state...  22.1 us
    pallas_call x1, Pallas kernels, donors(): pl.pallas_call(donor_kernel, grid=(1,), in_specs=[whole(cell.shape), whol...  21.4 us
    ppermute x4, starting transfers between devices, back(): return lax.ppermute(value, axis, [((i + 1) % size, i) for i in range(size)])  18.7 us
    all_to_all x1, starting transfers between devices, body(): slot = lax.all_to_all(slot, 'wrap', split_axis=0, concat_axis=0, tiled=True)  5.91 us
    ppermute x1, starting transfers between devices, body(): lax.ppermute(wall, 'wrap', [(i, wrap_count - 1 - i) for i in range(wrap_c...  4.13 us
    pallas_call x1, Pallas kernels, pack(): pl.pallas_call(pack_kernel, in_specs=[whole(state.shape)], out_specs=[who...  3.1 us
    unnamed x20, local copies, waits for them, and re-layouts  2.46 us
  transfers between devices with their start and end apart: 10, of which 0 were waited for; matrix products, arithmetic and copies ran while one was open for 0% of the time, Pallas kernels for 38%

profile of v2, /device:TPU:0, one launch (start us, length us, event | category | flops | bytes accessed | tf_op | source)
XLA Modules:
  0.0 104.3 jit_solution(14404451814708508688)
XLA Ops:
  0.6 21.4 %donors.1 = f32[8,5,1024]{2,1,0:T(8,128)} custom-call(s32[8,1024]{1,0:T(8,128)} %bitcast.14, f32[3,8,1024]{2,1,0:T(8,128)} %bitcast.13, f32[5,16,32,256]{3,2,1,0:T(8,128)} %q_ref.3), custom_call_target="tpu_custom_call" | custom-call | tf_op jit(solution)/shard_map/donors/pallas_call | solution.py:469
  22.1 5.9 %all-to-all-start = ((f32[8,5,1024]{2,1,0:T(8,128)}), f32[8,5,1024]{2,1,0:T(8,128)S(1)}, u32[]{:S(2)}, u32[]{:S(2)}) async-start(f32[8,5,1024]{2,1,0:T(8,128)} %donors.1), calls=%async_computation | async-start | bytes 524288 | tf_op jit(solution)/shard_map/all_to_all | solution.py:574
  28.0 3.1 %cgrid_pack.1 = (f32[5,2,16,256]{3,2,1,0:T(8,128)}, f32[5,2,16,256]{3,2,1,0:T(8,128)}, f32[5,2,32,256]{3,2,1,0:T(8,128)}, f32[5,2,32,256]{3,2,1,0:T(8,128)}, f32[5,32,32]{2,1,0:T(8,128)}) custom-call(f32[5,16,32,256]{3,2,1,0:T(8,128)} %q_ref.3), custom_call_target="tpu_custom_call" | custom-call | tf_op jit(solution)/shard_map/cgrid_pack/pallas_call | solution.py:66
  31.1 4.1 %collective-permute-start.4 = (f32[5,32,32]{2,1,0:T(8,128)}, f32[5,32,32]{2,1,0:T(8,128)S(1)}, u32[]{:S(2)}, u32[]{:S(2)}) collective-permute-start(f32[5,32,32]{2,1,0:T(8,128)} %get-tuple-element.16.refs_2_), channel_id=1, source_target_pairs={{0,112},{16,96},{32,80},{48,64},{64,48},{80,32},{96,16},{112,0},{1... | collective-permute-start | bytes 61448 | tf_op jit(solution)/shard_map/ppermute | solution.py:567
  35.2 0.3 collective-permute-start.2
  35.5 3.9 %collective-permute-start.3 = (f32[5,2,16,256]{3,2,1,0:T(8,128)}, f32[5,2,16,256]{3,2,1,0:T(8,128)S(1)}, u32[]{:S(2)}, u32[]{:S(2)}) collective-permute-start(f32[5,2,16,256]{3,2,1,0:T(8,128)} %get-tuple-element.15.refs_0_), channel_id=1, source_target_pairs={{16,0},{32,16},{48,32},{64,48},{80,64},{96,80},{112,96},{0,112},{1... | collective-permute-start | bytes 491528 | tf_op jit(solution)/shard_map/ppermute | solution.py:564
  39.3 0.0 collective-permute-start
  39.3 5.4 %collective-permute-start.1 = (f32[5,2,32,256]{3,2,1,0:T(8,128)}, f32[5,2,32,256]{3,2,1,0:T(8,128)S(1)}, u32[]{:S(2)}, u32[]{:S(2)}) collective-permute-start(f32[5,2,32,256]{3,2,1,0:T(8,128)} %get-tuple-element.13), channel_id=1, source_target_pairs={{1,0},{2,1},{3,2},{4,3},{5,4},{6,5},{7,6},{8,7},{9,8},{10,9},{11,1... | collective-permute-start | bytes 983048 | tf_op jit(solution)/shard_map/ppermute | solution.py:564
  44.7 0.0 all-to-all-done.slot_ref
  44.7 0.7 copy-done.6
  45.4 22.1 %fill.1 = (f32[5,12,16,512]{3,2,1,0:T(8,128)}, f32[5,2,16,512]{3,2,1,0:T(8,128)}, f32[5,2,16,512]{3,2,1,0:T(8,128)}, f32[5,2,12,512]{3,2,1,0:T(8,128)}, f32[5,2,12,512]{3,2,1,0:T(8,128)}) custom-call(s32[12,16,512]{2,1,0:T(8,128)} %bitcast.16, s32[12,16,512]{2,1,0:T(8,128)} %bitcast.11, f32[5,12,16,512]{3,2,1,0:T(8,128)} %bitcast.15, f32[8,5,1024]{2,1,0:T(8,128)} %copy-done.6), custom_call_target="tpu_custom_call" | custom-call | flops 24000000000 | bytes 6000000 | tf_op jit(solution)/shard_map/fill/pallas_call | solution.py:540
  67.6 0.0 collective-permute-done.4.refs_3_
  67.6 0.1 collective-permute-start.5
  67.7 0.0 collective-permute-done.2.sub_lo
  67.7 4.1 %collective-permute-start.6 = (f32[5,2,16,512]{3,2,1,0:T(8,128)}, f32[5,2,16,512]{3,2,1,0:T(8,128)S(1)}, u32[]{:S(2)}, u32[]{:S(2)}) collective-permute-start(f32[5,2,16,512]{3,2,1,0:T(8,128)} %get-tuple-element.19), channel_id=1, source_target_pairs={{16,0},{32,16},{48,32},{64,48},{80,64},{96,80},{112,96},{0,112},{1... | collective-permute-start | bytes 983048 | tf_op jit(solution)/shard_map/ppermute | solution.py:564
  71.8 0.0 collective-permute-done.3.sub_hi
  71.8 0.0 collective-permute-start.7
  71.8 0.0 collective-permute-done.major_lo
  71.8 5.3 %collective-permute-start.8 = (f32[5,2,12,512]{3,2,1,0:T(8,128)}, f32[5,2,12,512]{3,2,1,0:T(8,128)S(1)}, u32[]{:S(2)}, u32[]{:S(2)}) collective-permute-start(f32[5,2,12,512]{3,2,1,0:T(8,128)} %get-tuple-element.21), channel_id=1, source_target_pairs={{1,0},{2,1},{3,2},{4,3},{5,4},{6,5},{7,6},{8,7},{9,8},{10,9},{11,1... | collective-permute-start | bytes 737288 | tf_op jit(solution)/shard_map/ppermute | solution.py:564
  77.2 0.0 collective-permute-done.1.major_hi
  77.2 0.0 copy-start.1
  77.2 0.7 copy-done.1
  77.9 14.5 %cgrid_rate.1 = f32[5,16,32,256]{3,2,1,0:T(8,128)} custom-call(f32[5,16,32,256]{3,2,1,0:T(8,128)} %q_ref.3, f32[5,2,32,256]{3,2,1,0:T(8,128)} %copy-done, f32[5,2,32,256]{3,2,1,0:T(8,128)} %copy-done.1, f32[5,2,16,256]{3,2,1,0:T(8,128)} %copy-done.7, f32[5,2,16,256]{3,2,1,0:T(8,128)} %copy-done.8, f32[5,2,16,256]{3,2,1,0:T(8,128)} %get-tuple-element.15.refs_0_, ...), custom_call_target="tpu_custom_call" | custom-call | flops 39321600 | bytes 7864320 | tf_op jit(solution)/shard_map/cgrid_rate/pallas_call | solution.py:253
  92.4 0.0 collective-permute-done.7.sub_lo
  92.4 0.0 collective-permute-done.8.sub_hi
  92.5 0.0 collective-permute-done.5.major_lo
  92.5 0.0 collective-permute-done.6.major_hi
  92.5 0.6 copy-done.4
  93.2 0.1 copy-done.5
  93.3 0.1 copy-done.2
  93.4 0.1 copy-done.3
  93.5 10.8 %flap_rate.1 = f32[5,12,16,512]{3,2,1,0:T(8,128)} custom-call(f32[5,12,16,512]{3,2,1,0:T(8,128)} %get-tuple-element.17.q_hbm, f32[5,2,16,512]{3,2,1,0:T(8,128)} %copy-done.2, f32[5,2,16,512]{3,2,1,0:T(8,128)} %copy-done.3, f32[5,2,12,512]{3,2,1,0:T(8,128)} %copy-done.4, f32[5,2,12,512]{3,2,1,0:T(8,128)} %copy-done.5, s32[12,16,512]{2,1,0:T(8,128)} %bitcast.12, ...), custom_call_target="tpu_custom_call" | custom-call | flops 29491200 | bytes 5898240 | tf_op jit(solution)/shard_map/flap_rate/pallas_call | solution.py:253
  (13 shorter events, 0.0 us)
Async XLA Ops:
  22.1 22.6 %all-to-all-start = ((f32[8,5,1024]{2,1,0:T(8,128)}), f32[8,5,1024]{2,1,0:T(8,128)S(1)}, u32[]{:S(2)}, u32[]{:S(2)}) async-start(f32[8,5,1024]{2,1,0:T(8,128)} %donors.1), calls=%async_computation | async-start | bytes 524288 | tf_op jit(solution)/shard_map/all_to_all | solution.py:574
  31.1 36.5 %collective-permute-start.4 = (f32[5,32,32]{2,1,0:T(8,128)}, f32[5,32,32]{2,1,0:T(8,128)S(1)}, u32[]{:S(2)}, u32[]{:S(2)}) collective-permute-start(f32[5,32,32]{2,1,0:T(8,128)} %get-tuple-element.16.refs_2_), channel_id=1, source_target_pairs={{0,112},{16,96},{32,80},{48,64},{64,48},{80,32},{96,16},{112,0},{1... | collective-permute-start | bytes 61448 | tf_op jit(solution)/shard_map/ppermute | solution.py:567
  35.2 32.4 %collective-permute-start.2 = (f32[5,2,16,256]{3,2,1,0:T(8,128)}, f32[5,2,16,256]{3,2,1,0:T(8,128)S(1)}, u32[]{:S(2)}, u32[]{:S(2)}) collective-permute-start(f32[5,2,16,256]{3,2,1,0:T(8,128)} %get-tuple-element.14.refs_1_), channel_id=1, source_target_pairs={{0,16},{16,32},{32,48},{48,64},{64,80},{80,96},{96,112},{112,0},{1... | collective-permute-start | bytes 491528 | tf_op jit(solution)/shard_map/ppermute | solution.py:560
  35.5 36.3 %collective-permute-start.3 = (f32[5,2,16,256]{3,2,1,0:T(8,128)}, f32[5,2,16,256]{3,2,1,0:T(8,128)S(1)}, u32[]{:S(2)}, u32[]{:S(2)}) collective-permute-start(f32[5,2,16,256]{3,2,1,0:T(8,128)} %get-tuple-element.15.refs_0_), channel_id=1, source_target_pairs={{16,0},{32,16},{48,32},{64,48},{80,64},{96,80},{112,96},{0,112},{1... | collective-permute-start | bytes 491528 | tf_op jit(solution)/shard_map/ppermute | solution.py:564
  39.3 32.5 %collective-permute-start = (f32[5,2,32,256]{3,2,1,0:T(8,128)}, f32[5,2,32,256]{3,2,1,0:T(8,128)S(1)}, u32[]{:S(2)}, u32[]{:S(2)}) collective-permute-start(f32[5,2,32,256]{3,2,1,0:T(8,128)} %get-tuple-element.12), channel_id=1, source_target_pairs={{0,1},{1,2},{2,3},{3,4},{4,5},{5,6},{6,7},{7,8},{8,9},{9,10},{10,1... | collective-permute-start | bytes 983048 | tf_op jit(solution)/shard_map/ppermute | solution.py:560
  39.3 37.8 %collective-permute-start.1 = (f32[5,2,32,256]{3,2,1,0:T(8,128)}, f32[5,2,32,256]{3,2,1,0:T(8,128)S(1)}, u32[]{:S(2)}, u32[]{:S(2)}) collective-permute-start(f32[5,2,32,256]{3,2,1,0:T(8,128)} %get-tuple-element.13), channel_id=1, source_target_pairs={{1,0},{2,1},{3,2},{4,3},{5,4},{6,5},{7,6},{8,7},{9,8},{10,9},{11,1... | collective-permute-start | bytes 983048 | tf_op jit(solution)/shard_map/ppermute | solution.py:564
  44.7 0.7 copy-start.6
  67.6 9.6 %copy-start.9 = (f32[5,32,32]{2,1,0:T(8,128)}, f32[5,32,32]{2,1,0:T(8,128)S(1)}, u32[]{:S(2)}) copy-start(f32[5,32,32]{2,1,0:T(8,128)S(1)} %collective-permute-done.4.refs_3_) | copy-start | bytes 61444
  67.6 24.9 %collective-permute-start.5 = (f32[5,2,16,512]{3,2,1,0:T(8,128)}, f32[5,2,16,512]{3,2,1,0:T(8,128)S(1)}, u32[]{:S(2)}, u32[]{:S(2)}) collective-permute-start(f32[5,2,16,512]{3,2,1,0:T(8,128)} %get-tuple-element.18), channel_id=1, source_target_pairs={{0,16},{16,32},{32,48},{48,64},{64,80},{80,96},{96,112},{112,0},{1... | collective-permute-start | bytes 983048 | tf_op jit(solution)/shard_map/ppermute | solution.py:560
  67.7 9.5 %copy-start.7 = (f32[5,2,16,256]{3,2,1,0:T(8,128)}, f32[5,2,16,256]{3,2,1,0:T(8,128)S(1)}, u32[]{:S(2)}) copy-start(f32[5,2,16,256]{3,2,1,0:T(8,128)S(1)} %collective-permute-done.2.sub_lo) | copy-start | bytes 491524
  67.7 24.8 %collective-permute-start.6 = (f32[5,2,16,512]{3,2,1,0:T(8,128)}, f32[5,2,16,512]{3,2,1,0:T(8,128)S(1)}, u32[]{:S(2)}, u32[]{:S(2)}) collective-permute-start(f32[5,2,16,512]{3,2,1,0:T(8,128)} %get-tuple-element.19), channel_id=1, source_target_pairs={{16,0},{32,16},{48,32},{64,48},{80,64},{96,80},{112,96},{0,112},{1... | collective-permute-start | bytes 983048 | tf_op jit(solution)/shard_map/ppermute | solution.py:564
  71.8 5.4 %copy-start.8 = (f32[5,2,16,256]{3,2,1,0:T(8,128)}, f32[5,2,16,256]{3,2,1,0:T(8,128)S(1)}, u32[]{:S(2)}) copy-start(f32[5,2,16,256]{3,2,1,0:T(8,128)S(1)} %collective-permute-done.3.sub_hi) | copy-start | bytes 491524
  71.8 20.6 %collective-permute-start.7 = (f32[5,2,12,512]{3,2,1,0:T(8,128)}, f32[5,2,12,512]{3,2,1,0:T(8,128)S(1)}, u32[]{:S(2)}, u32[]{:S(2)}) collective-permute-start(f32[5,2,12,512]{3,2,1,0:T(8,128)} %get-tuple-element.20), channel_id=1, source_target_pairs={{0,1},{1,2},{2,3},{3,4},{4,5},{5,6},{6,7},{7,8},{8,9},{9,10},{10,1... | collective-permute-start | bytes 737288 | tf_op jit(solution)/shard_map/ppermute | solution.py:560
  71.8 5.4 %copy-start = (f32[5,2,32,256]{3,2,1,0:T(8,128)}, f32[5,2,32,256]{3,2,1,0:T(8,128)S(1)}, u32[]{:S(2)}) copy-start(f32[5,2,32,256]{3,2,1,0:T(8,128)S(1)} %collective-permute-done.major_lo) | copy-start | bytes 983044
  71.8 20.6 %collective-permute-start.8 = (f32[5,2,12,512]{3,2,1,0:T(8,128)}, f32[5,2,12,512]{3,2,1,0:T(8,128)S(1)}, u32[]{:S(2)}, u32[]{:S(2)}) collective-permute-start(f32[5,2,12,512]{3,2,1,0:T(8,128)} %get-tuple-element.21), channel_id=1, source_target_pairs={{1,0},{2,1},{3,2},{4,3},{5,4},{6,5},{7,6},{8,7},{9,8},{10,9},{11,1... | collective-permute-start | bytes 737288 | tf_op jit(solution)/shard_map/ppermute | solution.py:564
  77.2 0.7 copy-start.1
  92.4 0.7 copy-start.4
  92.5 0.8 copy-start.5
  92.5 0.9 copy-start.2
  92.5 1.0 copy-start.3

commit v3 on v2

--- a/solution.py
+++ b/solution.py
@@ -29,19 +29,23 @@
     v = [q[m] * inverse for m in (1, 2, 3)]
     kinetic = 0.5 * (v[0] * v[0] + v[1] * v[1] + v[2] * v[2])
     pressure = 0.4 * (q[4] - q[0] * kinetic)
-    return v + [pressure, viscosity * kinetic + conduction * (pressure * inverse)]
+    return v + [pressure, kinetic + (conduction / viscosity) * (pressure * inverse)]
+
+
+def wrapped(place, count):
+    return (place < count // 4) | (place >= count - count // 4)
 
 
 def flux(q, prims, m):
-    u = prims[m - 1]
+    u = (0.5 / damping) * prims[m - 1]
     f = [q[0] * u]
     for c in (1, 2, 3):
-        f.append(q[c] * u + prims[3] if c == m else q[c] * u)
+        f.append(q[c] * u + (0.5 / damping) * prims[3] if c == m else q[c] * u)
     f.append((q[4] + prims[3]) * u)
     return f
 
 
-def pack_kernel(q_ref, wrap_lo, wrap_hi, span_lo, span_hi, wall):
+def pack(q_ref, wrap_lo, wrap_hi, span_lo, span_hi, wall):
     spans, rows = q_ref.shape[1], q_ref.shape[2]
     lane = lax.broadcasted_iota(i32, (rows, 128), 1)
     for c in range(5):
@@ -58,20 +62,6 @@
                 near = pltpu.roll(near, 2 * k, 1)
             cells = jnp.where(lane // 2 == k, near, cells)
         wall[c] = cells[:, 0 : 2 * spans]
-
-
-def pack(state):
-    _, spans, rows, lanes = state.shape
-    shapes = [(5, 2, spans, lanes)] * 2 + [(5, 2, rows, lanes)] * 2 + [(5, rows, 2 * spans)]
-    return pl.pallas_call(
-        pack_kernel,
-        in_specs=[whole(state.shape)],
-        out_specs=[whole(s) for s in shapes],
-        out_shape=[jax.ShapeDtypeStruct(s, f32) for s in shapes],
-        grid=(1,),
-        compiler_params=params(),
-        name="cgrid_pack",
-    )(state)
 
 
 def rate_kernel(
@@ -101,22 +91,33 @@
     def edge_fields(q1, q2, m, side):
         prims = primitives(q1)
         fl = flux(q1, prims, m)
-        lead = [(-0.5 * side) * fl[c] + 0.125 * q1[c] - damping * q2[c] for c in range(5)]
+        lead = [4.0 * q1[c] - side * fl[c] - q2[c] for c in range(5)]
         return lead + q1 + prims[:3] + prims[4:]
 
     def store_prims(k, slot):
-        for i, x in enumerate(primitives([qe[c, k] for c in range(5)])):
+        q = [qe[c, k] for c in range(5)]
+        prims = primitives(q)
+        for i, x in enumerate(prims + flux(q, prims, major_m)):
             prim[slot, i] = x
+
+    steps = planes // step_planes
+
+    def part(n):
+        n = n * step_planes
+        return pltpu.make_async_copy(
+            q_hbm.at[:, pl.ds(n, step_planes)], qe.at[:, pl.ds(n + 2, step_planes)], sems.at[n // step_planes]
+        )
 
     @pl.when(step == 0)
     def _():
         copies = [
-            pltpu.make_async_copy(q_hbm, qe.at[:, pl.ds(2, planes)], sems.at[0]),
-            pltpu.make_async_copy(major_lo, qe.at[:, pl.ds(0, 2)], sems.at[1]),
-            pltpu.make_async_copy(major_hi, qe.at[:, pl.ds(planes + 2, 2)], sems.at[2]),
+            pltpu.make_async_copy(major_lo, qe.at[:, pl.ds(0, 2)], sems.at[steps]),
+            pltpu.make_async_copy(major_hi, qe.at[:, pl.ds(planes + 2, 2)], sems.at[steps + 1]),
         ]
-        for copy in copies:
-            copy.start()
+        copies[0].start()
+        for n in range(steps):
+            part(n).start()
+        copies[1].start()
         for side, ref, own in ((-1, sub_lo, own_lo), (1, sub_hi, own_hi)):
             near, far = (1, 0) if side < 0 else (0, 1)
             q1 = [ref[c, near] for c in range(5)]
@@ -129,7 +130,7 @@
             for i, x in enumerate(edge_fields(q1, q2, sub_m, side)):
                 sub_edge[(side + 1) // 2, i] = x
         if cgrid:
-            in_wake = (place < count // 4) | (place >= count - count // 4)
+            in_wake = wrapped(place, count)
             turn = 7 - lax.broadcasted_iota(i32, (8, 128), 0)
             ghosts = []
             for c in range(5):
@@ -146,8 +147,10 @@
             second = [pltpu.roll(x, 127, 1) for x in ghosts]
             for i, x in enumerate(edge_fields(ghosts, second, lane_m, -1)):
                 lane_edge[i] = x
-        for copy in copies:
-            copy.wait()
+        copies[0].wait()
+        part(0).wait()
+        part(1).wait()
+        copies[1].wait()
         if not cgrid:
 
             @pl.when(at_start)
@@ -157,19 +160,25 @@
                     qe[c, 1] = sign * qe[c, 2]
                     qe[c, 0] = sign * qe[c, 3]
 
-            @pl.when(at_end)
-            def _():
-                for c in range(5):
-                    qe[c, planes + 2] = qe[c, planes + 1]
-                    qe[c, planes + 3] = qe[c, planes + 1]
-
         store_prims(1, 0)
         store_prims(2, 1)
 
-    row_at = lax.broadcasted_iota(i32, (rows, lanes), 0)
-    lane_at = lax.broadcasted_iota(i32, (rows, lanes), 1)
-    row_first, row_last = row_at == 0, row_at == rows - 1
-    lane_first, lane_last = lane_at == 0, lane_at == lanes - 1
+    @pl.when((step > 0) & (step < steps - 1))
+    def _():
+        part(step + 1).wait()
+
+    if not cgrid:
+
+        @pl.when((step == steps - 1) & at_end)
+        def _():
+            for c in range(5):
+                qe[c, planes + 2] = qe[c, planes + 1]
+                qe[c, planes + 3] = qe[c, planes + 1]
+
+    row_at = lax.broadcasted_iota(i32, (8, lanes), 0)
+    lane_at = lax.broadcasted_iota(i32, (rows, 128), 1)
+    row_first, row_last = row_at == 0, row_at == 7
+    lane_first, lane_last = lane_at == 0, lane_at == 127
 
     def one(b, _):
         k = step * step_planes + b
@@ -177,60 +186,69 @@
         store_prims(k + 3, above)
 
         def sub_next(x, i):
-            return jnp.where(row_last, sub_edge[1, i, pl.ds(k, 1), :], pltpu.roll(x, rows - 1, 0))
+            moved = [pltpu.roll(x[r : r + 8], 7, 0) for r in range(0, rows, 8)]
+            moved.append(sub_edge[1, i, pl.ds(k, 1), :])
+            return jnp.concatenate(
+                [jnp.where(row_last, moved[r + 1], moved[r]) for r in range(rows // 8)], axis=0
+            )
 
         def sub_prior(x, i):
-            return jnp.where(row_first, sub_edge[0, i, pl.ds(k, 1), :], pltpu.roll(x, 1, 0))
+            moved = [sub_edge[0, i, pl.ds(k, 1), :]]
+            moved += [pltpu.roll(x[r : r + 8], 1, 0) for r in range(0, rows, 8)]
+            return jnp.concatenate(
+                [jnp.where(row_first, moved[r], moved[r + 1]) for r in range(rows // 8)], axis=0
+            )
 
         def lane_next(x):
-            moved = pltpu.roll(x, lanes - 1, 1)
-            return jnp.where(lane_last, x, moved) if cgrid else moved
+            moved = [pltpu.roll(x[:, t : t + 128], 127, 1) for t in range(0, lanes, 128)]
+            moved.append(x[:, lanes - 128 :] if cgrid else moved[0])
+            return jnp.concatenate(
+                [jnp.where(lane_last, moved[t + 1], moved[t]) for t in range(lanes // 128)], axis=1
+            )
 
         def lane_prior(x, i):
-            moved = pltpu.roll(x, 1, 1)
-            if not cgrid:
-                return moved
-            ghost = pltpu.roll(lane_edge[i], lax.rem(128 - 2 * k, 128), 1)
-            ghost = jnp.concatenate([ghost] * (lanes // 128), axis=1)
-            return jnp.where(lane_first, ghost, moved)
+            moved = [pltpu.roll(x[:, t : t + 128], 1, 1) for t in range(0, lanes, 128)]
+            if cgrid:
+                moved.insert(0, pltpu.roll(lane_edge[i], lax.rem(128 - 2 * k, 128), 1))
+            else:
+                moved.insert(0, moved[-1])
+            return jnp.concatenate(
+                [jnp.where(lane_first, moved[t], moved[t + 1]) for t in range(lanes // 128)], axis=1
+            )
 
         gm = metric_ref[metric_rows[0], b]
         gs = metric_ref[metric_rows[1], b]
         gl = metric_ref[metric_rows[2], b]
-        gm2, gs2, gl2 = gm * gm, gs * gs, gl * gl
+        gm2, gs2, gl2 = viscosity * gm * gm, viscosity * gs * gs, viscosity * gl * gl
+        gm, gs, gl = damping * gm, damping * gs, damping * gl
+        all2 = 2.0 * (gm2 + gs2 + gl2)
+        all6 = 6.0 * (gm + gs + gl)
         mine = [prim[here, i] for i in range(5)]
         viscous = {}
-        for i, field, c, e in ((0, 0, 1, 10), (1, 1, 2, 11), (2, 2, 3, 12), (4, 4, 4, 13)):
-            x = mine[field]
-            twice = 2.0 * x
-            total = gm2 * (prim[above, i] + prim[below, i] - twice)
-            total += gs2 * (sub_next(x, e) + sub_prior(x, e) - twice)
-            total += gl2 * (lane_next(x) + lane_prior(x, e) - twice)
-            viscous[c] = total if c == 4 else viscosity * total
+        for i, c, e in ((0, 1, 10), (1, 2, 11), (2, 3, 12), (4, 4, 13)):
+            x = mine[i]
+            total = gm2 * (prim[above, i] + prim[below, i])
+            total += gs2 * (sub_next(x, e) + sub_prior(x, e))
+            total += gl2 * (lane_next(x) + lane_prior(x, e))
+            viscous[c] = total - all2 * x
         q = [qe[c, k + 2] for c in range(5)]
         sub_flux = flux(q, mine, sub_m)
         lane_flux = flux(q, mine, lane_m)
-        next_flux = flux([qe[c, k + 3] for c in range(5)], [prim[above, i] for i in range(5)], major_m)
-        prior_flux = flux([qe[c, k + 1] for c in range(5)], [prim[below, i] for i in range(5)], major_m)
         for c in range(5):
             x = q[c]
-            middle = (6.0 * damping) * x
-            eighth = 0.125 * x
-            bend = (
-                0.125 * (qe[c, k + 3] + qe[c, k + 1])
-                - damping * (qe[c, k + 4] + qe[c, k])
-                - 0.5 * (next_flux[c] - prior_flux[c])
-                - middle
+            four = 4.0 * x
+            total = gm * (
+                4.0 * (qe[c, k + 3] + qe[c, k + 1])
+                - (qe[c, k + 4] + qe[c, k])
+                - (prim[above, 5 + c] - prim[below, 5 + c])
             )
-            total = gm * bend
-            half = 0.5 * sub_flux[c]
-            up = eighth - half - damping * sub_next(x, 5 + c)
-            down = eighth + half - damping * sub_prior(x, 5 + c)
-            total += gs * (sub_next(up, c) + sub_prior(down, c) - middle)
-            half = 0.5 * lane_flux[c]
-            up = eighth - half - damping * lane_next(x)
-            down = eighth + half - damping * lane_prior(x, 5 + c)
-            total += gl * (lane_next(up) + lane_prior(down, c) - middle)
+            up = four - sub_flux[c] - sub_next(x, 5 + c)
+            down = four + sub_flux[c] - sub_prior(x, 5 + c)
+            total += gs * (sub_next(up, c) + sub_prior(down, c))
+            up = four - lane_flux[c] - lane_next(x)
+            down = four + lane_flux[c] - lane_prior(x, 5 + c)
+            total += gl * (lane_next(up) + lane_prior(down, c))
+            total -= all6 * x
             if c:
                 total += viscous[c]
             if not cgrid:
@@ -264,11 +282,11 @@
         out_shape=jax.ShapeDtypeStruct(q.shape, f32),
         scratch_shapes=[
             pltpu.VMEM((5, planes + 4, rows, lanes), f32),
-            pltpu.VMEM((3, 5, rows, lanes), f32),
+            pltpu.VMEM((3, 10, rows, lanes), f32),
             pltpu.VMEM((2, 14, planes, lanes), f32),
         ]
         + [pltpu.VMEM((14, rows, 128), f32)] * cgrid
-        + [pltpu.SemaphoreType.DMA((3,))],
+        + [pltpu.SemaphoreType.DMA((planes // step_planes + 2,))],
         compiler_params=params(),
         cost_estimate=pl.CostEstimate(
             flops=300 * planes * rows * lanes, bytes_accessed=60 * planes * rows * lanes, transcendentals=0
@@ -312,7 +330,24 @@
 
 
 def donor_kernel(
-    cell_ref, frac_ref, q_ref, out_ref, planes, pieces, rank_ref, ordered, where_ref, first, partial, table, sem
+    cell_ref,
+    frac_ref,
+    q_ref,
+    out_ref,
+    wrap_lo,
+    wrap_hi,
+    span_lo,
+    span_hi,
+    wall,
+    planes,
+    pieces,
+    rank_ref,
+    ordered,
+    where_ref,
+    first,
+    partial,
+    table,
+    sem,
 ):
     spans, rows, lanes = q_ref.shape[1:]
     count, slots = cell_ref.shape
@@ -320,6 +355,7 @@
     tiles = count * slots // tile
     wide = slots // 128
     one, zero = jnp.ones((), bf16), jnp.zeros((), bf16)
+    pack(q_ref, wrap_lo, wrap_hi, span_lo, span_hi, wall)
 
     def prepare(k, _):
         for c in range(5):
@@ -466,12 +502,14 @@
     _, spans, rows, lanes = state.shape
     count, slots = cell.shape
     tiles = count * slots // 256
+    shapes = [(count, 5, slots)]
+    shapes += [(5, 2, spans, lanes)] * 2 + [(5, 2, rows, lanes)] * 2 + [(5, rows, 2 * spans)]
     return pl.pallas_call(
         donor_kernel,
         grid=(1,),
         in_specs=[whole(cell.shape), whole(frac.shape), whole(state.shape)],
-        out_specs=whole((count, 5, slots)),
-        out_shape=jax.ShapeDtypeStruct((count, 5, slots), f32),
+        out_specs=[whole(x) for x in shapes],
+        out_shape=[jax.ShapeDtypeStruct(x, f32) for x in shapes],
         scratch_shapes=[
             pltpu.VMEM(((spans + 1) * 5 * rows, 3 * lanes), bf16),
             pltpu.VMEM((9, count, slots), f32),
@@ -555,22 +593,25 @@
 ):
     wrap_count = lax.axis_size("wrap")
 
+    def ring(axis):
+        size = lax.axis_size(axis)
+        return [(i, (i + 1) % size) for i in range(size if axis == "span" else size - 1)]
+
     def onward(value, axis):
-        size = lax.axis_size(axis)
-        return lax.ppermute(value, axis, [(i, (i + 1) % size) for i in range(size)])
+        return lax.ppermute(value, axis, ring(axis))
 
     def back(value, axis):
-        size = lax.axis_size(axis)
-        return lax.ppermute(value, axis, [((i + 1) % size, i) for i in range(size)])
-
-    wrap_lo, wrap_hi, span_lo, span_hi, wall = pack(cgrid_state)
+        return lax.ppermute(value, axis, [(j, i) for i, j in ring(axis)])
+
+    slot, wrap_lo, wrap_hi, span_lo, span_hi, wall = donors(
+        donor_cell[0], jnp.transpose(donor_frac[0], (1, 0, 2)), cgrid_state
+    )
     far = lax.ppermute(
-        wall, "wrap", [(i, wrap_count - 1 - i) for i in range(wrap_count)]
+        wall, "wrap", [(i, wrap_count - 1 - i) for i in range(wrap_count) if wrapped(i, wrap_count)]
     )
     majors = (onward(span_hi, "span"), back(span_lo, "span"))
     subs = (onward(wrap_hi, "wrap"), back(wrap_lo, "wrap"))
 
-    slot = donors(donor_cell[0], jnp.transpose(donor_frac[0], (1, 0, 2)), cgrid_state)
     slot = lax.all_to_all(slot, "wrap", split_axis=0, concat_axis=0, tiled=True)
 
     turned = lambda x: jnp.swapaxes(x, -3, -2)

time: 105 us -> 107 us (1.019); the launches traced: 104 us -> 105 us
  starting transfers between devices: 29.1 us -> 32.1 us
  Pallas kernels: 71.9 us -> 69.5 us
    pallas_call x1 -> x0, Pallas kernels: 3.1 us -> none  [pack(): pl.pallas_call(pack_kernel, in_specs=[whole(state.shape)], out_specs=[who...]
    ppermute x1, starting transfers between devices: 4.13 us -> 6.66 us  [body(): lax.ppermute(wall, 'wrap', [(i, wrap_count - 1 - i) for i in range(wrap_c...]
  transfers between devices with their start and end apart: 10 -> 10, of which waited for: 0 -> 0; matrix products, arithmetic and copies ran while one was open for 0% -> 0% of each run, Pallas kernels for 38% -> 35%
where the time goes in v3:
time: 107 us; the launch traced here: 105 us
  Pallas kernels  69.5 us (65%)
  starting transfers between devices  32.1 us (30%)
  local copies, waits for them, and re-layouts  2.46 us (2%)
    pallas_call x2, Pallas kernels, rate(): pl.pallas_call(functools.partial(rate_kernel, cgrid=cgrid, step_planes=st...  25.4 us
    pallas_call x1, Pallas kernels, fill(): pl.pallas_call(fill_kernel, grid=(planes,), in_specs=[plane, plane, state...  22.1 us
    pallas_call x1, Pallas kernels, donors(): pl.pallas_call(donor_kernel, grid=(1,), in_specs=[whole(cell.shape), whol...  22 us
    ppermute x4, starting transfers between devices, back(): return lax.ppermute(value, axis, [(j, i) for i, j in ring(axis)])  13.3 us
    ppermute x1, starting transfers between devices, body(): lax.ppermute(wall, 'wrap', [(i, wrap_count - 1 - i) for i in range(wrap_c...  6.66 us
    ppermute x4, starting transfers between devices, onward(): return lax.ppermute(value, axis, ring(axis))  6.24 us
    all_to_all x1, starting transfers between devices, body(): slot = lax.all_to_all(slot, 'wrap', split_axis=0, concat_axis=0, tiled=True)  5.93 us
    unnamed x20, local copies, waits for them, and re-layouts  2.46 us
  transfers between devices with their start and end apart: 10, of which 0 were waited for; matrix products, arithmetic and copies ran while one was open for 0% of the time, Pallas kernels for 35%

profile of v3, /device:TPU:0, one launch (start us, length us, event | category | flops | bytes accessed | tf_op | source)
XLA Modules:
  0.0 104.9 jit_solution(3838277268895112200)
XLA Ops:
  0.6 22.0 %donors.1 = (f32[8,5,1024]{2,1,0:T(8,128)}, f32[5,2,16,256]{3,2,1,0:T(8,128)}, f32[5,2,16,256]{3,2,1,0:T(8,128)}, f32[5,2,32,256]{3,2,1,0:T(8,128)}, f32[5,2,32,256]{3,2,1,0:T(8,128)}, /*index=5*/f32[5,32,32]{2,1,0:T(8,128)}) custom-call(s32[8,1024]{1,0:T(8,128)} %bitcast.14, f32[3,8,1024]{2,1,0:T(8,128)} %bitcast.13, f32[5,16,32,256]{3,2,1,0:T(8,128)} %q_hbm.1), custom_call_target="tpu_custom_call" | custom-call | tf_op jit(solution)/shard_map/donors/pallas_call | solution.py:507
  22.6 5.9 %all-to-all-start = ((f32[8,5,1024]{2,1,0:T(8,128)}), f32[8,5,1024]{2,1,0:T(8,128)S(1)}, u32[]{:S(2)}, u32[]{:S(2)}) async-start(f32[8,5,1024]{2,1,0:T(8,128)} %get-tuple-element.18), calls=%async_computation | async-start | bytes 524288 | tf_op jit(solution)/shard_map/all_to_all | solution.py:615
  28.5 3.9 %collective-permute-start.2 = (f32[5,2,16,256]{3,2,1,0:T(8,128)}, f32[5,2,16,256]{3,2,1,0:T(8,128)S(1)}, u32[]{:S(2)}, u32[]{:S(2)}) collective-permute-start(f32[5,2,16,256]{3,2,1,0:T(8,128)} %get-tuple-element.15.refs_1_), channel_id=1, source_target_pairs={{0,16},{16,32},{32,48},{48,64},{64,80},{80,96},{96,112},{1,17},{17... | collective-permute-start | bytes 491528 | tf_op jit(solution)/shard_map/ppermute | solution.py:601
  32.5 1.3 %collective-permute-start.3 = (f32[5,2,16,256]{3,2,1,0:T(8,128)}, f32[5,2,16,256]{3,2,1,0:T(8,128)S(1)}, u32[]{:S(2)}, u32[]{:S(2)}) collective-permute-start(f32[5,2,16,256]{3,2,1,0:T(8,128)} %get-tuple-element.16.refs_0_), channel_id=1, source_target_pairs={{16,0},{32,16},{48,32},{64,48},{80,64},{96,80},{112,96},{17,1},{33... | collective-permute-start | bytes 491528 | tf_op jit(solution)/shard_map/ppermute | solution.py:604
  33.8 6.7 %collective-permute-start.4 = (f32[5,32,32]{2,1,0:T(8,128)}, f32[5,32,32]{2,1,0:T(8,128)S(1)}, u32[]{:S(2)}, u32[]{:S(2)}) collective-permute-start(f32[5,32,32]{2,1,0:T(8,128)} %get-tuple-element.17.refs_2_), channel_id=1, source_target_pairs={{0,112},{16,96},{96,16},{112,0},{1,113},{17,97},{97,17},{113,1},{2... | collective-permute-start | bytes 61448 | tf_op jit(solution)/shard_map/ppermute | solution.py:609
  40.4 0.1 collective-permute-start
  40.5 5.3 %collective-permute-start.1 = (f32[5,2,32,256]{3,2,1,0:T(8,128)}, f32[5,2,32,256]{3,2,1,0:T(8,128)S(1)}, u32[]{:S(2)}, u32[]{:S(2)}) collective-permute-start(f32[5,2,32,256]{3,2,1,0:T(8,128)} %get-tuple-element.14), channel_id=1, source_target_pairs={{1,0},{2,1},{3,2},{4,3},{5,4},{6,5},{7,6},{8,7},{9,8},{10,9},{11,1... | collective-permute-start | bytes 983048 | tf_op jit(solution)/shard_map/ppermute | solution.py:604
  45.9 0.0 all-to-all-done.slot_ref
  45.9 0.7 copy-done.6
  46.6 22.1 %fill.1 = (f32[5,12,16,512]{3,2,1,0:T(8,128)}, f32[5,2,16,512]{3,2,1,0:T(8,128)}, f32[5,2,16,512]{3,2,1,0:T(8,128)}, f32[5,2,12,512]{3,2,1,0:T(8,128)}, f32[5,2,12,512]{3,2,1,0:T(8,128)}) custom-call(s32[12,16,512]{2,1,0:T(8,128)} %bitcast.16, s32[12,16,512]{2,1,0:T(8,128)} %bitcast.11, f32[5,12,16,512]{3,2,1,0:T(8,128)} %bitcast.15, f32[8,5,1024]{2,1,0:T(8,128)} %copy-done.6), custom_call_target="tpu_custom_call" | custom-call | flops 24000000000 | bytes 6000000 | tf_op jit(solution)/shard_map/fill/pallas_call | solution.py:578
  68.7 0.0 collective-permute-done.4.refs_3_
  68.7 2.2 %collective-permute-start.5 = (f32[5,2,16,512]{3,2,1,0:T(8,128)}, f32[5,2,16,512]{3,2,1,0:T(8,128)S(1)}, u32[]{:S(2)}, u32[]{:S(2)}) collective-permute-start(f32[5,2,16,512]{3,2,1,0:T(8,128)} %get-tuple-element.20), channel_id=1, source_target_pairs={{0,16},{16,32},{32,48},{48,64},{64,80},{80,96},{96,112},{1,17},{17... | collective-permute-start | bytes 983048 | tf_op jit(solution)/shard_map/ppermute | solution.py:601
  70.9 0.0 collective-permute-done.2.sub_lo
  70.9 1.3 %collective-permute-start.6 = (f32[5,2,16,512]{3,2,1,0:T(8,128)}, f32[5,2,16,512]{3,2,1,0:T(8,128)S(1)}, u32[]{:S(2)}, u32[]{:S(2)}) collective-permute-start(f32[5,2,16,512]{3,2,1,0:T(8,128)} %get-tuple-element.21), channel_id=1, source_target_pairs={{16,0},{32,16},{48,32},{64,48},{80,64},{96,80},{112,96},{17,1},{33... | collective-permute-start | bytes 983048 | tf_op jit(solution)/shard_map/ppermute | solution.py:604
  72.2 0.0 collective-permute-done.3.sub_hi
  72.2 0.0 copy-start.8
  72.2 0.1 collective-permute-start.7
  72.3 0.0 collective-permute-done.major_lo
  72.3 5.3 %collective-permute-start.8 = (f32[5,2,12,512]{3,2,1,0:T(8,128)}, f32[5,2,12,512]{3,2,1,0:T(8,128)S(1)}, u32[]{:S(2)}, u32[]{:S(2)}) collective-permute-start(f32[5,2,12,512]{3,2,1,0:T(8,128)} %get-tuple-element.23), channel_id=1, source_target_pairs={{1,0},{2,1},{3,2},{4,3},{5,4},{6,5},{7,6},{8,7},{9,8},{10,9},{11,1... | collective-permute-start | bytes 737288 | tf_op jit(solution)/shard_map/ppermute | solution.py:604
  77.7 0.0 collective-permute-done.1.major_hi
  77.7 0.0 copy-start.1
  77.7 0.7 copy-done.1
  78.4 14.4 %cgrid_rate.1 = f32[5,16,32,256]{3,2,1,0:T(8,128)} custom-call(f32[5,16,32,256]{3,2,1,0:T(8,128)} %q_hbm.1, f32[5,2,32,256]{3,2,1,0:T(8,128)} %copy-done, f32[5,2,32,256]{3,2,1,0:T(8,128)} %copy-done.1, f32[5,2,16,256]{3,2,1,0:T(8,128)} %copy-done.7, f32[5,2,16,256]{3,2,1,0:T(8,128)} %copy-done.8, f32[5,2,16,256]{3,2,1,0:T(8,128)} %get-tuple-element.16.refs_0_, ...), custom_call_target="tpu_custom_call" | custom-call | flops 39321600 | bytes 7864320 | tf_op jit(solution)/shard_map/cgrid_rate/pallas_call | solution.py:271
  92.8 0.0 collective-permute-done.7.sub_lo
  92.8 0.0 collective-permute-done.8.sub_hi
  92.8 0.0 collective-permute-done.5.major_lo
  92.9 0.0 collective-permute-done.6.major_hi
  92.9 0.6 copy-done.4
  93.5 0.1 copy-done.5
  93.7 0.1 copy-done.2
  93.8 0.1 copy-done.3
  93.9 11.0 %flap_rate.1 = f32[5,12,16,512]{3,2,1,0:T(8,128)} custom-call(f32[5,12,16,512]{3,2,1,0:T(8,128)} %get-tuple-element.19.q_hbm, f32[5,2,16,512]{3,2,1,0:T(8,128)} %copy-done.2, f32[5,2,16,512]{3,2,1,0:T(8,128)} %copy-done.3, f32[5,2,12,512]{3,2,1,0:T(8,128)} %copy-done.4, f32[5,2,12,512]{3,2,1,0:T(8,128)} %copy-done.5, s32[12,16,512]{2,1,0:T(8,128)} %bitcast.12, ...), custom_call_target="tpu_custom_call" | custom-call | flops 29491200 | bytes 5898240 | tf_op jit(solution)/shard_map/flap_rate/pallas_call | solution.py:271
  (12 shorter events, 0.0 us)
Async XLA Ops:
  22.6 23.3 %all-to-all-start = ((f32[8,5,1024]{2,1,0:T(8,128)}), f32[8,5,1024]{2,1,0:T(8,128)S(1)}, u32[]{:S(2)}, u32[]{:S(2)}) async-start(f32[8,5,1024]{2,1,0:T(8,128)} %get-tuple-element.18), calls=%async_computation | async-start | bytes 524288 | tf_op jit(solution)/shard_map/all_to_all | solution.py:615
  28.5 42.4 %collective-permute-start.2 = (f32[5,2,16,256]{3,2,1,0:T(8,128)}, f32[5,2,16,256]{3,2,1,0:T(8,128)S(1)}, u32[]{:S(2)}, u32[]{:S(2)}) collective-permute-start(f32[5,2,16,256]{3,2,1,0:T(8,128)} %get-tuple-element.15.refs_1_), channel_id=1, source_target_pairs={{0,16},{16,32},{32,48},{48,64},{64,80},{80,96},{96,112},{1,17},{17... | collective-permute-start | bytes 491528 | tf_op jit(solution)/shard_map/ppermute | solution.py:601
  32.5 39.8 %collective-permute-start.3 = (f32[5,2,16,256]{3,2,1,0:T(8,128)}, f32[5,2,16,256]{3,2,1,0:T(8,128)S(1)}, u32[]{:S(2)}, u32[]{:S(2)}) collective-permute-start(f32[5,2,16,256]{3,2,1,0:T(8,128)} %get-tuple-element.16.refs_0_), channel_id=1, source_target_pairs={{16,0},{32,16},{48,32},{64,48},{80,64},{96,80},{112,96},{17,1},{33... | collective-permute-start | bytes 491528 | tf_op jit(solution)/shard_map/ppermute | solution.py:604
  33.8 35.0 %collective-permute-start.4 = (f32[5,32,32]{2,1,0:T(8,128)}, f32[5,32,32]{2,1,0:T(8,128)S(1)}, u32[]{:S(2)}, u32[]{:S(2)}) collective-permute-start(f32[5,32,32]{2,1,0:T(8,128)} %get-tuple-element.17.refs_2_), channel_id=1, source_target_pairs={{0,112},{16,96},{96,16},{112,0},{1,113},{17,97},{97,17},{113,1},{2... | collective-permute-start | bytes 61448 | tf_op jit(solution)/shard_map/ppermute | solution.py:609
  40.4 31.9 %collective-permute-start = (f32[5,2,32,256]{3,2,1,0:T(8,128)}, f32[5,2,32,256]{3,2,1,0:T(8,128)S(1)}, u32[]{:S(2)}, u32[]{:S(2)}) collective-permute-start(f32[5,2,32,256]{3,2,1,0:T(8,128)} %get-tuple-element.13), channel_id=1, source_target_pairs={{0,1},{1,2},{2,3},{3,4},{4,5},{5,6},{6,7},{7,8},{8,9},{9,10},{10,1... | collective-permute-start | bytes 983048 | tf_op jit(solution)/shard_map/ppermute | solution.py:601
  40.5 37.2 %collective-permute-start.1 = (f32[5,2,32,256]{3,2,1,0:T(8,128)}, f32[5,2,32,256]{3,2,1,0:T(8,128)S(1)}, u32[]{:S(2)}, u32[]{:S(2)}) collective-permute-start(f32[5,2,32,256]{3,2,1,0:T(8,128)} %get-tuple-element.14), channel_id=1, source_target_pairs={{1,0},{2,1},{3,2},{4,3},{5,4},{6,5},{7,6},{8,7},{9,8},{10,9},{11,1... | collective-permute-start | bytes 983048 | tf_op jit(solution)/shard_map/ppermute | solution.py:604
  45.9 0.7 copy-start.6
  68.7 9.0 %copy-start.9 = (f32[5,32,32]{2,1,0:T(8,128)}, f32[5,32,32]{2,1,0:T(8,128)S(1)}, u32[]{:S(2)}) copy-start(f32[5,32,32]{2,1,0:T(8,128)S(1)} %collective-permute-done.4.refs_3_) | copy-start | bytes 61444
  68.7 24.1 %collective-permute-start.5 = (f32[5,2,16,512]{3,2,1,0:T(8,128)}, f32[5,2,16,512]{3,2,1,0:T(8,128)S(1)}, u32[]{:S(2)}, u32[]{:S(2)}) collective-permute-start(f32[5,2,16,512]{3,2,1,0:T(8,128)} %get-tuple-element.20), channel_id=1, source_target_pairs={{0,16},{16,32},{32,48},{48,64},{64,80},{80,96},{96,112},{1,17},{17... | collective-permute-start | bytes 983048 | tf_op jit(solution)/shard_map/ppermute | solution.py:601
  70.9 6.8 %copy-start.7 = (f32[5,2,16,256]{3,2,1,0:T(8,128)}, f32[5,2,16,256]{3,2,1,0:T(8,128)S(1)}, u32[]{:S(2)}) copy-start(f32[5,2,16,256]{3,2,1,0:T(8,128)S(1)} %collective-permute-done.2.sub_lo) | copy-start | bytes 491524
  70.9 21.9 %collective-permute-start.6 = (f32[5,2,16,512]{3,2,1,0:T(8,128)}, f32[5,2,16,512]{3,2,1,0:T(8,128)S(1)}, u32[]{:S(2)}, u32[]{:S(2)}) collective-permute-start(f32[5,2,16,512]{3,2,1,0:T(8,128)} %get-tuple-element.21), channel_id=1, source_target_pairs={{16,0},{32,16},{48,32},{64,48},{80,64},{96,80},{112,96},{17,1},{33... | collective-permute-start | bytes 983048 | tf_op jit(solution)/shard_map/ppermute | solution.py:604
  72.2 5.5 %copy-start.8 = (f32[5,2,16,256]{3,2,1,0:T(8,128)}, f32[5,2,16,256]{3,2,1,0:T(8,128)S(1)}, u32[]{:S(2)}) copy-start(f32[5,2,16,256]{3,2,1,0:T(8,128)S(1)} %collective-permute-done.3.sub_hi) | copy-start | bytes 491524
  72.2 20.6 %collective-permute-start.7 = (f32[5,2,12,512]{3,2,1,0:T(8,128)}, f32[5,2,12,512]{3,2,1,0:T(8,128)S(1)}, u32[]{:S(2)}, u32[]{:S(2)}) collective-permute-start(f32[5,2,12,512]{3,2,1,0:T(8,128)} %get-tuple-element.22), channel_id=1, source_target_pairs={{0,1},{1,2},{2,3},{3,4},{4,5},{5,6},{6,7},{7,8},{8,9},{9,10},{10,1... | collective-permute-start | bytes 737288 | tf_op jit(solution)/shard_map/ppermute | solution.py:601
  72.3 5.4 %copy-start = (f32[5,2,32,256]{3,2,1,0:T(8,128)}, f32[5,2,32,256]{3,2,1,0:T(8,128)S(1)}, u32[]{:S(2)}) copy-start(f32[5,2,32,256]{3,2,1,0:T(8,128)S(1)} %collective-permute-done.major_lo) | copy-start | bytes 983044
  72.3 20.5 %collective-permute-start.8 = (f32[5,2,12,512]{3,2,1,0:T(8,128)}, f32[5,2,12,512]{3,2,1,0:T(8,128)S(1)}, u32[]{:S(2)}, u32[]{:S(2)}) collective-permute-start(f32[5,2,12,512]{3,2,1,0:T(8,128)} %get-tuple-element.23), channel_id=1, source_target_pairs={{1,0},{2,1},{3,2},{4,3},{5,4},{6,5},{7,6},{8,7},{9,8},{10,9},{11,1... | collective-permute-start | bytes 737288 | tf_op jit(solution)/shard_map/ppermute | solution.py:604
  77.7 0.7 copy-start.1
  92.8 0.7 copy-start.4
  92.8 0.8 copy-start.5
  92.9 0.9 copy-start.2
  92.9 1.0 copy-start.3

commit v4 on v3

--- a/solution.py
+++ b/solution.py
@@ -10,7 +10,8 @@
 viscosity = 0.05
 conduction = 0.07
 damping = 1.0 / 32.0
-VMEM_LIMIT = 56 * 1024 * 1024
+VMEM_LIMIT = 40 * 1024 * 1024
+IN_VMEM = pl.BlockSpec(memory_space=pltpu.VMEM)
 GROUP = 8
 
 f32, bf16, i32 = jnp.float32, jnp.bfloat16, jnp.int32
@@ -277,7 +278,7 @@
             metric_rows=metric_rows,
         ),
         grid=(planes // step_planes,),
-        in_specs=[anywhere] * 3 + [whole(x.shape) for x in (*subs, *extras)] + last_specs,
+        in_specs=[anywhere] + [IN_VMEM] * (4 + len(extras)) + last_specs,
         out_specs=block(5),
         out_shape=jax.ShapeDtypeStruct(q.shape, f32),
         scratch_shapes=[
@@ -302,7 +303,8 @@
 
 def lookup(both, at):
     width = at.shape[1]
-    highs = both.shape[0] // 10
+    highs = 32
+    components = both.shape[0] // (2 * highs)
     cells = lax.broadcasted_iota(i32, (256, width), 0).astype(f32).astype(bf16)
     sub = lax.broadcasted_iota(i32, (8, width), 0)
     pick = jnp.where(
@@ -312,14 +314,31 @@
     found = jnp.dot(both, pick, preferred_element_type=f32)
     masks = [sub + 8 * g == high for g in range(highs // 8)]
     values = []
-    for c in range(5):
+    for c in range(components):
         value = None
         for g, mask in enumerate(masks):
             r = c * highs + 8 * g
-            piece = found[r : r + 8] + found[5 * highs + r : 5 * highs + r + 8]
+            remainder = components * highs + r
+            piece = found[r : r + 8] + found[remainder : remainder + 8]
             value = jnp.where(mask, piece, 0.0 if value is None else value)
         values.append(jnp.sum(value, axis=0, keepdims=True))
     return values
+
+
+def take_lanes(values, lanes):
+    return lax.gather(
+        values,
+        lanes[..., None],
+        lax.GatherDimensionNumbers(
+            offset_dims=(),
+            collapsed_slice_dims=(1,),
+            start_index_map=(1,),
+            operand_batching_dims=(0,),
+            start_indices_batching_dims=(0,),
+        ),
+        slice_sizes=(1, 1),
+        mode=lax.GatherScatterMode.PROMISE_IN_BOUNDS,
+    )
 
 
 def add_remainders(table):
@@ -526,32 +545,48 @@
     )(cell, frac, state)
 
 
-def fill_kernel(from_ref, mask_ref, q_ref, slot_ref, out_ref, norm_lo, norm_hi, span_lo, span_hi, table):
+def fill_kernel(
+    from_ref, mask_ref, q_ref, slot_ref, out_ref, norm_lo, norm_hi, span_lo, span_hi, table, spread
+):
     planes = pl.num_programs(0)
     rows, lanes = from_ref.shape[1:]
-    low = 256
-    highs = table.shape[0] // 10
+    count, _, slots = slot_ref.shape
     j = pl.program_id(0)
 
     @pl.when(j == 0)
     def _():
-        per = slot_ref.shape[2] // low
-        for c in range(5):
-            for w in range(slot_ref.shape[0]):
+        per = slots // 256
+        for c in range(4):
+            for w in range(count):
                 for r in range(per):
-                    value = slot_ref[w, c : c + 1, r * low : (r + 1) * low]
-                    table[c * highs + w * per + r : c * highs + w * per + r + 1, :] = value
+                    at = c * count * per + w * per + r
+                    table[at : at + 1, :] = slot_ref[w, c : c + 1, r * 256 : (r + 1) * 256]
         add_remainders(table)
+        for w in range(count):
+            for r in range(slots // 128):
+                value = slot_ref[w, 4:5, r * 128 : (r + 1) * 128]
+                spread[w * (slots // 128) + r] = jnp.broadcast_to(value, (8, 128))
 
     both = table[...].astype(bf16)
-
-    def row(s, _):
-        keep = mask_ref[0, pl.ds(s, 1), :] == 1
-        for c, value in enumerate(lookup(both, from_ref[0, pl.ds(s, 1), :])):
-            out_ref[c, 0, pl.ds(s, 1), :] = jnp.where(keep, q_ref[c, 0, pl.ds(s, 1), :], value)
-        return 0
-
-    lax.fori_loop(0, rows, row, 0, unroll=16)
+    lines = spread.shape[0]
+    share = (rows // 8) * (lanes // 128) * lines // rows
+    value = None
+    for s in range(rows):
+        keep = mask_ref[0, s : s + 1, :] == 1
+        for c, found in enumerate(lookup(both, from_ref[0, s : s + 1, :])):
+            out_ref[c, 0, s : s + 1, :] = jnp.where(keep, q_ref[c, 0, s : s + 1, :], found)
+        for n in range(s * share, (s + 1) * share):
+            line = n % lines
+            if line == 0:
+                row, lane = divmod(n // lines, lanes // 128)
+                here = (slice(8 * row, 8 * row + 8), slice(128 * lane, 128 * lane + 128))
+                at = from_ref[0, here[0], here[1]]
+                low, high = at & 127, at // 128
+                value = jnp.zeros((8, 128), f32)
+            value = jnp.where(high == line, take_lanes(spread[line], low), value)
+            if line == lines - 1:
+                keep = mask_ref[0, here[0], here[1]] == 1
+                out_ref[4, 0, here[0], here[1]] = jnp.where(keep, q_ref[4, 0, here[0], here[1]], value)
 
     for c in range(5):
         for l in range(2):
@@ -578,10 +613,13 @@
     return pl.pallas_call(
         fill_kernel,
         grid=(planes,),
-        in_specs=[plane, plane, state_plane, whole(slot.shape)],
+        in_specs=[plane, plane, state_plane, IN_VMEM],
         out_specs=[state_plane] + [whole(s) for s in edges],
         out_shape=[jax.ShapeDtypeStruct(s, f32) for s in [state.shape] + edges],
-        scratch_shapes=[pltpu.VMEM((10 * count * slots // 256, 256), f32)],
+        scratch_shapes=[
+            pltpu.VMEM((8 * count * slots // 256, 256), f32),
+            pltpu.VMEM((count * slots // 128, 8, 128), f32),
+        ],
         compiler_params=params(),
         cost_estimate=pl.CostEstimate(flops=24 * 10**9, bytes_accessed=6 * 10**6, transcendentals=0),
         name="fill",
@@ -595,7 +633,7 @@
 
     def ring(axis):
         size = lax.axis_size(axis)
-        return [(i, (i + 1) % size) for i in range(size if axis == "span" else size - 1)]
+        return [(i, (i + 1) % size) for i in range(size)]
 
     def onward(value, axis):
         return lax.ppermute(value, axis, ring(axis))
@@ -607,7 +645,9 @@
         donor_cell[0], jnp.transpose(donor_frac[0], (1, 0, 2)), cgrid_state
     )
     far = lax.ppermute(
-        wall, "wrap", [(i, wrap_count - 1 - i) for i in range(wrap_count) if wrapped(i, wrap_count)]
+        wall,
+        "wrap",
+        [(i, wrap_count - 1 - i if wrapped(i, wrap_count) else i) for i in range(wrap_count)],
     )
     majors = (onward(span_hi, "span"), back(span_lo, "span"))
     subs = (onward(wrap_hi, "wrap"), back(wrap_lo, "wrap"))

time: 107 us -> 92.6 us (0.87); the launches traced: 105 us -> 92.2 us
  Pallas kernels: 69.5 us -> 57.5 us
  starting transfers between devices: 32.1 us -> 29 us
  local copies, waits for them, and re-layouts: 2.46 us -> 4.95 us
    pallas_call x1, Pallas kernels: 22.1 us -> 17 us  [fill(): pl.pallas_call(fill_kernel, grid=(planes,), in_specs=[plane, plane, state...]
    pallas_call x2, Pallas kernels: 25.4 us -> 20.3 us  [rate(): pl.pallas_call(functools.partial(rate_kernel, cgrid=cgrid, step_planes=st...]
    ppermute x4, starting transfers between devices: 6.24 us -> 2.42 us  [onward(): return lax.ppermute(value, axis, ring(axis))]
    ppermute x4, starting transfers between devices: 13.3 us -> 16.7 us  [back(): return lax.ppermute(value, axis, [(j, i) for i, j in ring(axis)])]
    ppermute x1, starting transfers between devices: 6.66 us -> 3.89 us  [body(): lax.ppermute(wall, 'wrap', [(i, wrap_count - 1 - i if wrapped(i, wrap_cou...]
    unnamed x20 -> x18, local copies, waits for them, and re-layouts: 2.46 us -> 4.95 us
    pallas_call x1, Pallas kernels: 22 us -> 20.3 us  [donors(): pl.pallas_call(donor_kernel, grid=(1,), in_specs=[whole(cell.shape), whol...]
  transfers between devices with their start and end apart: 10 -> 10, of which waited for: 0 -> 0; matrix products, arithmetic and copies ran while one was open for 0% -> 0% of each run, Pallas kernels for 35% -> 31%
where the time goes in v4:
time: 92.6 us; the launch traced here: 92.2 us
  Pallas kernels  57.5 us (62%)
  starting transfers between devices  29 us (31%)
  local copies, waits for them, and re-layouts  4.95 us (5%)
    pallas_call x2, Pallas kernels, rate(): pl.pallas_call(functools.partial(rate_kernel, cgrid=cgrid, step_planes=st...  20.3 us
    pallas_call x1, Pallas kernels, donors(): pl.pallas_call(donor_kernel, grid=(1,), in_specs=[whole(cell.shape), whol...  20.3 us
    pallas_call x1, Pallas kernels, fill(): pl.pallas_call(fill_kernel, grid=(planes,), in_specs=[plane, plane, state...  17 us
    ppermute x4, starting transfers between devices, back(): return lax.ppermute(value, axis, [(j, i) for i, j in ring(axis)])  16.7 us
    all_to_all x1, starting transfers between devices, body(): slot = lax.all_to_all(slot, 'wrap', split_axis=0, concat_axis=0, tiled=True)  5.93 us
    unnamed x18, local copies, waits for them, and re-layouts  4.95 us
    ppermute x1, starting transfers between devices, body(): lax.ppermute(wall, 'wrap', [(i, wrap_count - 1 - i if wrapped(i, wrap_cou...  3.89 us
    ppermute x4, starting transfers between devices, onward(): return lax.ppermute(value, axis, ring(axis))  2.42 us
  transfers between devices with their start and end apart: 10, of which 0 were waited for; matrix products, arithmetic and copies ran while one was open for 0% of the time, Pallas kernels for 31%

profile of v4, /device:TPU:0, one launch (start us, length us, event | category | flops | bytes accessed | tf_op | source)
XLA Modules:
  0.0 92.2 jit_solution(511390184592559852)
XLA Ops:
  0.6 0.0 copy-start
  0.6 1.7 %copy-done = f32[5,16,32,256]{3,2,1,0:T(8,128)S(1)} copy-done((f32[5,16,32,256]{3,2,1,0:T(8,128)S(1)}, f32[5,16,32,256]{3,2,1,0:T(8,128)}, u32[]{:S(2)}) %copy-start) | copy-done | bytes 2621464
  2.4 0.9 copy-done.5
  3.3 0.8 copy-done.6
  4.0 20.3 %donors.1 = (f32[8,5,1024]{2,1,0:T(8,128)}, f32[5,2,16,256]{3,2,1,0:T(8,128)S(1)}, f32[5,2,16,256]{3,2,1,0:T(8,128)S(1)}, f32[5,2,32,256]{3,2,1,0:T(8,128)S(1)},...) custom-call(s32[8,1024]{1,0:T(8,128)S(1)} %bitcast.13, f32[3,8,1024]{2,1,0:T(8,128)S(1)} %bitcast.12, ...), custom_call_target="tpu_custom_call" | custom-call | tf_op jit(solution)/shard_map/donors/pallas_call | solution.py:526
  24.3 5.9 %all-to-all-start = ((f32[8,5,1024]{2,1,0:T(8,128)}), f32[8,5,1024]{2,1,0:T(8,128)S(1)}, u32[]{:S(2)}, u32[]{:S(2)}) async-start(f32[8,5,1024]{2,1,0:T(8,128)} %get-tuple-element.18), calls=%async_computation | async-start | bytes 524288 | tf_op jit(solution)/shard_map/all_to_all | solution.py:655
  30.2 2.0 %collective-permute-start.2 = (f32[5,2,16,256]{3,2,1,0:T(8,128)S(1)}, f32[5,2,16,256]{3,2,1,0:T(8,128)S(1)}, u32[]{:S(2)}, u32[]{:S(2)}) collective-permute-start(f32[5,2,16,256]{3,2,1,0:T(8,128)S(1)} %get-tuple-element.15.refs_1_), channel_id=1, source_target_pairs={{0,16},{16,32},{32,48},{48,64},{64,80},{80,96},{96,112},{112,0},{1... | collective-permute-start | bytes 491528 | tf_op jit(solution)/shard_map/ppermute | solution.py:639
  32.3 2.1 %collective-permute-start.3 = (f32[5,2,16,256]{3,2,1,0:T(8,128)S(1)}, f32[5,2,16,256]{3,2,1,0:T(8,128)S(1)}, u32[]{:S(2)}, u32[]{:S(2)}) collective-permute-start(f32[5,2,16,256]{3,2,1,0:T(8,128)S(1)} %get-tuple-element.16.refs_0_), channel_id=1, source_target_pairs={{16,0},{32,16},{48,32},{64,48},{80,64},{96,80},{112,96},{0,112},{1... | collective-permute-start | bytes 491528 | tf_op jit(solution)/shard_map/ppermute | solution.py:642
  34.4 3.9 %collective-permute-start.4 = (f32[5,32,32]{2,1,0:T(8,128)S(1)}, f32[5,32,32]{2,1,0:T(8,128)S(1)}, u32[]{:S(2)}, u32[]{:S(2)}) collective-permute-start(f32[5,32,32]{2,1,0:T(8,128)S(1)} %get-tuple-element.17.refs_2_), channel_id=1, source_target_pairs={{0,112},{16,96},{32,32},{48,48},{64,64},{80,80},{96,16},{112,0},{1... | collective-permute-start | bytes 61448 | tf_op jit(solution)/shard_map/ppermute | solution.py:647
  38.3 0.1 collective-permute-start
  38.4 5.3 %collective-permute-start.1 = (f32[5,2,32,256]{3,2,1,0:T(8,128)S(1)}, f32[5,2,32,256]{3,2,1,0:T(8,128)S(1)}, u32[]{:S(2)}, u32[]{:S(2)}) collective-permute-start(f32[5,2,32,256]{3,2,1,0:T(8,128)S(1)} %get-tuple-element.14), channel_id=1, source_target_pairs={{1,0},{2,1},{3,2},{4,3},{5,4},{6,5},{7,6},{8,7},{9,8},{10,9},{11,1... | collective-permute-start | bytes 983048 | tf_op jit(solution)/shard_map/ppermute | solution.py:642
  43.7 0.0 all-to-all-done.slot_ref
  43.7 0.0 copy-start.7
  43.8 1.5 %copy-done.7 = f32[5,16,12,512]{3,1,2,0:T(8,128)S(1)} copy-done((f32[5,16,12,512]{3,1,2,0:T(8,128)S(1)}, f32[5,16,12,512]{3,1,2,0:T(8,128)}, u32[]{:S(2)}) %copy-start.7) | copy-done | bytes 1966104
  45.3 17.0 %fill.1 = (f32[5,12,16,512]{3,2,1,0:T(8,128)S(1)}, f32[5,2,16,512]{3,2,1,0:T(8,128)S(1)}, f32[5,2,16,512]{3,2,1,0:T(8,128)S(1)}, f32[5,2,12,512]{3,2,1,0:T(8,128)S(1)}, f32[5,2,12,512]{3,2,1,0:T(8,128)S(1)}) custom-call(s32[12,16,512]{2,1,0:T(8,128)S(1)} %bitcast.15, s32[12,16,512]{2,1,0:T(8,128)S(1)} %bitcast.10, f32[5,12,16,512]{3,2,1,0:T(8,128)S(1)} %bitcast.14, ...), custom_call_target="tpu_custom_call" | custom-call | flops 24000000000 | bytes 6000000 | tf_op jit(solution)/shard_map/fill/pallas_call | solution.py:613
  62.3 0.0 collective-permute-done.4.refs_3_
  62.3 0.3 collective-permute-start.5
  62.6 0.0 collective-permute-done.2.sub_lo
  62.6 3.9 %collective-permute-start.6 = (f32[5,2,16,512]{3,2,1,0:T(8,128)S(1)}, f32[5,2,16,512]{3,2,1,0:T(8,128)S(1)}, u32[]{:S(2)}, u32[]{:S(2)}) collective-permute-start(f32[5,2,16,512]{3,2,1,0:T(8,128)S(1)} %get-tuple-element.21), channel_id=1, source_target_pairs={{16,0},{32,16},{48,32},{64,48},{80,64},{96,80},{112,96},{0,112},{1... | collective-permute-start | bytes 983048 | tf_op jit(solution)/shard_map/ppermute | solution.py:642
  66.5 0.0 collective-permute-done.3.sub_hi
  66.5 0.0 collective-permute-start.7
  66.5 0.0 collective-permute-done.major_lo
  66.5 0.0 copy-start.3
  66.5 5.3 %collective-permute-start.8 = (f32[5,2,12,512]{3,2,1,0:T(8,128)S(1)}, f32[5,2,12,512]{3,2,1,0:T(8,128)S(1)}, u32[]{:S(2)}, u32[]{:S(2)}) collective-permute-start(f32[5,2,12,512]{3,2,1,0:T(8,128)S(1)} %get-tuple-element.23), channel_id=1, source_target_pairs={{1,0},{2,1},{3,2},{4,3},{5,4},{6,5},{7,6},{8,7},{9,8},{10,9},{11,1... | collective-permute-start | bytes 737288 | tf_op jit(solution)/shard_map/ppermute | solution.py:642
  71.8 0.0 collective-permute-done.1.major_hi
  71.9 0.0 copy-done.2
  71.9 11.7 %cgrid_rate.1 = f32[5,16,32,256]{3,2,1,0:T(8,128)} custom-call(f32[5,16,32,256]{3,2,1,0:T(8,128)S(1)} %copy-done.1, f32[5,2,32,256]{3,2,1,0:T(8,128)S(1)} %collective-permute-done.major_lo, f32[5,2,32,256]{3,2,1,0:T(8,128)S(1)} %collective-permute-done.1.major_hi, f32[5,2,16,256]{3,2,1,0:T(8,128)S(1)} %collective-permute-done.2.sub_lo, ...), custom_call_target="tpu_custom_call" | custom-call | flops 39321600 | bytes 7864320 | tf_op jit(solution)/shard_map/cgrid_rate/pallas_call | solution.py:272
  83.5 0.0 collective-permute-done.7.sub_lo
  83.5 0.0 collective-permute-done.8.sub_hi
  83.6 0.0 collective-permute-done.5.major_lo
  83.6 0.0 collective-permute-done.6.major_hi
  83.6 8.7 %flap_rate.1 = f32[5,12,16,512]{3,2,1,0:T(8,128)} custom-call(f32[5,12,16,512]{3,2,1,0:T(8,128)S(1)} %get-tuple-element.19.q_hbm, f32[5,2,16,512]{3,2,1,0:T(8,128)S(1)} %collective-permute-done.5.major_lo, f32[5,2,16,512]{3,2,1,0:T(8,128)S(1)} %collective-permute-done.6.major_hi, f32[5,2,12,512]{3,2,1,0:T(8,128)S(1)} %collective-permute-done.7.sub_lo, ...), custom_call_target="tpu_custom_call" | custom-call | flops 29491200 | bytes 5898240 | tf_op jit(solution)/shard_map/flap_rate/pallas_call | solution.py:272
  (10 shorter events, 0.0 us)
Async XLA Ops:
  0.6 1.7 %copy-start = (f32[5,16,32,256]{3,2,1,0:T(8,128)S(1)}, f32[5,16,32,256]{3,2,1,0:T(8,128)}, u32[]{:S(2)}) copy-start(f32[5,16,32,256]{3,2,1,0:T(8,128)} %q_hbm.1) | copy-start | bytes 7864324
  2.4 0.9 copy-start.5
  3.3 0.8 copy-start.6
  4.0 39.7 %copy-start.4 = (s32[16,12,512]{2,0,1:T(8,128)S(1)}, s32[16,12,512]{2,0,1:T(8,128)}, u32[]{:S(2)}) copy-start(s32[16,12,512]{2,0,1:T(8,128)} %param.12) | copy-start | bytes 1179652
  4.0 39.7 %copy-start.8 = (s32[16,12,512]{2,0,1:T(8,128)S(1)}, s32[16,12,512]{2,0,1:T(8,128)}, u32[]{:S(2)}) copy-start(s32[16,12,512]{2,0,1:T(8,128)} %param.13) | copy-start | bytes 1179652
  24.3 19.4 %all-to-all-start = ((f32[8,5,1024]{2,1,0:T(8,128)}), f32[8,5,1024]{2,1,0:T(8,128)S(1)}, u32[]{:S(2)}, u32[]{:S(2)}) async-start(f32[8,5,1024]{2,1,0:T(8,128)} %get-tuple-element.18), calls=%async_computation | async-start | bytes 524288 | tf_op jit(solution)/shard_map/all_to_all | solution.py:655
  30.2 32.4 %collective-permute-start.2 = (f32[5,2,16,256]{3,2,1,0:T(8,128)S(1)}, f32[5,2,16,256]{3,2,1,0:T(8,128)S(1)}, u32[]{:S(2)}, u32[]{:S(2)}) collective-permute-start(f32[5,2,16,256]{3,2,1,0:T(8,128)S(1)} %get-tuple-element.15.refs_1_), channel_id=1, source_target_pairs={{0,16},{16,32},{32,48},{48,64},{64,80},{80,96},{96,112},{112,0},{1... | collective-permute-start | bytes 491528 | tf_op jit(solution)/shard_map/ppermute | solution.py:639
  32.3 34.2 %collective-permute-start.3 = (f32[5,2,16,256]{3,2,1,0:T(8,128)S(1)}, f32[5,2,16,256]{3,2,1,0:T(8,128)S(1)}, u32[]{:S(2)}, u32[]{:S(2)}) collective-permute-start(f32[5,2,16,256]{3,2,1,0:T(8,128)S(1)} %get-tuple-element.16.refs_0_), channel_id=1, source_target_pairs={{16,0},{32,16},{48,32},{64,48},{80,64},{96,80},{112,96},{0,112},{1... | collective-permute-start | bytes 491528 | tf_op jit(solution)/shard_map/ppermute | solution.py:642
  34.4 27.9 %collective-permute-start.4 = (f32[5,32,32]{2,1,0:T(8,128)S(1)}, f32[5,32,32]{2,1,0:T(8,128)S(1)}, u32[]{:S(2)}, u32[]{:S(2)}) collective-permute-start(f32[5,32,32]{2,1,0:T(8,128)S(1)} %get-tuple-element.17.refs_2_), channel_id=1, source_target_pairs={{0,112},{16,96},{32,32},{48,48},{64,64},{80,80},{96,16},{112,0},{1... | collective-permute-start | bytes 61448 | tf_op jit(solution)/shard_map/ppermute | solution.py:647
  38.3 28.2 %collective-permute-start = (f32[5,2,32,256]{3,2,1,0:T(8,128)S(1)}, f32[5,2,32,256]{3,2,1,0:T(8,128)S(1)}, u32[]{:S(2)}, u32[]{:S(2)}) collective-permute-start(f32[5,2,32,256]{3,2,1,0:T(8,128)S(1)} %get-tuple-element.13), channel_id=1, source_target_pairs={{0,1},{1,2},{2,3},{3,4},{4,5},{5,6},{6,7},{7,8},{8,9},{9,10},{10,1... | collective-permute-start | bytes 983048 | tf_op jit(solution)/shard_map/ppermute | solution.py:639
  38.4 33.5 %collective-permute-start.1 = (f32[5,2,32,256]{3,2,1,0:T(8,128)S(1)}, f32[5,2,32,256]{3,2,1,0:T(8,128)S(1)}, u32[]{:S(2)}, u32[]{:S(2)}) collective-permute-start(f32[5,2,32,256]{3,2,1,0:T(8,128)S(1)} %get-tuple-element.14), channel_id=1, source_target_pairs={{1,0},{2,1},{3,2},{4,3},{5,4},{6,5},{7,6},{8,7},{9,8},{10,9},{11,1... | collective-permute-start | bytes 983048 | tf_op jit(solution)/shard_map/ppermute | solution.py:642
  43.7 1.5 %copy-start.7 = (f32[5,16,12,512]{3,1,2,0:T(8,128)S(1)}, f32[5,16,12,512]{3,1,2,0:T(8,128)}, u32[]{:S(2)}) copy-start(f32[5,16,12,512]{3,1,2,0:T(8,128)} %param.10) | copy-start | bytes 5898244
  45.3 26.6 %copy-start.1 = (f32[5,16,32,256]{3,2,1,0:T(8,128)S(1)}, f32[5,16,32,256]{3,2,1,0:T(8,128)}, u32[]{:S(2)}) copy-start(f32[5,16,32,256]{3,2,1,0:T(8,128)} %q_hbm.1) | copy-start | bytes 7864324
  45.3 26.6 %copy-start.2 = (f32[3,16,32,256]{3,2,1,0:T(8,128)S(1)}, f32[3,16,32,256]{3,2,1,0:T(8,128)}, u32[]{:S(2)}) copy-start(f32[3,16,32,256]{3,2,1,0:T(8,128)} %refs_4_.1) | copy-start | bytes 4718596
  62.3 21.3 %collective-permute-start.5 = (f32[5,2,16,512]{3,2,1,0:T(8,128)S(1)}, f32[5,2,16,512]{3,2,1,0:T(8,128)S(1)}, u32[]{:S(2)}, u32[]{:S(2)}) collective-permute-start(f32[5,2,16,512]{3,2,1,0:T(8,128)S(1)} %get-tuple-element.20), channel_id=1, source_target_pairs={{0,16},{16,32},{32,48},{48,64},{64,80},{80,96},{96,112},{112,0},{1... | collective-permute-start | bytes 983048 | tf_op jit(solution)/shard_map/ppermute | solution.py:639
  62.6 21.0 %collective-permute-start.6 = (f32[5,2,16,512]{3,2,1,0:T(8,128)S(1)}, f32[5,2,16,512]{3,2,1,0:T(8,128)S(1)}, u32[]{:S(2)}, u32[]{:S(2)}) collective-permute-start(f32[5,2,16,512]{3,2,1,0:T(8,128)S(1)} %get-tuple-element.21), channel_id=1, source_target_pairs={{16,0},{32,16},{48,32},{64,48},{80,64},{96,80},{112,96},{0,112},{1... | collective-permute-start | bytes 983048 | tf_op jit(solution)/shard_map/ppermute | solution.py:642
  66.5 17.1 %collective-permute-start.7 = (f32[5,2,12,512]{3,2,1,0:T(8,128)S(1)}, f32[5,2,12,512]{3,2,1,0:T(8,128)S(1)}, u32[]{:S(2)}, u32[]{:S(2)}) collective-permute-start(f32[5,2,12,512]{3,2,1,0:T(8,128)S(1)} %get-tuple-element.22), channel_id=1, source_target_pairs={{0,1},{1,2},{2,3},{3,4},{4,5},{5,6},{6,7},{7,8},{8,9},{9,10},{10,1... | collective-permute-start | bytes 737288 | tf_op jit(solution)/shard_map/ppermute | solution.py:639
  66.5 17.1 %copy-start.3 = (f32[3,16,12,512]{3,1,2,0:T(8,128)S(1)}, f32[3,16,12,512]{3,1,2,0:T(8,128)}, u32[]{:S(2)}) copy-start(f32[3,16,12,512]{3,1,2,0:T(8,128)} %param.11) | copy-start | bytes 3538948
  66.5 17.0 %collective-permute-start.8 = (f32[5,2,12,512]{3,2,1,0:T(8,128)S(1)}, f32[5,2,12,512]{3,2,1,0:T(8,128)S(1)}, u32[]{:S(2)}, u32[]{:S(2)}) collective-permute-start(f32[5,2,12,512]{3,2,1,0:T(8,128)S(1)} %get-tuple-element.23), channel_id=1, source_target_pairs={{1,0},{2,1},{3,2},{4,3},{5,4},{6,5},{7,6},{8,7},{9,8},{10,9},{11,1... | collective-permute-start | bytes 737288 | tf_op jit(solution)/shard_map/ppermute | solution.py:642

commit v5 on v4

--- a/solution.py
+++ b/solution.py
@@ -11,6 +11,7 @@
 conduction = 0.07
 damping = 1.0 / 32.0
 VMEM_LIMIT = 40 * 1024 * 1024
+IN_HBM = pl.BlockSpec(memory_space=pltpu.HBM)
 IN_VMEM = pl.BlockSpec(memory_space=pltpu.VMEM)
 GROUP = 8
 
@@ -351,13 +352,14 @@
 def donor_kernel(
     cell_ref,
     frac_ref,
-    q_ref,
+    q_hbm,
     out_ref,
     wrap_lo,
     wrap_hi,
     span_lo,
     span_hi,
     wall,
+    q_ref,
     planes,
     pieces,
     rank_ref,
@@ -366,7 +368,7 @@
     first,
     partial,
     table,
-    sem,
+    sems,
 ):
     spans, rows, lanes = q_ref.shape[1:]
     count, slots = cell_ref.shape
@@ -374,19 +376,8 @@
     tiles = count * slots // tile
     wide = slots // 128
     one, zero = jnp.ones((), bf16), jnp.zeros((), bf16)
-    pack(q_ref, wrap_lo, wrap_hi, span_lo, span_hi, wall)
-
-    def prepare(k, _):
-        for c in range(5):
-            high, low = split_two(q_ref[c, k])
-            here = pl.ds(pl.multiple_of(k * 5 * rows + c * rows, 16), rows)
-            planes[here, 0:lanes] = high
-            planes[here, lanes : 2 * lanes] = low
-            planes[here, 2 * lanes : 3 * lanes] = high
-        return 0
-
-    lax.fori_loop(0, spans, prepare, 0)
-    planes[spans * 5 * rows :, :] = jnp.zeros((5 * rows, 3 * lanes), bf16)
+    fetch = pltpu.make_async_copy(q_hbm, q_ref, sems.at[0])
+    fetch.start()
 
     cell = cell_ref[...]
     upper = jnp.floor((cell.astype(f32) + 0.5) * (1.0 / (lanes - 1)))
@@ -441,10 +432,24 @@
         )
         return 0
 
-    lax.fori_loop(0, count, order, 0)
+    lax.fori_loop(0, count, order, 0, unroll=4)
     where_ref[...] = ordered[0:tiles, :].astype(i32)
-    copy = pltpu.make_async_copy(where_ref, first, sem)
+    copy = pltpu.make_async_copy(where_ref, first, sems.at[1])
     copy.start()
+
+    fetch.wait()
+    pack(q_ref, wrap_lo, wrap_hi, span_lo, span_hi, wall)
+
+    def prepare(k, _):
+        for c in range(5):
+            high, low = split_two(q_ref[c, k])
+            here = pl.ds(pl.multiple_of(k * 5 * rows + c * rows, 16), rows)
+            planes[here, 0:lanes] = high
+            planes[here, lanes : 2 * lanes] = low
+            planes[here, 2 * lanes : 3 * lanes] = high
+        return 0
+
+    lax.fori_loop(0, spans, prepare, 0)
     copy.wait()
 
     def weights(cells, at, frac):
@@ -457,15 +462,19 @@
 
         span, wrap, normal = piece(0).astype(i32), piece(1).astype(i32), piece(2).astype(i32)
         f0, f1, f2 = [piece(3 + 2 * d) + piece(4 + 2 * d) for d in range(3)]
-        high, low = split_two(weights(lanes, normal, f2))
+        cells = lax.broadcasted_iota(i32, (lanes, tile), 0).astype(f32).astype(bf16)
+        at_lower, at_upper = [cells == (normal + n).astype(f32).astype(bf16) for n in range(2)]
+        (lower_high, lower_low), (upper_high, upper_low) = split_two(1.0 - f2), split_two(f2)
+        high = jnp.where(at_lower, lower_high, jnp.where(at_upper, upper_high, zero))
+        low = jnp.where(at_lower, lower_low, jnp.where(at_upper, upper_low, zero))
         return span, f0, jnp.concatenate([high, high, low], axis=0), weights(rows, wrap, f1)
 
-    def pair(k, made, sums):
+    def add_planes(k, number, made, sums):
         span, f0, along, across = made
-        from_row = pl.ds(pl.multiple_of(k * 5 * rows, 16), 10 * rows)
+        from_row = pl.ds(pl.multiple_of(k * 5 * rows, 16), number * 5 * rows)
         mixed = jnp.dot(planes[from_row, :], along, preferred_element_type=f32)
         new = list(sums)
-        for n in range(2):
+        for n in range(number):
             ws = jnp.where(span == k + n, 1.0 - f0, jnp.where(span + 1 == k + n, f0, 0.0))
             for c in range(5):
                 r0 = (5 * n + c) * rows
@@ -478,19 +487,19 @@
     def step(g, _):
         for n in range(GROUP):
             i = g * GROUP + n
-            for c, x in enumerate(pair(first[i, 0], tile_of(i), (None,) * 5)):
+            for c, x in enumerate(add_planes(first[i, 0], 2, tile_of(i), (None,) * 5)):
                 partial[n, c] = x
         for n in range(GROUP):
             i = g * GROUP + n
             lowest = first[i, 0]
-            more = (first[i, tile - 1] + 1 - lowest) // 2
+            more = first[i, tile - 1] - lowest
 
             @pl.when(more > 0)
             def _():
                 made = tile_of(i)
 
                 def again(m, _):
-                    sums = pair(lowest + 2 + 2 * m, made, tuple(partial[n, c] for c in range(5)))
+                    sums = add_planes(lowest + 2 + m, 1, made, tuple(partial[n, c] for c in range(5)))
                     for c in range(5):
                         partial[n, c] = sums[c]
                     return 0
@@ -526,11 +535,12 @@
     return pl.pallas_call(
         donor_kernel,
         grid=(1,),
-        in_specs=[whole(cell.shape), whole(frac.shape), whole(state.shape)],
+        in_specs=[IN_VMEM, IN_VMEM, IN_HBM],
         out_specs=[whole(x) for x in shapes],
         out_shape=[jax.ShapeDtypeStruct(x, f32) for x in shapes],
         scratch_shapes=[
-            pltpu.VMEM(((spans + 1) * 5 * rows, 3 * lanes), bf16),
+            pltpu.VMEM(state.shape, f32),
+            pltpu.VMEM((spans * 5 * rows, 3 * lanes), bf16),
             pltpu.VMEM((9, count, slots), f32),
             pltpu.VMEM((count, slots), i32),
             pltpu.VMEM((9 * tiles, 256), f32),
@@ -538,7 +548,7 @@
             pltpu.SMEM((tiles, 256), i32),
             pltpu.VMEM((GROUP, 5, 8, 256), f32),
             pltpu.VMEM((10 * tiles, 256), f32),
-            pltpu.SemaphoreType.DMA(()),
+            pltpu.SemaphoreType.DMA((2,)),
         ],
         compiler_params=params(),
         name="donors",
@@ -546,15 +556,32 @@
 
 
 def fill_kernel(
-    from_ref, mask_ref, q_ref, slot_ref, out_ref, norm_lo, norm_hi, span_lo, span_hi, table, spread
+    from_ref,
+    mask_ref,
+    q_hbm,
+    slot_ref,
+    out_ref,
+    norm_lo,
+    norm_hi,
+    span_lo,
+    span_hi,
+    table,
+    spread,
+    q_ref,
+    sems,
 ):
     planes = pl.num_programs(0)
     rows, lanes = from_ref.shape[1:]
     count, _, slots = slot_ref.shape
     j = pl.program_id(0)
 
+    def fetch(n):
+        return pltpu.make_async_copy(q_hbm.at[:, n], q_ref.at[:, n], sems.at[n])
+
     @pl.when(j == 0)
     def _():
+        for n in range(q_ref.shape[1]):
+            fetch(n).start()
         per = slots // 256
         for c in range(4):
             for w in range(count):
@@ -567,6 +594,7 @@
                 value = slot_ref[w, 4:5, r * 128 : (r + 1) * 128]
                 spread[w * (slots // 128) + r] = jnp.broadcast_to(value, (8, 128))
 
+    fetch(j).wait()
     both = table[...].astype(bf16)
     lines = spread.shape[0]
     share = (rows // 8) * (lanes // 128) * lines // rows
@@ -574,7 +602,7 @@
     for s in range(rows):
         keep = mask_ref[0, s : s + 1, :] == 1
         for c, found in enumerate(lookup(both, from_ref[0, s : s + 1, :])):
-            out_ref[c, 0, s : s + 1, :] = jnp.where(keep, q_ref[c, 0, s : s + 1, :], found)
+            out_ref[c, 0, s : s + 1, :] = jnp.where(keep, q_ref[c, j, s : s + 1, :], found)
         for n in range(s * share, (s + 1) * share):
             line = n % lines
             if line == 0:
@@ -586,7 +614,7 @@
             value = jnp.where(high == line, take_lanes(spread[line], low), value)
             if line == lines - 1:
                 keep = mask_ref[0, here[0], here[1]] == 1
-                out_ref[4, 0, here[0], here[1]] = jnp.where(keep, q_ref[4, 0, here[0], here[1]], value)
+                out_ref[4, 0, here[0], here[1]] = jnp.where(keep, q_ref[4, j, here[0], here[1]], value)
 
     for c in range(5):
         for l in range(2):
@@ -613,12 +641,14 @@
     return pl.pallas_call(
         fill_kernel,
         grid=(planes,),
-        in_specs=[plane, plane, state_plane, IN_VMEM],
+        in_specs=[plane, plane, IN_HBM, IN_VMEM],
         out_specs=[state_plane] + [whole(s) for s in edges],
         out_shape=[jax.ShapeDtypeStruct(s, f32) for s in [state.shape] + edges],
         scratch_shapes=[
             pltpu.VMEM((8 * count * slots // 256, 256), f32),
             pltpu.VMEM((count * slots // 128, 8, 128), f32),
+            pltpu.VMEM(state.shape, f32),
+            pltpu.SemaphoreType.DMA((planes,)),
         ],
         compiler_params=params(),
         cost_estimate=pl.CostEstimate(flops=24 * 10**9, bytes_accessed=6 * 10**6, transcendentals=0),

time: 92.6 us -> 88.3 us (0.954)
  Pallas kernels: 57.5 us -> 53.2 us
    pallas_call x2, Pallas kernels: 37.2 us -> 32.9 us  [the longest x1 17.4 us: fill(): pl.pallas_call(fill_kernel, grid=(planes,), in_specs=[plane, plane, IN_HB...]
  transfers between devices with their start and end apart: 10 -> 10, of which waited for: 0 -> 0; matrix products, arithmetic and copies ran while one was open for 0% -> 0% of each run, Pallas kernels for 31% -> 33%
where the time goes in v5:
time: 88.3 us; the launch traced here: 87.9 us
  Pallas kernels  53.2 us (60%)
  starting transfers between devices  28.9 us (33%)
  local copies, waits for them, and re-layouts  4.95 us (6%)
    pallas_call x2, Pallas kernels, rate(): pl.pallas_call(functools.partial(rate_kernel, cgrid=cgrid, step_planes=st...  20.3 us
    pallas_call x1, Pallas kernels, fill(): pl.pallas_call(fill_kernel, grid=(planes,), in_specs=[plane, plane, IN_HB...  17.4 us
    ppermute x4, starting transfers between devices, back(): return lax.ppermute(value, axis, [(j, i) for i, j in ring(axis)])  16.7 us
    pallas_call x1, Pallas kernels, donors(): pl.pallas_call(donor_kernel, grid=(1,), in_specs=[IN_VMEM, IN_VMEM, IN_HB...  15.6 us
    all_to_all x1, starting transfers between devices, body(): slot = lax.all_to_all(slot, 'wrap', split_axis=0, concat_axis=0, tiled=True)  5.91 us
    unnamed x18, local copies, waits for them, and re-layouts  4.95 us
    ppermute x1, starting transfers between devices, body(): lax.ppermute(wall, 'wrap', [(i, wrap_count - 1 - i if wrapped(i, wrap_cou...  3.89 us
    ppermute x4, starting transfers between devices, onward(): return lax.ppermute(value, axis, ring(axis))  2.42 us
  transfers between devices with their start and end apart: 10, of which 0 were waited for; matrix products, arithmetic and copies ran while one was open for 0% of the time, Pallas kernels for 33%

profile of v5, /device:TPU:0, one launch (start us, length us, event | category | flops | bytes accessed | tf_op | source)
XLA Modules:
  0.0 87.9 jit_solution(3763607668836394819)
XLA Ops:
  0.6 0.0 copy-start
  0.6 1.7 %copy-done = f32[5,16,32,256]{3,2,1,0:T(8,128)S(1)} copy-done((f32[5,16,32,256]{3,2,1,0:T(8,128)S(1)}, f32[5,16,32,256]{3,2,1,0:T(8,128)}, u32[]{:S(2)}) %copy-start) | copy-done | bytes 2621464
  2.4 0.9 %copy-done.5 = f32[1,8,3,1024]{3,1,2,0:T(8,128)S(1)} copy-done((f32[1,8,3,1024]{3,1,2,0:T(8,128)S(1)}, f32[1,8,3,1024]{3,1,2,0:T(8,128)}, u32[]{:S(2)}) %copy-start.5) | copy-done | bytes 98328
  3.3 0.8 copy-done.6
  4.0 15.6 %donors.1 = (f32[8,5,1024]{2,1,0:T(8,128)}, f32[5,2,16,256]{3,2,1,0:T(8,128)S(1)}, f32[5,2,16,256]{3,2,1,0:T(8,128)S(1)}, f32[5,2,32,256]{3,2,1,0:T(8,128)S(1)},...) custom-call(s32[8,1024]{1,0:T(8,128)S(1)} %bitcast.13, f32[3,8,1024]{2,1,0:T(8,128)S(1)} %bitcast.12, ...), custom_call_target="tpu_custom_call" | custom-call | tf_op jit(solution)/shard_map/donors/pallas_call | solution.py:535
  19.6 5.9 %all-to-all-start = ((f32[8,5,1024]{2,1,0:T(8,128)}), f32[8,5,1024]{2,1,0:T(8,128)S(1)}, u32[]{:S(2)}, u32[]{:S(2)}) async-start(f32[8,5,1024]{2,1,0:T(8,128)} %get-tuple-element.18), calls=%async_computation | async-start | bytes 524288 | tf_op jit(solution)/shard_map/all_to_all | solution.py:685
  25.5 2.0 %collective-permute-start.2 = (f32[5,2,16,256]{3,2,1,0:T(8,128)S(1)}, f32[5,2,16,256]{3,2,1,0:T(8,128)S(1)}, u32[]{:S(2)}, u32[]{:S(2)}) collective-permute-start(f32[5,2,16,256]{3,2,1,0:T(8,128)S(1)} %get-tuple-element.15.refs_1_), channel_id=1, source_target_pairs={{0,16},{16,32},{32,48},{48,64},{64,80},{80,96},{96,112},{112,0},{1... | collective-permute-start | bytes 491528 | tf_op jit(solution)/shard_map/ppermute | solution.py:669
  27.5 2.1 %collective-permute-start.3 = (f32[5,2,16,256]{3,2,1,0:T(8,128)S(1)}, f32[5,2,16,256]{3,2,1,0:T(8,128)S(1)}, u32[]{:S(2)}, u32[]{:S(2)}) collective-permute-start(f32[5,2,16,256]{3,2,1,0:T(8,128)S(1)} %get-tuple-element.16.refs_0_), channel_id=1, source_target_pairs={{16,0},{32,16},{48,32},{64,48},{80,64},{96,80},{112,96},{0,112},{1... | collective-permute-start | bytes 491528 | tf_op jit(solution)/shard_map/ppermute | solution.py:672
  29.7 3.9 %collective-permute-start.4 = (f32[5,32,32]{2,1,0:T(8,128)S(1)}, f32[5,32,32]{2,1,0:T(8,128)S(1)}, u32[]{:S(2)}, u32[]{:S(2)}) collective-permute-start(f32[5,32,32]{2,1,0:T(8,128)S(1)} %get-tuple-element.17.refs_2_), channel_id=1, source_target_pairs={{0,112},{16,96},{32,32},{48,48},{64,64},{80,80},{96,16},{112,0},{1... | collective-permute-start | bytes 61448 | tf_op jit(solution)/shard_map/ppermute | solution.py:677
  33.6 0.1 collective-permute-start
  33.7 5.3 %collective-permute-start.1 = (f32[5,2,32,256]{3,2,1,0:T(8,128)S(1)}, f32[5,2,32,256]{3,2,1,0:T(8,128)S(1)}, u32[]{:S(2)}, u32[]{:S(2)}) collective-permute-start(f32[5,2,32,256]{3,2,1,0:T(8,128)S(1)} %get-tuple-element.14), channel_id=1, source_target_pairs={{1,0},{2,1},{3,2},{4,3},{5,4},{6,5},{7,6},{8,7},{9,8},{10,9},{11,1... | collective-permute-start | bytes 983048 | tf_op jit(solution)/shard_map/ppermute | solution.py:672
  39.0 0.0 all-to-all-done.slot_ref
  39.0 0.0 copy-done.4
  39.0 0.0 copy-start.7
  39.0 1.5 %copy-done.7 = f32[5,16,12,512]{3,1,2,0:T(8,128)S(1)} copy-done((f32[5,16,12,512]{3,1,2,0:T(8,128)S(1)}, f32[5,16,12,512]{3,1,2,0:T(8,128)}, u32[]{:S(2)}) %copy-start.7) | copy-done | bytes 1966104
  40.6 17.4 %fill.1 = (f32[5,12,16,512]{3,2,1,0:T(8,128)S(1)}, f32[5,2,16,512]{3,2,1,0:T(8,128)S(1)}, f32[5,2,16,512]{3,2,1,0:T(8,128)S(1)}, f32[5,2,12,512]{3,2,1,0:T(8,128)S(1)}, f32[5,2,12,512]{3,2,1,0:T(8,128)S(1)}) custom-call(s32[12,16,512]{2,1,0:T(8,128)S(1)} %bitcast.15, s32[12,16,512]{2,1,0:T(8,128)S(1)} %bitcast.10, f32[5,12,16,512]{3,2,1,0:T(8,128)S(1)} %bitcast.14, ...), custom_call_target="tpu_custom_call" | custom-call | flops 24000000000 | bytes 6000000 | tf_op jit(solution)/shard_map/fill/pallas_call | solution.py:641
  57.9 0.0 collective-permute-done.4.refs_3_
  58.0 0.3 collective-permute-start.5
  58.3 0.0 collective-permute-done.2.sub_lo
  58.3 3.9 %collective-permute-start.6 = (f32[5,2,16,512]{3,2,1,0:T(8,128)S(1)}, f32[5,2,16,512]{3,2,1,0:T(8,128)S(1)}, u32[]{:S(2)}, u32[]{:S(2)}) collective-permute-start(f32[5,2,16,512]{3,2,1,0:T(8,128)S(1)} %get-tuple-element.21), channel_id=1, source_target_pairs={{16,0},{32,16},{48,32},{64,48},{80,64},{96,80},{112,96},{0,112},{1... | collective-permute-start | bytes 983048 | tf_op jit(solution)/shard_map/ppermute | solution.py:672
  62.2 0.0 collective-permute-done.3.sub_hi
  62.2 0.0 collective-permute-start.7
  62.2 0.0 collective-permute-done.major_lo
  62.2 0.0 copy-start.3
  62.2 5.3 %collective-permute-start.8 = (f32[5,2,12,512]{3,2,1,0:T(8,128)S(1)}, f32[5,2,12,512]{3,2,1,0:T(8,128)S(1)}, u32[]{:S(2)}, u32[]{:S(2)}) collective-permute-start(f32[5,2,12,512]{3,2,1,0:T(8,128)S(1)} %get-tuple-element.23), channel_id=1, source_target_pairs={{1,0},{2,1},{3,2},{4,3},{5,4},{6,5},{7,6},{8,7},{9,8},{10,9},{11,1... | collective-permute-start | bytes 737288 | tf_op jit(solution)/shard_map/ppermute | solution.py:672
  67.5 0.0 collective-permute-done.1.major_hi
  67.5 11.7 %cgrid_rate.1 = f32[5,16,32,256]{3,2,1,0:T(8,128)} custom-call(f32[5,16,32,256]{3,2,1,0:T(8,128)S(1)} %copy-done.1, f32[5,2,32,256]{3,2,1,0:T(8,128)S(1)} %collective-permute-done.major_lo, f32[5,2,32,256]{3,2,1,0:T(8,128)S(1)} %collective-permute-done.1.major_hi, f32[5,2,16,256]{3,2,1,0:T(8,128)S(1)} %collective-permute-done.2.sub_lo, ...), custom_call_target="tpu_custom_call" | custom-call | flops 39321600 | bytes 7864320 | tf_op jit(solution)/shard_map/cgrid_rate/pallas_call | solution.py:273
  79.2 0.0 collective-permute-done.7.sub_lo
  79.2 0.0 collective-permute-done.8.sub_hi
  79.2 0.0 collective-permute-done.5.major_lo
  79.2 0.0 collective-permute-done.6.major_hi
  79.3 8.7 %flap_rate.1 = f32[5,12,16,512]{3,2,1,0:T(8,128)} custom-call(f32[5,12,16,512]{3,2,1,0:T(8,128)S(1)} %get-tuple-element.19.q_hbm, f32[5,2,16,512]{3,2,1,0:T(8,128)S(1)} %collective-permute-done.5.major_lo, f32[5,2,16,512]{3,2,1,0:T(8,128)S(1)} %collective-permute-done.6.major_hi, f32[5,2,12,512]{3,2,1,0:T(8,128)S(1)} %collective-permute-done.7.sub_lo, ...), custom_call_target="tpu_custom_call" | custom-call | flops 29491200 | bytes 5898240 | tf_op jit(solution)/shard_map/flap_rate/pallas_call | solution.py:273
  (10 shorter events, 0.0 us)
Async XLA Ops:
  0.6 1.7 %copy-start = (f32[5,16,32,256]{3,2,1,0:T(8,128)S(1)}, f32[5,16,32,256]{3,2,1,0:T(8,128)}, u32[]{:S(2)}) copy-start(f32[5,16,32,256]{3,2,1,0:T(8,128)} %q_hbm.3) | copy-start | bytes 7864324
  2.4 0.9 %copy-start.5 = (f32[1,8,3,1024]{3,1,2,0:T(8,128)S(1)}, f32[1,8,3,1024]{3,1,2,0:T(8,128)}, u32[]{:S(2)}) copy-start(f32[1,8,3,1024]{3,1,2,0:T(8,128)} %param.15) | copy-start | bytes 294916
  3.3 0.8 copy-start.6
  4.0 35.0 %copy-start.4 = (s32[16,12,512]{2,0,1:T(8,128)S(1)}, s32[16,12,512]{2,0,1:T(8,128)}, u32[]{:S(2)}) copy-start(s32[16,12,512]{2,0,1:T(8,128)} %param.12) | copy-start | bytes 1179652
  4.0 35.0 %copy-start.8 = (s32[16,12,512]{2,0,1:T(8,128)S(1)}, s32[16,12,512]{2,0,1:T(8,128)}, u32[]{:S(2)}) copy-start(s32[16,12,512]{2,0,1:T(8,128)} %param.13) | copy-start | bytes 1179652
  19.6 19.4 %all-to-all-start = ((f32[8,5,1024]{2,1,0:T(8,128)}), f32[8,5,1024]{2,1,0:T(8,128)S(1)}, u32[]{:S(2)}, u32[]{:S(2)}) async-start(f32[8,5,1024]{2,1,0:T(8,128)} %get-tuple-element.18), calls=%async_computation | async-start | bytes 524288 | tf_op jit(solution)/shard_map/all_to_all | solution.py:685
  25.5 32.8 %collective-permute-start.2 = (f32[5,2,16,256]{3,2,1,0:T(8,128)S(1)}, f32[5,2,16,256]{3,2,1,0:T(8,128)S(1)}, u32[]{:S(2)}, u32[]{:S(2)}) collective-permute-start(f32[5,2,16,256]{3,2,1,0:T(8,128)S(1)} %get-tuple-element.15.refs_1_), channel_id=1, source_target_pairs={{0,16},{16,32},{32,48},{48,64},{64,80},{80,96},{96,112},{112,0},{1... | collective-permute-start | bytes 491528 | tf_op jit(solution)/shard_map/ppermute | solution.py:669
  27.5 34.6 %collective-permute-start.3 = (f32[5,2,16,256]{3,2,1,0:T(8,128)S(1)}, f32[5,2,16,256]{3,2,1,0:T(8,128)S(1)}, u32[]{:S(2)}, u32[]{:S(2)}) collective-permute-start(f32[5,2,16,256]{3,2,1,0:T(8,128)S(1)} %get-tuple-element.16.refs_0_), channel_id=1, source_target_pairs={{16,0},{32,16},{48,32},{64,48},{80,64},{96,80},{112,96},{0,112},{1... | collective-permute-start | bytes 491528 | tf_op jit(solution)/shard_map/ppermute | solution.py:672
  29.7 28.3 %collective-permute-start.4 = (f32[5,32,32]{2,1,0:T(8,128)S(1)}, f32[5,32,32]{2,1,0:T(8,128)S(1)}, u32[]{:S(2)}, u32[]{:S(2)}) collective-permute-start(f32[5,32,32]{2,1,0:T(8,128)S(1)} %get-tuple-element.17.refs_2_), channel_id=1, source_target_pairs={{0,112},{16,96},{32,32},{48,48},{64,64},{80,80},{96,16},{112,0},{1... | collective-permute-start | bytes 61448 | tf_op jit(solution)/shard_map/ppermute | solution.py:677
  33.6 28.6 %collective-permute-start = (f32[5,2,32,256]{3,2,1,0:T(8,128)S(1)}, f32[5,2,32,256]{3,2,1,0:T(8,128)S(1)}, u32[]{:S(2)}, u32[]{:S(2)}) collective-permute-start(f32[5,2,32,256]{3,2,1,0:T(8,128)S(1)} %get-tuple-element.13), channel_id=1, source_target_pairs={{0,1},{1,2},{2,3},{3,4},{4,5},{5,6},{6,7},{7,8},{8,9},{9,10},{10,1... | collective-permute-start | bytes 983048 | tf_op jit(solution)/shard_map/ppermute | solution.py:669
  33.7 33.9 %collective-permute-start.1 = (f32[5,2,32,256]{3,2,1,0:T(8,128)S(1)}, f32[5,2,32,256]{3,2,1,0:T(8,128)S(1)}, u32[]{:S(2)}, u32[]{:S(2)}) collective-permute-start(f32[5,2,32,256]{3,2,1,0:T(8,128)S(1)} %get-tuple-element.14), channel_id=1, source_target_pairs={{1,0},{2,1},{3,2},{4,3},{5,4},{6,5},{7,6},{8,7},{9,8},{10,9},{11,1... | collective-permute-start | bytes 983048 | tf_op jit(solution)/shard_map/ppermute | solution.py:672
  39.0 1.5 %copy-start.7 = (f32[5,16,12,512]{3,1,2,0:T(8,128)S(1)}, f32[5,16,12,512]{3,1,2,0:T(8,128)}, u32[]{:S(2)}) copy-start(f32[5,16,12,512]{3,1,2,0:T(8,128)} %param.10) | copy-start | bytes 5898244
  40.6 27.0 %copy-start.1 = (f32[5,16,32,256]{3,2,1,0:T(8,128)S(1)}, f32[5,16,32,256]{3,2,1,0:T(8,128)}, u32[]{:S(2)}) copy-start(f32[5,16,32,256]{3,2,1,0:T(8,128)} %q_hbm.3) | copy-start | bytes 7864324
  40.6 27.0 %copy-start.2 = (f32[3,16,32,256]{3,2,1,0:T(8,128)S(1)}, f32[3,16,32,256]{3,2,1,0:T(8,128)}, u32[]{:S(2)}) copy-start(f32[3,16,32,256]{3,2,1,0:T(8,128)} %refs_4_.1) | copy-start | bytes 4718596
  58.0 21.3 %collective-permute-start.5 = (f32[5,2,16,512]{3,2,1,0:T(8,128)S(1)}, f32[5,2,16,512]{3,2,1,0:T(8,128)S(1)}, u32[]{:S(2)}, u32[]{:S(2)}) collective-permute-start(f32[5,2,16,512]{3,2,1,0:T(8,128)S(1)} %get-tuple-element.20), channel_id=1, source_target_pairs={{0,16},{16,32},{32,48},{48,64},{64,80},{80,96},{96,112},{112,0},{1... | collective-permute-start | bytes 983048 | tf_op jit(solution)/shard_map/ppermute | solution.py:669
  58.3 21.0 %collective-permute-start.6 = (f32[5,2,16,512]{3,2,1,0:T(8,128)S(1)}, f32[5,2,16,512]{3,2,1,0:T(8,128)S(1)}, u32[]{:S(2)}, u32[]{:S(2)}) collective-permute-start(f32[5,2,16,512]{3,2,1,0:T(8,128)S(1)} %get-tuple-element.21), channel_id=1, source_target_pairs={{16,0},{32,16},{48,32},{64,48},{80,64},{96,80},{112,96},{0,112},{1... | collective-permute-start | bytes 983048 | tf_op jit(solution)/shard_map/ppermute | solution.py:672
  62.2 17.1 %collective-permute-start.7 = (f32[5,2,12,512]{3,2,1,0:T(8,128)S(1)}, f32[5,2,12,512]{3,2,1,0:T(8,128)S(1)}, u32[]{:S(2)}, u32[]{:S(2)}) collective-permute-start(f32[5,2,12,512]{3,2,1,0:T(8,128)S(1)} %get-tuple-element.22), channel_id=1, source_target_pairs={{0,1},{1,2},{2,3},{3,4},{4,5},{5,6},{6,7},{7,8},{8,9},{9,10},{10,1... | collective-permute-start | bytes 737288 | tf_op jit(solution)/shard_map/ppermute | solution.py:669
  62.2 17.1 %copy-start.3 = (f32[3,16,12,512]{3,1,2,0:T(8,128)S(1)}, f32[3,16,12,512]{3,1,2,0:T(8,128)}, u32[]{:S(2)}) copy-start(f32[3,16,12,512]{3,1,2,0:T(8,128)} %param.11) | copy-start | bytes 3538948
  62.2 17.0 %collective-permute-start.8 = (f32[5,2,12,512]{3,2,1,0:T(8,128)S(1)}, f32[5,2,12,512]{3,2,1,0:T(8,128)S(1)}, u32[]{:S(2)}, u32[]{:S(2)}) collective-permute-start(f32[5,2,12,512]{3,2,1,0:T(8,128)S(1)} %get-tuple-element.23), channel_id=1, source_target_pairs={{1,0},{2,1},{3,2},{4,3},{5,4},{6,5},{7,6},{8,7},{9,8},{10,9},{11,1... | collective-permute-start | bytes 737288 | tf_op jit(solution)/shard_map/ppermute | solution.py:672

commit v6 on v5

--- a/solution.py
+++ b/solution.py
@@ -22,8 +22,8 @@
     return pl.BlockSpec(shape, lambda *_: (0,) * len(shape))
 
 
-def params():
-    return pltpu.CompilerParams(vmem_limit_bytes=VMEM_LIMIT)
+def params(limit=VMEM_LIMIT):
+    return pltpu.CompilerParams(vmem_limit_bytes=limit)
 
 
 def primitives(q):
@@ -550,7 +550,7 @@
             pltpu.VMEM((10 * tiles, 256), f32),
             pltpu.SemaphoreType.DMA((2,)),
         ],
-        compiler_params=params(),
+        compiler_params=params(60 * 1024 * 1024),
         name="donors",
     )(cell, frac, state)
 
@@ -650,7 +650,7 @@
             pltpu.VMEM(state.shape, f32),
             pltpu.SemaphoreType.DMA((planes,)),
         ],
-        compiler_params=params(),
+        compiler_params=params(52 * 1024 * 1024),
         cost_estimate=pl.CostEstimate(flops=24 * 10**9, bytes_accessed=6 * 10**6, transcendentals=0),
         name="fill",
     )(source, mask, state, slot)

time: 88.3 us -> 86.6 us (0.981)
  local copies, waits for them, and re-layouts: 4.95 us -> 0.04 us
  Pallas kernels: 53.2 us -> 56.4 us
    unnamed x18, local copies, waits for them, and re-layouts: 4.95 us -> 0.04 us
    pallas_call x1, Pallas kernels: 17.4 us -> 19.8 us  [fill(): pl.pallas_call(fill_kernel, grid=(planes,), in_specs=[plane, plane, IN_HB...]
  transfers between devices with their start and end apart: 10 -> 10, of which waited for: 0 -> 0; matrix products, arithmetic and copies ran while one was open for 0% -> 0% of each run, Pallas kernels for 33% -> 36%
where the time goes in v6:
time: 86.6 us; the launch traced here: 86.3 us
  Pallas kernels  56.4 us (65%)
  starting transfers between devices  29 us (33%)
    pallas_call x2, Pallas kernels, rate(): pl.pallas_call(functools.partial(rate_kernel, cgrid=cgrid, step_planes=st...  20.3 us
    pallas_call x1, Pallas kernels, fill(): pl.pallas_call(fill_kernel, grid=(planes,), in_specs=[plane, plane, IN_HB...  19.8 us
    ppermute x4, starting transfers between devices, back(): return lax.ppermute(value, axis, [(j, i) for i, j in ring(axis)])  16.8 us
    pallas_call x1, Pallas kernels, donors(): pl.pallas_call(donor_kernel, grid=(1,), in_specs=[IN_VMEM, IN_VMEM, IN_HB...  16.4 us
    all_to_all x1, starting transfers between devices, body(): slot = lax.all_to_all(slot, 'wrap', split_axis=0, concat_axis=0, tiled=True)  5.91 us
    ppermute x1, starting transfers between devices, body(): lax.ppermute(wall, 'wrap', [(i, wrap_count - 1 - i if wrapped(i, wrap_cou...  3.89 us
    ppermute x4, starting transfers between devices, onward(): return lax.ppermute(value, axis, ring(axis))  2.42 us
  transfers between devices with their start and end apart: 10, of which 0 were waited for; matrix products, arithmetic and copies ran while one was open for 0% of the time, Pallas kernels for 36%

profile of v6, /device:TPU:0, one launch (start us, length us, event | category | flops | bytes accessed | tf_op | source)
XLA Modules:
  0.0 86.3 jit_solution(9660795938719837484)
XLA Ops:
  0.6 0.0 copy-start.8
  0.6 16.4 %donors.1 = (f32[8,5,1024]{2,1,0:T(8,128)}, f32[5,2,16,256]{3,2,1,0:T(8,128)}, f32[5,2,16,256]{3,2,1,0:T(8,128)}, f32[5,2,32,256]{3,2,1,0:T(8,128)}, f32[5,2,32,256]{3,2,1,0:T(8,128)}, /*index=5*/f32[5,32,32]{2,1,0:T(8,128)}) custom-call(s32[8,1024]{1,0:T(8,128)} %bitcast.15, f32[3,8,1024]{2,1,0:T(8,128)} %bitcast.14, f32[5,16,32,256]{3,2,1,0:T(8,128)} %q_hbm.3), custom_call_target="tpu_custom_call" | custom-call | tf_op jit(solution)/shard_map/donors/pallas_call | solution.py:535
  17.0 5.9 %all-to-all-start = ((f32[8,5,1024]{2,1,0:T(8,128)}), f32[8,5,1024]{2,1,0:T(8,128)S(1)}, u32[]{:S(2)}, u32[]{:S(2)}) async-start(f32[8,5,1024]{2,1,0:T(8,128)} %get-tuple-element.18), calls=%async_computation | async-start | bytes 524288 | tf_op jit(solution)/shard_map/all_to_all | solution.py:685
  22.9 2.0 %collective-permute-start.2 = (f32[5,2,16,256]{3,2,1,0:T(8,128)}, f32[5,2,16,256]{3,2,1,0:T(8,128)S(1)}, u32[]{:S(2)}, u32[]{:S(2)}) collective-permute-start(f32[5,2,16,256]{3,2,1,0:T(8,128)} %get-tuple-element.15.refs_1_), channel_id=1, source_target_pairs={{0,16},{16,32},{32,48},{48,64},{64,80},{80,96},{96,112},{112,0},{1... | collective-permute-start | bytes 491528 | tf_op jit(solution)/shard_map/ppermute | solution.py:669
  24.9 2.1 %collective-permute-start.3 = (f32[5,2,16,256]{3,2,1,0:T(8,128)}, f32[5,2,16,256]{3,2,1,0:T(8,128)S(1)}, u32[]{:S(2)}, u32[]{:S(2)}) collective-permute-start(f32[5,2,16,256]{3,2,1,0:T(8,128)} %get-tuple-element.16.refs_0_), channel_id=1, source_target_pairs={{16,0},{32,16},{48,32},{64,48},{80,64},{96,80},{112,96},{0,112},{1... | collective-permute-start | bytes 491528 | tf_op jit(solution)/shard_map/ppermute | solution.py:672
  27.1 3.9 %collective-permute-start.4 = (f32[5,32,32]{2,1,0:T(8,128)}, f32[5,32,32]{2,1,0:T(8,128)S(1)}, u32[]{:S(2)}, u32[]{:S(2)}) collective-permute-start(f32[5,32,32]{2,1,0:T(8,128)} %get-tuple-element.17.refs_2_), channel_id=1, source_target_pairs={{0,112},{16,96},{32,32},{48,48},{64,64},{80,80},{96,16},{112,0},{1... | collective-permute-start | bytes 61448 | tf_op jit(solution)/shard_map/ppermute | solution.py:677
  31.0 0.1 collective-permute-start
  31.1 5.3 %collective-permute-start.1 = (f32[5,2,32,256]{3,2,1,0:T(8,128)}, f32[5,2,32,256]{3,2,1,0:T(8,128)S(1)}, u32[]{:S(2)}, u32[]{:S(2)}) collective-permute-start(f32[5,2,32,256]{3,2,1,0:T(8,128)} %get-tuple-element.14), channel_id=1, source_target_pairs={{1,0},{2,1},{3,2},{4,3},{5,4},{6,5},{7,6},{8,7},{9,8},{10,9},{11,1... | collective-permute-start | bytes 983048 | tf_op jit(solution)/shard_map/ppermute | solution.py:672
  36.4 0.0 all-to-all-done.slot_ref
  36.4 0.0 copy-done.8
  36.5 19.8 %fill.1 = (f32[5,12,16,512]{3,2,1,0:T(8,128)}, f32[5,2,16,512]{3,2,1,0:T(8,128)S(1)}, f32[5,2,16,512]{3,2,1,0:T(8,128)S(1)}, f32[5,2,12,512]{3,2,1,0:T(8,128)S(1)}, f32[5,2,12,512]{3,2,1,0:T(8,128)S(1)}) custom-call(s32[12,16,512]{2,1,0:T(8,128)S(1)} %bitcast.12, s32[12,16,512]{2,1,0:T(8,128)} %bitcast.10, f32[5,12,16,512]{3,2,1,0:T(8,128)} %bitcast.16, ...), custom_call_target="tpu_custom_call" | custom-call | flops 24000000000 | bytes 6000000 | tf_op jit(solution)/shard_map/fill/pallas_call | solution.py:641
  56.2 0.0 collective-permute-done.4.refs_3_
  56.2 0.3 collective-permute-start.5
  56.5 0.0 collective-permute-done.2.sub_lo
  56.6 3.9 %collective-permute-start.6 = (f32[5,2,16,512]{3,2,1,0:T(8,128)S(1)}, f32[5,2,16,512]{3,2,1,0:T(8,128)S(1)}, u32[]{:S(2)}, u32[]{:S(2)}) collective-permute-start(f32[5,2,16,512]{3,2,1,0:T(8,128)S(1)} %get-tuple-element.21), channel_id=1, source_target_pairs={{16,0},{32,16},{48,32},{64,48},{80,64},{96,80},{112,96},{0,112},{1... | collective-permute-start | bytes 983048 | tf_op jit(solution)/shard_map/ppermute | solution.py:672
  60.4 0.0 collective-permute-done.3.sub_hi
  60.4 0.0 collective-permute-start.7
  60.4 0.0 collective-permute-done.major_lo
  60.5 0.0 copy-start.1
  60.5 0.0 copy-start.3
  60.5 0.0 copy-start.4
  60.5 5.4 %collective-permute-start.8 = (f32[5,2,12,512]{3,2,1,0:T(8,128)S(1)}, f32[5,2,12,512]{3,2,1,0:T(8,128)S(1)}, u32[]{:S(2)}, u32[]{:S(2)}) collective-permute-start(f32[5,2,12,512]{3,2,1,0:T(8,128)S(1)} %get-tuple-element.23), channel_id=1, source_target_pairs={{1,0},{2,1},{3,2},{4,3},{5,4},{6,5},{7,6},{8,7},{9,8},{10,9},{11,1... | collective-permute-start | bytes 737288 | tf_op jit(solution)/shard_map/ppermute | solution.py:672
  65.9 0.0 collective-permute-done.1.major_hi
  65.9 11.7 %cgrid_rate.1 = f32[5,16,32,256]{3,2,1,0:T(8,128)} custom-call(f32[5,16,32,256]{3,2,1,0:T(8,128)S(1)} %copy-done, f32[5,2,32,256]{3,2,1,0:T(8,128)S(1)} %collective-permute-done.major_lo, f32[5,2,32,256]{3,2,1,0:T(8,128)S(1)} %collective-permute-done.1.major_hi, f32[5,2,16,256]{3,2,1,0:T(8,128)S(1)} %collective-permute-done.2.sub_lo, ...), custom_call_target="tpu_custom_call" | custom-call | flops 39321600 | bytes 7864320 | tf_op jit(solution)/shard_map/cgrid_rate/pallas_call | solution.py:273
  77.6 0.0 collective-permute-done.7.sub_lo
  77.6 0.0 collective-permute-done.8.sub_hi
  77.6 0.0 collective-permute-done.5.major_lo
  77.6 0.0 collective-permute-done.6.major_hi
  77.6 0.0 copy-done.1
  77.7 0.0 copy-done.3
  77.7 0.0 copy-done.4
  77.7 8.7 %flap_rate.1 = f32[5,12,16,512]{3,2,1,0:T(8,128)} custom-call(f32[5,12,16,512]{3,2,1,0:T(8,128)S(1)} %copy-done.1, f32[5,2,16,512]{3,2,1,0:T(8,128)S(1)} %collective-permute-done.5.major_lo, f32[5,2,16,512]{3,2,1,0:T(8,128)S(1)} %collective-permute-done.6.major_hi, f32[5,2,12,512]{3,2,1,0:T(8,128)S(1)} %collective-permute-done.7.sub_lo, ...), custom_call_target="tpu_custom_call" | custom-call | flops 29491200 | bytes 5898240 | tf_op jit(solution)/shard_map/flap_rate/pallas_call | solution.py:273
  (10 shorter events, 0.0 us)
Async XLA Ops:
  0.6 35.8 %copy-start.8 = (s32[16,12,512]{2,0,1:T(8,128)S(1)}, s32[16,12,512]{2,0,1:T(8,128)}, u32[]{:S(2)}) copy-start(s32[16,12,512]{2,0,1:T(8,128)} %param.13) | copy-start | bytes 1179652
  17.0 19.4 %all-to-all-start = ((f32[8,5,1024]{2,1,0:T(8,128)}), f32[8,5,1024]{2,1,0:T(8,128)S(1)}, u32[]{:S(2)}, u32[]{:S(2)}) async-start(f32[8,5,1024]{2,1,0:T(8,128)} %get-tuple-element.18), calls=%async_computation | async-start | bytes 524288 | tf_op jit(solution)/shard_map/all_to_all | solution.py:685
  22.9 33.6 %collective-permute-start.2 = (f32[5,2,16,256]{3,2,1,0:T(8,128)}, f32[5,2,16,256]{3,2,1,0:T(8,128)S(1)}, u32[]{:S(2)}, u32[]{:S(2)}) collective-permute-start(f32[5,2,16,256]{3,2,1,0:T(8,128)} %get-tuple-element.15.refs_1_), channel_id=1, source_target_pairs={{0,16},{16,32},{32,48},{48,64},{64,80},{80,96},{96,112},{112,0},{1... | collective-permute-start | bytes 491528 | tf_op jit(solution)/shard_map/ppermute | solution.py:669
  24.9 35.5 %collective-permute-start.3 = (f32[5,2,16,256]{3,2,1,0:T(8,128)}, f32[5,2,16,256]{3,2,1,0:T(8,128)S(1)}, u32[]{:S(2)}, u32[]{:S(2)}) collective-permute-start(f32[5,2,16,256]{3,2,1,0:T(8,128)} %get-tuple-element.16.refs_0_), channel_id=1, source_target_pairs={{16,0},{32,16},{48,32},{64,48},{80,64},{96,80},{112,96},{0,112},{1... | collective-permute-start | bytes 491528 | tf_op jit(solution)/shard_map/ppermute | solution.py:672
  27.1 29.1 %collective-permute-start.4 = (f32[5,32,32]{2,1,0:T(8,128)}, f32[5,32,32]{2,1,0:T(8,128)S(1)}, u32[]{:S(2)}, u32[]{:S(2)}) collective-permute-start(f32[5,32,32]{2,1,0:T(8,128)} %get-tuple-element.17.refs_2_), channel_id=1, source_target_pairs={{0,112},{16,96},{32,32},{48,48},{64,64},{80,80},{96,16},{112,0},{1... | collective-permute-start | bytes 61448 | tf_op jit(solution)/shard_map/ppermute | solution.py:677
  31.0 29.5 %collective-permute-start = (f32[5,2,32,256]{3,2,1,0:T(8,128)}, f32[5,2,32,256]{3,2,1,0:T(8,128)S(1)}, u32[]{:S(2)}, u32[]{:S(2)}) collective-permute-start(f32[5,2,32,256]{3,2,1,0:T(8,128)} %get-tuple-element.13), channel_id=1, source_target_pairs={{0,1},{1,2},{2,3},{3,4},{4,5},{5,6},{6,7},{7,8},{8,9},{9,10},{10,1... | collective-permute-start | bytes 983048 | tf_op jit(solution)/shard_map/ppermute | solution.py:669
  31.1 34.8 %collective-permute-start.1 = (f32[5,2,32,256]{3,2,1,0:T(8,128)}, f32[5,2,32,256]{3,2,1,0:T(8,128)S(1)}, u32[]{:S(2)}, u32[]{:S(2)}) collective-permute-start(f32[5,2,32,256]{3,2,1,0:T(8,128)} %get-tuple-element.14), channel_id=1, source_target_pairs={{1,0},{2,1},{3,2},{4,3},{5,4},{6,5},{7,6},{8,7},{9,8},{10,9},{11,1... | collective-permute-start | bytes 983048 | tf_op jit(solution)/shard_map/ppermute | solution.py:672
  36.4 29.5 %copy-start = (f32[5,16,32,256]{3,2,1,0:T(8,128)S(1)}, f32[5,16,32,256]{3,2,1,0:T(8,128)}, u32[]{:S(2)}) copy-start(f32[5,16,32,256]{3,2,1,0:T(8,128)} %q_hbm.3) | copy-start | bytes 7864324
  36.4 29.5 %copy-start.2 = (f32[3,16,32,256]{3,2,1,0:T(8,128)S(1)}, f32[3,16,32,256]{3,2,1,0:T(8,128)}, u32[]{:S(2)}) copy-start(f32[3,16,32,256]{3,2,1,0:T(8,128)} %refs_4_.1) | copy-start | bytes 4718596
  36.4 29.5 %copy-start.5 = (f32[5,2,16,256]{3,2,1,0:T(8,128)S(1)}, f32[5,2,16,256]{3,2,1,0:T(8,128)}, u32[]{:S(2)}) copy-start(f32[5,2,16,256]{3,2,1,0:T(8,128)} %get-tuple-element.16.refs_0_) | copy-start | bytes 491524
  36.4 29.5 %copy-start.6 = (f32[5,2,16,256]{3,2,1,0:T(8,128)S(1)}, f32[5,2,16,256]{3,2,1,0:T(8,128)}, u32[]{:S(2)}) copy-start(f32[5,2,16,256]{3,2,1,0:T(8,128)} %get-tuple-element.15.refs_1_) | copy-start | bytes 491524
  36.4 29.5 %copy-start.7 = (f32[5,32,32]{2,1,0:T(8,128)S(1)}, f32[5,32,32]{2,1,0:T(8,128)}, u32[]{:S(2)}) copy-start(f32[5,32,32]{2,1,0:T(8,128)} %get-tuple-element.17.refs_2_) | copy-start | bytes 61444
  56.2 21.4 %collective-permute-start.5 = (f32[5,2,16,512]{3,2,1,0:T(8,128)S(1)}, f32[5,2,16,512]{3,2,1,0:T(8,128)S(1)}, u32[]{:S(2)}, u32[]{:S(2)}) collective-permute-start(f32[5,2,16,512]{3,2,1,0:T(8,128)S(1)} %get-tuple-element.20), channel_id=1, source_target_pairs={{0,16},{16,32},{32,48},{48,64},{64,80},{80,96},{96,112},{112,0},{1... | collective-permute-start | bytes 983048 | tf_op jit(solution)/shard_map/ppermute | solution.py:669
  56.6 21.1 %collective-permute-start.6 = (f32[5,2,16,512]{3,2,1,0:T(8,128)S(1)}, f32[5,2,16,512]{3,2,1,0:T(8,128)S(1)}, u32[]{:S(2)}, u32[]{:S(2)}) collective-permute-start(f32[5,2,16,512]{3,2,1,0:T(8,128)S(1)} %get-tuple-element.21), channel_id=1, source_target_pairs={{16,0},{32,16},{48,32},{64,48},{80,64},{96,80},{112,96},{0,112},{1... | collective-permute-start | bytes 983048 | tf_op jit(solution)/shard_map/ppermute | solution.py:672
  60.4 17.2 %collective-permute-start.7 = (f32[5,2,12,512]{3,2,1,0:T(8,128)S(1)}, f32[5,2,12,512]{3,2,1,0:T(8,128)S(1)}, u32[]{:S(2)}, u32[]{:S(2)}) collective-permute-start(f32[5,2,12,512]{3,2,1,0:T(8,128)S(1)} %get-tuple-element.22), channel_id=1, source_target_pairs={{0,1},{1,2},{2,3},{3,4},{4,5},{5,6},{6,7},{7,8},{8,9},{9,10},{10,1... | collective-permute-start | bytes 737288 | tf_op jit(solution)/shard_map/ppermute | solution.py:669
  60.5 17.2 %copy-start.1 = (f32[5,12,16,512]{3,2,1,0:T(8,128)S(1)}, f32[5,12,16,512]{3,2,1,0:T(8,128)}, u32[]{:S(2)}) copy-start(f32[5,12,16,512]{3,2,1,0:T(8,128)} %get-tuple-element.19.q_hbm) | copy-start | bytes 5898244
  60.5 17.2 %copy-start.3 = (f32[3,16,12,512]{3,1,2,0:T(8,128)S(1)}, f32[3,16,12,512]{3,1,2,0:T(8,128)}, u32[]{:S(2)}) copy-start(f32[3,16,12,512]{3,1,2,0:T(8,128)} %param.11) | copy-start | bytes 3538948
  60.5 17.2 %copy-start.4 = (s32[16,12,512]{2,0,1:T(8,128)S(1)}, s32[16,12,512]{2,0,1:T(8,128)}, u32[]{:S(2)}) copy-start(s32[16,12,512]{2,0,1:T(8,128)} %param.12) | copy-start | bytes 1179652
  60.5 17.1 %collective-permute-start.8 = (f32[5,2,12,512]{3,2,1,0:T(8,128)S(1)}, f32[5,2,12,512]{3,2,1,0:T(8,128)S(1)}, u32[]{:S(2)}, u32[]{:S(2)}) collective-permute-start(f32[5,2,12,512]{3,2,1,0:T(8,128)S(1)} %get-tuple-element.23), channel_id=1, source_target_pairs={{1,0},{2,1},{3,2},{4,3},{5,4},{6,5},{7,6},{8,7},{9,8},{10,9},{11,1... | collective-permute-start | bytes 737288 | tf_op jit(solution)/shard_map/ppermute | solution.py:672

commit v7 on v6

--- a/solution.py
+++ b/solution.py
@@ -484,22 +484,25 @@
                 new[c] = ws * total if new[c] is None else new[c] + ws * total
         return tuple(new)
 
+    def lowest_of(i):
+        return jnp.minimum(first[i, 0], spans - 3)
+
     def step(g, _):
         for n in range(GROUP):
             i = g * GROUP + n
-            for c, x in enumerate(add_planes(first[i, 0], 2, tile_of(i), (None,) * 5)):
+            for c, x in enumerate(add_planes(lowest_of(i), 3, tile_of(i), (None,) * 5)):
                 partial[n, c] = x
         for n in range(GROUP):
             i = g * GROUP + n
-            lowest = first[i, 0]
-            more = first[i, tile - 1] - lowest
+            lowest = lowest_of(i)
+            more = first[i, tile - 1] - 1 - lowest
 
             @pl.when(more > 0)
             def _():
                 made = tile_of(i)
 
                 def again(m, _):
-                    sums = add_planes(lowest + 2 + m, 1, made, tuple(partial[n, c] for c in range(5)))
+                    sums = add_planes(lowest + 3 + m, 1, made, tuple(partial[n, c] for c in range(5)))
                     for c in range(5):
                         partial[n, c] = sums[c]
                     return 0
@@ -650,7 +653,7 @@
             pltpu.VMEM(state.shape, f32),
             pltpu.SemaphoreType.DMA((planes,)),
         ],
-        compiler_params=params(52 * 1024 * 1024),
+        compiler_params=params(40 * 1024 * 1024),
         cost_estimate=pl.CostEstimate(flops=24 * 10**9, bytes_accessed=6 * 10**6, transcendentals=0),
         name="fill",
     )(source, mask, state, slot)

time: 86.6 us -> 83.5 us (0.964)
  Pallas kernels: 56.4 us -> 51.9 us
  local copies, waits for them, and re-layouts: 0.04 us -> 1.57 us
    pallas_call x1, Pallas kernels: 19.8 us -> 17.4 us  [fill(): pl.pallas_call(fill_kernel, grid=(planes,), in_specs=[plane, plane, IN_HB...]
    pallas_call x1, Pallas kernels: 16.4 us -> 14.1 us  [donors(): pl.pallas_call(donor_kernel, grid=(1,), in_specs=[IN_VMEM, IN_VMEM, IN_HB...]
    unnamed x18, local copies, waits for them, and re-layouts: 0.04 us -> 1.57 us
  transfers between devices with their start and end apart: 10 -> 10, of which waited for: 0 -> 0; matrix products, arithmetic and copies ran while one was open for 0% -> 0% of each run, Pallas kernels for 36% -> 35%
where the time goes in v7:
time: 83.5 us; the launch traced here: 83.2 us
  Pallas kernels  51.9 us (62%)
  starting transfers between devices  28.9 us (35%)
  local copies, waits for them, and re-layouts  1.57 us (2%)
    pallas_call x2, Pallas kernels, rate(): pl.pallas_call(functools.partial(rate_kernel, cgrid=cgrid, step_planes=st...  20.3 us
    pallas_call x1, Pallas kernels, fill(): pl.pallas_call(fill_kernel, grid=(planes,), in_specs=[plane, plane, IN_HB...  17.4 us
    ppermute x4, starting transfers between devices, back(): return lax.ppermute(value, axis, [(j, i) for i, j in ring(axis)])  16.7 us
    pallas_call x1, Pallas kernels, donors(): pl.pallas_call(donor_kernel, grid=(1,), in_specs=[IN_VMEM, IN_VMEM, IN_HB...  14.1 us
    all_to_all x1, starting transfers between devices, body(): slot = lax.all_to_all(slot, 'wrap', split_axis=0, concat_axis=0, tiled=True)  5.92 us
    ppermute x1, starting transfers between devices, body(): lax.ppermute(wall, 'wrap', [(i, wrap_count - 1 - i if wrapped(i, wrap_cou...  3.89 us
    ppermute x4, starting transfers between devices, onward(): return lax.ppermute(value, axis, ring(axis))  2.42 us
  transfers between devices with their start and end apart: 10, of which 0 were waited for; matrix products, arithmetic and copies ran while one was open for 0% of the time, Pallas kernels for 35%

profile of v7, /device:TPU:0, one launch (start us, length us, event | category | flops | bytes accessed | tf_op | source)
XLA Modules:
  0.0 83.2 jit_solution(5222001127203679971)
XLA Ops:
  0.6 0.0 copy-start.3
  0.7 14.1 %donors.1 = (f32[8,5,1024]{2,1,0:T(8,128)}, f32[5,2,16,256]{3,2,1,0:T(8,128)}, f32[5,2,16,256]{3,2,1,0:T(8,128)}, f32[5,2,32,256]{3,2,1,0:T(8,128)}, f32[5,2,32,256]{3,2,1,0:T(8,128)}, /*index=5*/f32[5,32,32]{2,1,0:T(8,128)}) custom-call(s32[8,1024]{1,0:T(8,128)} %bitcast.16, f32[3,8,1024]{2,1,0:T(8,128)} %bitcast.15, f32[5,16,32,256]{3,2,1,0:T(8,128)} %q_hbm.3), custom_call_target="tpu_custom_call" | custom-call | tf_op jit(solution)/shard_map/donors/pallas_call | solution.py:538
  14.8 5.9 %all-to-all-start = ((f32[8,5,1024]{2,1,0:T(8,128)}), f32[8,5,1024]{2,1,0:T(8,128)S(1)}, u32[]{:S(2)}, u32[]{:S(2)}) async-start(f32[8,5,1024]{2,1,0:T(8,128)} %get-tuple-element.18), calls=%async_computation | async-start | bytes 524288 | tf_op jit(solution)/shard_map/all_to_all | solution.py:688
  20.7 2.0 %collective-permute-start.2 = (f32[5,2,16,256]{3,2,1,0:T(8,128)}, f32[5,2,16,256]{3,2,1,0:T(8,128)S(1)}, u32[]{:S(2)}, u32[]{:S(2)}) collective-permute-start(f32[5,2,16,256]{3,2,1,0:T(8,128)} %get-tuple-element.15.refs_1_), channel_id=1, source_target_pairs={{0,16},{16,32},{32,48},{48,64},{64,80},{80,96},{96,112},{112,0},{1... | collective-permute-start | bytes 491528 | tf_op jit(solution)/shard_map/ppermute | solution.py:672
  22.7 2.1 %collective-permute-start.3 = (f32[5,2,16,256]{3,2,1,0:T(8,128)}, f32[5,2,16,256]{3,2,1,0:T(8,128)S(1)}, u32[]{:S(2)}, u32[]{:S(2)}) collective-permute-start(f32[5,2,16,256]{3,2,1,0:T(8,128)} %get-tuple-element.16.refs_0_), channel_id=1, source_target_pairs={{16,0},{32,16},{48,32},{64,48},{80,64},{96,80},{112,96},{0,112},{1... | collective-permute-start | bytes 491528 | tf_op jit(solution)/shard_map/ppermute | solution.py:675
  24.9 3.9 %collective-permute-start.4 = (f32[5,32,32]{2,1,0:T(8,128)}, f32[5,32,32]{2,1,0:T(8,128)S(1)}, u32[]{:S(2)}, u32[]{:S(2)}) collective-permute-start(f32[5,32,32]{2,1,0:T(8,128)} %get-tuple-element.17.refs_2_), channel_id=1, source_target_pairs={{0,112},{16,96},{32,32},{48,48},{64,64},{80,80},{96,16},{112,0},{1... | collective-permute-start | bytes 61448 | tf_op jit(solution)/shard_map/ppermute | solution.py:680
  28.8 0.1 collective-permute-start
  28.9 5.3 %collective-permute-start.1 = (f32[5,2,32,256]{3,2,1,0:T(8,128)}, f32[5,2,32,256]{3,2,1,0:T(8,128)S(1)}, u32[]{:S(2)}, u32[]{:S(2)}) collective-permute-start(f32[5,2,32,256]{3,2,1,0:T(8,128)} %get-tuple-element.14), channel_id=1, source_target_pairs={{1,0},{2,1},{3,2},{4,3},{5,4},{6,5},{7,6},{8,7},{9,8},{10,9},{11,1... | collective-permute-start | bytes 983048 | tf_op jit(solution)/shard_map/ppermute | solution.py:675
  34.2 0.0 all-to-all-done.slot_ref
  34.2 0.0 copy-done.8
  34.2 0.0 copy-start.7
  34.2 1.5 %copy-done.7 = f32[5,16,12,512]{3,1,2,0:T(8,128)S(1)} copy-done((f32[5,16,12,512]{3,1,2,0:T(8,128)S(1)}, f32[5,16,12,512]{3,1,2,0:T(8,128)}, u32[]{:S(2)}) %copy-start.7) | copy-done | bytes 1966104
  35.8 17.4 %fill.1 = (f32[5,12,16,512]{3,2,1,0:T(8,128)S(1)}, f32[5,2,16,512]{3,2,1,0:T(8,128)S(1)}, f32[5,2,16,512]{3,2,1,0:T(8,128)S(1)}, f32[5,2,12,512]{3,2,1,0:T(8,128)S(1)}, f32[5,2,12,512]{3,2,1,0:T(8,128)S(1)}) custom-call(s32[12,16,512]{2,1,0:T(8,128)S(1)} %bitcast.13, s32[12,16,512]{2,1,0:T(8,128)S(1)} %bitcast.10, f32[5,12,16,512]{3,2,1,0:T(8,128)S(1)} %bitcast.12, ...), custom_call_target="tpu_custom_call" | custom-call | flops 24000000000 | bytes 6000000 | tf_op jit(solution)/shard_map/fill/pallas_call | solution.py:644
  53.2 0.0 collective-permute-done.4.refs_3_
  53.2 0.3 collective-permute-start.5
  53.5 0.0 collective-permute-done.2.sub_lo
  53.5 3.9 %collective-permute-start.6 = (f32[5,2,16,512]{3,2,1,0:T(8,128)S(1)}, f32[5,2,16,512]{3,2,1,0:T(8,128)S(1)}, u32[]{:S(2)}, u32[]{:S(2)}) collective-permute-start(f32[5,2,16,512]{3,2,1,0:T(8,128)S(1)} %get-tuple-element.21), channel_id=1, source_target_pairs={{16,0},{32,16},{48,32},{64,48},{80,64},{96,80},{112,96},{0,112},{1... | collective-permute-start | bytes 983048 | tf_op jit(solution)/shard_map/ppermute | solution.py:675
  57.4 0.0 collective-permute-done.3.sub_hi
  57.4 0.0 collective-permute-start.7
  57.4 0.0 collective-permute-done.major_lo
  57.4 0.0 copy-start.2
  57.4 5.3 %collective-permute-start.8 = (f32[5,2,12,512]{3,2,1,0:T(8,128)S(1)}, f32[5,2,12,512]{3,2,1,0:T(8,128)S(1)}, u32[]{:S(2)}, u32[]{:S(2)}) collective-permute-start(f32[5,2,12,512]{3,2,1,0:T(8,128)S(1)} %get-tuple-element.23), channel_id=1, source_target_pairs={{1,0},{2,1},{3,2},{4,3},{5,4},{6,5},{7,6},{8,7},{9,8},{10,9},{11,1... | collective-permute-start | bytes 737288 | tf_op jit(solution)/shard_map/ppermute | solution.py:675
  62.8 0.0 collective-permute-done.1.major_hi
  62.8 0.0 copy-done.4
  62.8 0.0 copy-done.5
  62.8 0.0 copy-done.6
  62.8 11.7 %cgrid_rate.1 = f32[5,16,32,256]{3,2,1,0:T(8,128)} custom-call(f32[5,16,32,256]{3,2,1,0:T(8,128)S(1)} %copy-done, f32[5,2,32,256]{3,2,1,0:T(8,128)S(1)} %collective-permute-done.major_lo, f32[5,2,32,256]{3,2,1,0:T(8,128)S(1)} %collective-permute-done.1.major_hi, f32[5,2,16,256]{3,2,1,0:T(8,128)S(1)} %collective-permute-done.2.sub_lo, ...), custom_call_target="tpu_custom_call" | custom-call | flops 39321600 | bytes 7864320 | tf_op jit(solution)/shard_map/cgrid_rate/pallas_call | solution.py:273
  74.5 0.0 collective-permute-done.7.sub_lo
  74.5 0.0 collective-permute-done.8.sub_hi
  74.5 0.0 collective-permute-done.5.major_lo
  74.5 0.0 collective-permute-done.6.major_hi
  74.6 8.7 %flap_rate.1 = f32[5,12,16,512]{3,2,1,0:T(8,128)} custom-call(f32[5,12,16,512]{3,2,1,0:T(8,128)S(1)} %get-tuple-element.19.q_hbm, f32[5,2,16,512]{3,2,1,0:T(8,128)S(1)} %collective-permute-done.5.major_lo, f32[5,2,16,512]{3,2,1,0:T(8,128)S(1)} %collective-permute-done.6.major_hi, f32[5,2,12,512]{3,2,1,0:T(8,128)S(1)} %collective-permute-done.7.sub_lo, ...), custom_call_target="tpu_custom_call" | custom-call | flops 29491200 | bytes 5898240 | tf_op jit(solution)/shard_map/flap_rate/pallas_call | solution.py:273
  (10 shorter events, 0.0 us)
Async XLA Ops:
  0.6 33.6 %copy-start.3 = (s32[16,12,512]{2,0,1:T(8,128)S(1)}, s32[16,12,512]{2,0,1:T(8,128)}, u32[]{:S(2)}) copy-start(s32[16,12,512]{2,0,1:T(8,128)} %param.12) | copy-start | bytes 1179652
  0.6 33.6 %copy-start.8 = (s32[16,12,512]{2,0,1:T(8,128)S(1)}, s32[16,12,512]{2,0,1:T(8,128)}, u32[]{:S(2)}) copy-start(s32[16,12,512]{2,0,1:T(8,128)} %param.13) | copy-start | bytes 1179652
  14.8 19.4 %all-to-all-start = ((f32[8,5,1024]{2,1,0:T(8,128)}), f32[8,5,1024]{2,1,0:T(8,128)S(1)}, u32[]{:S(2)}, u32[]{:S(2)}) async-start(f32[8,5,1024]{2,1,0:T(8,128)} %get-tuple-element.18), calls=%async_computation | async-start | bytes 524288 | tf_op jit(solution)/shard_map/all_to_all | solution.py:688
  20.7 32.8 %collective-permute-start.2 = (f32[5,2,16,256]{3,2,1,0:T(8,128)}, f32[5,2,16,256]{3,2,1,0:T(8,128)S(1)}, u32[]{:S(2)}, u32[]{:S(2)}) collective-permute-start(f32[5,2,16,256]{3,2,1,0:T(8,128)} %get-tuple-element.15.refs_1_), channel_id=1, source_target_pairs={{0,16},{16,32},{32,48},{48,64},{64,80},{80,96},{96,112},{112,0},{1... | collective-permute-start | bytes 491528 | tf_op jit(solution)/shard_map/ppermute | solution.py:672
  22.7 34.7 %collective-permute-start.3 = (f32[5,2,16,256]{3,2,1,0:T(8,128)}, f32[5,2,16,256]{3,2,1,0:T(8,128)S(1)}, u32[]{:S(2)}, u32[]{:S(2)}) collective-permute-start(f32[5,2,16,256]{3,2,1,0:T(8,128)} %get-tuple-element.16.refs_0_), channel_id=1, source_target_pairs={{16,0},{32,16},{48,32},{64,48},{80,64},{96,80},{112,96},{0,112},{1... | collective-permute-start | bytes 491528 | tf_op jit(solution)/shard_map/ppermute | solution.py:675
  24.9 28.3 %collective-permute-start.4 = (f32[5,32,32]{2,1,0:T(8,128)}, f32[5,32,32]{2,1,0:T(8,128)S(1)}, u32[]{:S(2)}, u32[]{:S(2)}) collective-permute-start(f32[5,32,32]{2,1,0:T(8,128)} %get-tuple-element.17.refs_2_), channel_id=1, source_target_pairs={{0,112},{16,96},{32,32},{48,48},{64,64},{80,80},{96,16},{112,0},{1... | collective-permute-start | bytes 61448 | tf_op jit(solution)/shard_map/ppermute | solution.py:680
  28.8 28.6 %collective-permute-start = (f32[5,2,32,256]{3,2,1,0:T(8,128)}, f32[5,2,32,256]{3,2,1,0:T(8,128)S(1)}, u32[]{:S(2)}, u32[]{:S(2)}) collective-permute-start(f32[5,2,32,256]{3,2,1,0:T(8,128)} %get-tuple-element.13), channel_id=1, source_target_pairs={{0,1},{1,2},{2,3},{3,4},{4,5},{5,6},{6,7},{7,8},{8,9},{9,10},{10,1... | collective-permute-start | bytes 983048 | tf_op jit(solution)/shard_map/ppermute | solution.py:672
  28.9 33.9 %collective-permute-start.1 = (f32[5,2,32,256]{3,2,1,0:T(8,128)}, f32[5,2,32,256]{3,2,1,0:T(8,128)S(1)}, u32[]{:S(2)}, u32[]{:S(2)}) collective-permute-start(f32[5,2,32,256]{3,2,1,0:T(8,128)} %get-tuple-element.14), channel_id=1, source_target_pairs={{1,0},{2,1},{3,2},{4,3},{5,4},{6,5},{7,6},{8,7},{9,8},{10,9},{11,1... | collective-permute-start | bytes 983048 | tf_op jit(solution)/shard_map/ppermute | solution.py:675
  34.2 1.5 %copy-start.7 = (f32[5,16,12,512]{3,1,2,0:T(8,128)S(1)}, f32[5,16,12,512]{3,1,2,0:T(8,128)}, u32[]{:S(2)}) copy-start(f32[5,16,12,512]{3,1,2,0:T(8,128)} %param.10) | copy-start | bytes 5898244
  35.8 27.0 %copy-start = (f32[5,16,32,256]{3,2,1,0:T(8,128)S(1)}, f32[5,16,32,256]{3,2,1,0:T(8,128)}, u32[]{:S(2)}) copy-start(f32[5,16,32,256]{3,2,1,0:T(8,128)} %q_hbm.3) | copy-start | bytes 7864324
  35.8 27.0 %copy-start.1 = (f32[3,16,32,256]{3,2,1,0:T(8,128)S(1)}, f32[3,16,32,256]{3,2,1,0:T(8,128)}, u32[]{:S(2)}) copy-start(f32[3,16,32,256]{3,2,1,0:T(8,128)} %refs_4_.1) | copy-start | bytes 4718596
  35.8 27.0 %copy-start.4 = (f32[5,2,16,256]{3,2,1,0:T(8,128)S(1)}, f32[5,2,16,256]{3,2,1,0:T(8,128)}, u32[]{:S(2)}) copy-start(f32[5,2,16,256]{3,2,1,0:T(8,128)} %get-tuple-element.16.refs_0_) | copy-start | bytes 491524
  35.8 27.0 %copy-start.5 = (f32[5,2,16,256]{3,2,1,0:T(8,128)S(1)}, f32[5,2,16,256]{3,2,1,0:T(8,128)}, u32[]{:S(2)}) copy-start(f32[5,2,16,256]{3,2,1,0:T(8,128)} %get-tuple-element.15.refs_1_) | copy-start | bytes 491524
  35.8 27.0 %copy-start.6 = (f32[5,32,32]{2,1,0:T(8,128)S(1)}, f32[5,32,32]{2,1,0:T(8,128)}, u32[]{:S(2)}) copy-start(f32[5,32,32]{2,1,0:T(8,128)} %get-tuple-element.17.refs_2_) | copy-start | bytes 61444
  53.2 21.3 %collective-permute-start.5 = (f32[5,2,16,512]{3,2,1,0:T(8,128)S(1)}, f32[5,2,16,512]{3,2,1,0:T(8,128)S(1)}, u32[]{:S(2)}, u32[]{:S(2)}) collective-permute-start(f32[5,2,16,512]{3,2,1,0:T(8,128)S(1)} %get-tuple-element.20), channel_id=1, source_target_pairs={{0,16},{16,32},{32,48},{48,64},{64,80},{80,96},{96,112},{112,0},{1... | collective-permute-start | bytes 983048 | tf_op jit(solution)/shard_map/ppermute | solution.py:672
  53.5 21.0 %collective-permute-start.6 = (f32[5,2,16,512]{3,2,1,0:T(8,128)S(1)}, f32[5,2,16,512]{3,2,1,0:T(8,128)S(1)}, u32[]{:S(2)}, u32[]{:S(2)}) collective-permute-start(f32[5,2,16,512]{3,2,1,0:T(8,128)S(1)} %get-tuple-element.21), channel_id=1, source_target_pairs={{16,0},{32,16},{48,32},{64,48},{80,64},{96,80},{112,96},{0,112},{1... | collective-permute-start | bytes 983048 | tf_op jit(solution)/shard_map/ppermute | solution.py:675
  57.4 17.1 %collective-permute-start.7 = (f32[5,2,12,512]{3,2,1,0:T(8,128)S(1)}, f32[5,2,12,512]{3,2,1,0:T(8,128)S(1)}, u32[]{:S(2)}, u32[]{:S(2)}) collective-permute-start(f32[5,2,12,512]{3,2,1,0:T(8,128)S(1)} %get-tuple-element.22), channel_id=1, source_target_pairs={{0,1},{1,2},{2,3},{3,4},{4,5},{5,6},{6,7},{7,8},{8,9},{9,10},{10,1... | collective-permute-start | bytes 737288 | tf_op jit(solution)/shard_map/ppermute | solution.py:672
  57.4 17.1 %copy-start.2 = (f32[3,16,12,512]{3,1,2,0:T(8,128)S(1)}, f32[3,16,12,512]{3,1,2,0:T(8,128)}, u32[]{:S(2)}) copy-start(f32[3,16,12,512]{3,1,2,0:T(8,128)} %param.11) | copy-start | bytes 3538948
  57.4 17.1 %collective-permute-start.8 = (f32[5,2,12,512]{3,2,1,0:T(8,128)S(1)}, f32[5,2,12,512]{3,2,1,0:T(8,128)S(1)}, u32[]{:S(2)}, u32[]{:S(2)}) collective-permute-start(f32[5,2,12,512]{3,2,1,0:T(8,128)S(1)} %get-tuple-element.23), channel_id=1, source_target_pairs={{1,0},{2,1},{3,2},{4,3},{5,4},{6,5},{7,6},{8,7},{9,8},{10,9},{11,1... | collective-permute-start | bytes 737288 | tf_op jit(solution)/shard_map/ppermute | solution.py:675

commit v8 on v7

--- a/solution.py
+++ b/solution.py
@@ -79,7 +79,7 @@
     metric_rows,
 ):
     if cgrid:
-        own_lo, own_hi, wall_own, wall_far, metric_ref, out_ref, qe, prim, sub_edge, lane_edge, sems = refs
+        own_lo, own_hi, wall_own, wall_far, metric_ref, out_ref, qe, prim, sub_edge, lane_edge, mix, sems = refs
     else:
         own_lo = own_hi = None
         mask_ref, metric_ref, out_ref, qe, prim, sub_edge, sems = refs
@@ -147,8 +147,28 @@
                     parts.append(jnp.where(in_wake, far, sign * own))
                 ghosts.append(jnp.concatenate(parts, axis=0))
             second = [pltpu.roll(x, 127, 1) for x in ghosts]
-            for i, x in enumerate(edge_fields(ghosts, second, lane_m, -1)):
-                lane_edge[i] = x
+            fields = edge_fields(ghosts, second, lane_m, -1)
+            even = lax.broadcasted_iota(i32, (rows, 128), 1) % 2 == 0
+            for c in range(5):
+                lane_edge[c] = jnp.where(even, fields[c], -pltpu.roll(ghosts[c], 1, 1))
+            for i in range(4):
+                lane_edge[5 + i] = jnp.where(even, fields[10 + i], 0.0)
+
+            source = lax.broadcasted_iota(i32, (lanes, lanes), 0)
+            target = lax.broadcasted_iota(i32, (lanes, lanes), 1)
+
+            def band(*pairs):
+                total = jnp.zeros((lanes, lanes), f32)
+                for distance, factor in pairs:
+                    hit = source == jnp.minimum(target + distance, lanes - 1)
+                    total += jnp.where(hit, factor, 0.0)
+                return total.astype(bf16)
+
+            bands = [band((1, -1.0), (-1, 1.0))] * 2
+            bands += [band((1, 4.0), (-1, 4.0), (2, -1.0), (-2, -1.0))] * 2
+            bands += [band((1, 1.0), (-1, 1.0))] * 2
+            for i, x in enumerate(bands):
+                mix[i * lanes : (i + 1) * lanes, :] = x
         copies[0].wait()
         part(0).wait()
         part(1).wait()
@@ -203,17 +223,14 @@
 
         def lane_next(x):
             moved = [pltpu.roll(x[:, t : t + 128], 127, 1) for t in range(0, lanes, 128)]
-            moved.append(x[:, lanes - 128 :] if cgrid else moved[0])
+            moved.append(moved[0])
             return jnp.concatenate(
                 [jnp.where(lane_last, moved[t + 1], moved[t]) for t in range(lanes // 128)], axis=1
             )
 
-        def lane_prior(x, i):
+        def lane_prior(x):
             moved = [pltpu.roll(x[:, t : t + 128], 1, 1) for t in range(0, lanes, 128)]
-            if cgrid:
-                moved.insert(0, pltpu.roll(lane_edge[i], lax.rem(128 - 2 * k, 128), 1))
-            else:
-                moved.insert(0, moved[-1])
+            moved.insert(0, moved[-1])
             return jnp.concatenate(
                 [jnp.where(lane_first, moved[t], moved[t + 1]) for t in range(lanes // 128)], axis=1
             )
@@ -226,16 +243,33 @@
         all2 = 2.0 * (gm2 + gs2 + gl2)
         all6 = 6.0 * (gm + gs + gl)
         mine = [prim[here, i] for i in range(5)]
+        q = [qe[c, k + 2] for c in range(5)]
+        lane_flux = flux(q, mine, lane_m)
+
+        def lane_mixed(groups, mixer, edge):
+            parts = [[part for x in group for part in split_two(x)] for group in groups]
+            mixed = jnp.concatenate([jnp.concatenate(row, axis=1) for row in parts], axis=0)
+            mixed = jnp.dot(mixed, mixer, preferred_element_type=f32)
+            results = []
+            for i in range(len(groups)):
+                x = mixed[i * rows : (i + 1) * rows]
+                ghost = pltpu.roll(lane_edge[edge + i], lax.rem(128 - 2 * k, 128), 1)
+                results.append(
+                    jnp.concatenate([x[:, 0:128] + jnp.where(lane_at < 2, ghost, 0.0), x[:, 128:]], axis=1)
+                )
+            return results
+
+        if cgrid:
+            lane_damped = lane_mixed([(lane_flux[c], q[c]) for c in range(5)], mix[0 : 4 * lanes, :], 0)
+            lane_curved = lane_mixed([(mine[i],) for i in (0, 1, 2, 4)], mix[4 * lanes :, :], 5)
         viscous = {}
         for i, c, e in ((0, 1, 10), (1, 2, 11), (2, 3, 12), (4, 4, 13)):
             x = mine[i]
             total = gm2 * (prim[above, i] + prim[below, i])
             total += gs2 * (sub_next(x, e) + sub_prior(x, e))
-            total += gl2 * (lane_next(x) + lane_prior(x, e))
+            total += gl2 * (lane_curved[c - 1] if cgrid else lane_next(x) + lane_prior(x))
             viscous[c] = total - all2 * x
-        q = [qe[c, k + 2] for c in range(5)]
         sub_flux = flux(q, mine, sub_m)
-        lane_flux = flux(q, mine, lane_m)
         for c in range(5):
             x = q[c]
             four = 4.0 * x
@@ -247,9 +281,12 @@
             up = four - sub_flux[c] - sub_next(x, 5 + c)
             down = four + sub_flux[c] - sub_prior(x, 5 + c)
             total += gs * (sub_next(up, c) + sub_prior(down, c))
-            up = four - lane_flux[c] - lane_next(x)
-            down = four + lane_flux[c] - lane_prior(x, 5 + c)
-            total += gl * (lane_next(up) + lane_prior(down, c))
+            if cgrid:
+                total += gl * lane_damped[c]
+            else:
+                up = four - lane_flux[c] - lane_next(x)
+                down = four + lane_flux[c] - lane_prior(x)
+                total += gl * (lane_next(up) + lane_prior(down))
             total -= all6 * x
             if c:
                 total += viscous[c]
@@ -287,7 +324,7 @@
             pltpu.VMEM((3, 10, rows, lanes), f32),
             pltpu.VMEM((2, 14, planes, lanes), f32),
         ]
-        + [pltpu.VMEM((14, rows, 128), f32)] * cgrid
+        + [pltpu.VMEM((9, rows, 128), f32), pltpu.VMEM((6 * lanes, lanes), bf16)] * cgrid
         + [pltpu.SemaphoreType.DMA((planes // step_planes + 2,))],
         compiler_params=params(),
         cost_estimate=pl.CostEstimate(
@@ -653,7 +690,7 @@
             pltpu.VMEM(state.shape, f32),
             pltpu.SemaphoreType.DMA((planes,)),
         ],
-        compiler_params=params(40 * 1024 * 1024),
+        compiler_params=params(49 * 1024 * 1024),
         cost_estimate=pl.CostEstimate(flops=24 * 10**9, bytes_accessed=6 * 10**6, transcendentals=0),
         name="fill",
     )(source, mask, state, slot)

time: 83.5 us -> 79.8 us (0.956)
  Pallas kernels: 51.9 us -> 49.7 us
  local copies, waits for them, and re-layouts: 1.57 us -> 0.04 us
    pallas_call x2, Pallas kernels: 20.3 us -> 17.7 us  [rate(): pl.pallas_call(functools.partial(rate_kernel, cgrid=cgrid, step_planes=st...]
    unnamed x18 -> x16, local copies, waits for them, and re-layouts: 1.57 us -> 0.04 us
  transfers between devices with their start and end apart: 10 -> 10, of which waited for: 0 -> 0; matrix products, arithmetic and copies ran while one was open for 0% -> 0% of each run, Pallas kernels for 35% -> 34%
where the time goes in v8:
time: 79.8 us; the launch traced here: 79.5 us
  Pallas kernels  49.7 us (62%)
  starting transfers between devices  28.9 us (36%)
  between operations  0.82 us (1%)
    pallas_call x1, Pallas kernels, fill(): pl.pallas_call(fill_kernel, grid=(planes,), in_specs=[plane, plane, IN_HB...  17.9 us
    pallas_call x2, Pallas kernels, rate(): pl.pallas_call(functools.partial(rate_kernel, cgrid=cgrid, step_planes=st...  17.7 us
    ppermute x4, starting transfers between devices, back(): return lax.ppermute(value, axis, [(j, i) for i, j in ring(axis)])  16.7 us
    pallas_call x1, Pallas kernels, donors(): pl.pallas_call(donor_kernel, grid=(1,), in_specs=[IN_VMEM, IN_VMEM, IN_HB...  14.2 us
    all_to_all x1, starting transfers between devices, body(): slot = lax.all_to_all(slot, 'wrap', split_axis=0, concat_axis=0, tiled=True)  5.92 us
    ppermute x1, starting transfers between devices, body(): lax.ppermute(wall, 'wrap', [(i, wrap_count - 1 - i if wrapped(i, wrap_cou...  3.89 us
    ppermute x4, starting transfers between devices, onward(): return lax.ppermute(value, axis, ring(axis))  2.42 us
  transfers between devices with their start and end apart: 10, of which 0 were waited for; matrix products, arithmetic and copies ran while one was open for 0% of the time, Pallas kernels for 34%

profile of v8, /device:TPU:0, one launch (start us, length us, event | category | flops | bytes accessed | tf_op | source)
XLA Modules:
  0.0 79.5 jit_solution(18440342517052464951)
XLA Ops:
  0.6 0.0 copy-start.3
  0.6 0.0 copy-start.7
  0.7 14.2 %donors.1 = (f32[8,5,1024]{2,1,0:T(8,128)}, f32[5,2,16,256]{3,2,1,0:T(8,128)}, f32[5,2,16,256]{3,2,1,0:T(8,128)}, f32[5,2,32,256]{3,2,1,0:T(8,128)}, f32[5,2,32,256]{3,2,1,0:T(8,128)}, /*index=5*/f32[5,32,32]{2,1,0:T(8,128)}) custom-call(s32[8,1024]{1,0:T(8,128)} %bitcast.15, f32[3,8,1024]{2,1,0:T(8,128)} %bitcast.14, f32[5,16,32,256]{3,2,1,0:T(8,128)} %q_hbm.3), custom_call_target="tpu_custom_call" | custom-call | tf_op jit(solution)/shard_map/donors/pallas_call | solution.py:575
  14.8 5.9 %all-to-all-start = ((f32[8,5,1024]{2,1,0:T(8,128)}), f32[8,5,1024]{2,1,0:T(8,128)S(1)}, u32[]{:S(2)}, u32[]{:S(2)}) async-start(f32[8,5,1024]{2,1,0:T(8,128)} %get-tuple-element.18), calls=%async_computation | async-start | bytes 524288 | tf_op jit(solution)/shard_map/all_to_all | solution.py:725
  20.7 2.0 %collective-permute-start.2 = (f32[5,2,16,256]{3,2,1,0:T(8,128)}, f32[5,2,16,256]{3,2,1,0:T(8,128)S(1)}, u32[]{:S(2)}, u32[]{:S(2)}) collective-permute-start(f32[5,2,16,256]{3,2,1,0:T(8,128)} %get-tuple-element.15.refs_1_), channel_id=1, source_target_pairs={{0,16},{16,32},{32,48},{48,64},{64,80},{80,96},{96,112},{112,0},{1... | collective-permute-start | bytes 491528 | tf_op jit(solution)/shard_map/ppermute | solution.py:709
  22.8 2.1 %collective-permute-start.3 = (f32[5,2,16,256]{3,2,1,0:T(8,128)}, f32[5,2,16,256]{3,2,1,0:T(8,128)S(1)}, u32[]{:S(2)}, u32[]{:S(2)}) collective-permute-start(f32[5,2,16,256]{3,2,1,0:T(8,128)} %get-tuple-element.16.refs_0_), channel_id=1, source_target_pairs={{16,0},{32,16},{48,32},{64,48},{80,64},{96,80},{112,96},{0,112},{1... | collective-permute-start | bytes 491528 | tf_op jit(solution)/shard_map/ppermute | solution.py:712
  24.9 3.9 %collective-permute-start.4 = (f32[5,32,32]{2,1,0:T(8,128)}, f32[5,32,32]{2,1,0:T(8,128)S(1)}, u32[]{:S(2)}, u32[]{:S(2)}) collective-permute-start(f32[5,32,32]{2,1,0:T(8,128)} %get-tuple-element.17.refs_2_), channel_id=1, source_target_pairs={{0,112},{16,96},{32,32},{48,48},{64,64},{80,80},{96,16},{112,0},{1... | collective-permute-start | bytes 61448 | tf_op jit(solution)/shard_map/ppermute | solution.py:717
  28.8 0.1 collective-permute-start
  28.9 5.3 %collective-permute-start.1 = (f32[5,2,32,256]{3,2,1,0:T(8,128)}, f32[5,2,32,256]{3,2,1,0:T(8,128)S(1)}, u32[]{:S(2)}, u32[]{:S(2)}) collective-permute-start(f32[5,2,32,256]{3,2,1,0:T(8,128)} %get-tuple-element.14), channel_id=1, source_target_pairs={{1,0},{2,1},{3,2},{4,3},{5,4},{6,5},{7,6},{8,7},{9,8},{10,9},{11,1... | collective-permute-start | bytes 983048 | tf_op jit(solution)/shard_map/ppermute | solution.py:712
  34.2 0.0 all-to-all-done.slot_ref
  34.2 0.0 copy-done.3
  34.2 0.0 copy-done.7
  34.2 0.0 copy-start
  34.2 0.0 copy-start.1
  34.3 17.9 %fill.1 = (f32[5,12,16,512]{3,2,1,0:T(8,128)S(1)}, f32[5,2,16,512]{3,2,1,0:T(8,128)S(1)}, f32[5,2,16,512]{3,2,1,0:T(8,128)S(1)}, f32[5,2,12,512]{3,2,1,0:T(8,128)S(1)}, f32[5,2,12,512]{3,2,1,0:T(8,128)S(1)}) custom-call(s32[12,16,512]{2,1,0:T(8,128)S(1)} %bitcast.12, s32[12,16,512]{2,1,0:T(8,128)S(1)} %bitcast.10, f32[5,12,16,512]{3,2,1,0:T(8,128)} %bitcast.16, ...), custom_call_target="tpu_custom_call" | custom-call | flops 24000000000 | bytes 6000000 | tf_op jit(solution)/shard_map/fill/pallas_call | solution.py:681
  52.2 0.0 collective-permute-done.4.refs_3_
  52.2 0.3 collective-permute-start.5
  52.5 0.0 collective-permute-done.2.sub_lo
  52.5 3.9 %collective-permute-start.6 = (f32[5,2,16,512]{3,2,1,0:T(8,128)S(1)}, f32[5,2,16,512]{3,2,1,0:T(8,128)S(1)}, u32[]{:S(2)}, u32[]{:S(2)}) collective-permute-start(f32[5,2,16,512]{3,2,1,0:T(8,128)S(1)} %get-tuple-element.21), channel_id=1, source_target_pairs={{16,0},{32,16},{48,32},{64,48},{80,64},{96,80},{112,96},{0,112},{1... | collective-permute-start | bytes 983048 | tf_op jit(solution)/shard_map/ppermute | solution.py:712
  56.4 0.0 collective-permute-done.3.sub_hi
  56.4 0.0 collective-permute-start.7
  56.4 0.0 collective-permute-done.major_lo
  56.4 0.0 copy-start.2
  56.4 5.3 %collective-permute-start.8 = (f32[5,2,12,512]{3,2,1,0:T(8,128)S(1)}, f32[5,2,12,512]{3,2,1,0:T(8,128)S(1)}, u32[]{:S(2)}, u32[]{:S(2)}) collective-permute-start(f32[5,2,12,512]{3,2,1,0:T(8,128)S(1)} %get-tuple-element.23), channel_id=1, source_target_pairs={{1,0},{2,1},{3,2},{4,3},{5,4},{6,5},{7,6},{8,7},{9,8},{10,9},{11,1... | collective-permute-start | bytes 737288 | tf_op jit(solution)/shard_map/ppermute | solution.py:712
  61.8 0.0 collective-permute-done.1.major_hi
  61.8 0.0 copy-done
  61.8 9.0 %cgrid_rate.1 = f32[5,16,32,256]{3,2,1,0:T(8,128)} custom-call(f32[5,16,32,256]{3,2,1,0:T(8,128)S(1)} %copy-done, f32[5,2,32,256]{3,2,1,0:T(8,128)S(1)} %collective-permute-done.major_lo, f32[5,2,32,256]{3,2,1,0:T(8,128)S(1)} %collective-permute-done.1.major_hi, f32[5,2,16,256]{3,2,1,0:T(8,128)S(1)} %collective-permute-done.2.sub_lo, ...), custom_call_target="tpu_custom_call" | custom-call | flops 39321600 | bytes 7864320 | tf_op jit(solution)/shard_map/cgrid_rate/pallas_call | solution.py:310
  70.8 0.0 collective-permute-done.7.sub_lo
  70.8 0.0 collective-permute-done.8.sub_hi
  70.9 0.0 collective-permute-done.5.major_lo
  70.9 0.0 collective-permute-done.6.major_hi
  70.9 8.7 %flap_rate.1 = f32[5,12,16,512]{3,2,1,0:T(8,128)} custom-call(f32[5,12,16,512]{3,2,1,0:T(8,128)S(1)} %get-tuple-element.19.q_hbm, f32[5,2,16,512]{3,2,1,0:T(8,128)S(1)} %collective-permute-done.5.major_lo, f32[5,2,16,512]{3,2,1,0:T(8,128)S(1)} %collective-permute-done.6.major_hi, f32[5,2,12,512]{3,2,1,0:T(8,128)S(1)} %collective-permute-done.7.sub_lo, ...), custom_call_target="tpu_custom_call" | custom-call | flops 29491200 | bytes 5898240 | tf_op jit(solution)/shard_map/flap_rate/pallas_call | solution.py:310
  (8 shorter events, 0.0 us)
Async XLA Ops:
  0.6 33.6 %copy-start.3 = (s32[16,12,512]{2,0,1:T(8,128)S(1)}, s32[16,12,512]{2,0,1:T(8,128)}, u32[]{:S(2)}) copy-start(s32[16,12,512]{2,0,1:T(8,128)} %param.12) | copy-start | bytes 1179652
  0.6 33.6 %copy-start.7 = (s32[16,12,512]{2,0,1:T(8,128)S(1)}, s32[16,12,512]{2,0,1:T(8,128)}, u32[]{:S(2)}) copy-start(s32[16,12,512]{2,0,1:T(8,128)} %param.13) | copy-start | bytes 1179652
  14.8 19.4 %all-to-all-start = ((f32[8,5,1024]{2,1,0:T(8,128)}), f32[8,5,1024]{2,1,0:T(8,128)S(1)}, u32[]{:S(2)}, u32[]{:S(2)}) async-start(f32[8,5,1024]{2,1,0:T(8,128)} %get-tuple-element.18), calls=%async_computation | async-start | bytes 524288 | tf_op jit(solution)/shard_map/all_to_all | solution.py:725
  20.7 31.8 %collective-permute-start.2 = (f32[5,2,16,256]{3,2,1,0:T(8,128)}, f32[5,2,16,256]{3,2,1,0:T(8,128)S(1)}, u32[]{:S(2)}, u32[]{:S(2)}) collective-permute-start(f32[5,2,16,256]{3,2,1,0:T(8,128)} %get-tuple-element.15.refs_1_), channel_id=1, source_target_pairs={{0,16},{16,32},{32,48},{48,64},{64,80},{80,96},{96,112},{112,0},{1... | collective-permute-start | bytes 491528 | tf_op jit(solution)/shard_map/ppermute | solution.py:709
  22.8 33.6 %collective-permute-start.3 = (f32[5,2,16,256]{3,2,1,0:T(8,128)}, f32[5,2,16,256]{3,2,1,0:T(8,128)S(1)}, u32[]{:S(2)}, u32[]{:S(2)}) collective-permute-start(f32[5,2,16,256]{3,2,1,0:T(8,128)} %get-tuple-element.16.refs_0_), channel_id=1, source_target_pairs={{16,0},{32,16},{48,32},{64,48},{80,64},{96,80},{112,96},{0,112},{1... | collective-permute-start | bytes 491528 | tf_op jit(solution)/shard_map/ppermute | solution.py:712
  24.9 27.3 %collective-permute-start.4 = (f32[5,32,32]{2,1,0:T(8,128)}, f32[5,32,32]{2,1,0:T(8,128)S(1)}, u32[]{:S(2)}, u32[]{:S(2)}) collective-permute-start(f32[5,32,32]{2,1,0:T(8,128)} %get-tuple-element.17.refs_2_), channel_id=1, source_target_pairs={{0,112},{16,96},{32,32},{48,48},{64,64},{80,80},{96,16},{112,0},{1... | collective-permute-start | bytes 61448 | tf_op jit(solution)/shard_map/ppermute | solution.py:717
  28.8 27.6 %collective-permute-start = (f32[5,2,32,256]{3,2,1,0:T(8,128)}, f32[5,2,32,256]{3,2,1,0:T(8,128)S(1)}, u32[]{:S(2)}, u32[]{:S(2)}) collective-permute-start(f32[5,2,32,256]{3,2,1,0:T(8,128)} %get-tuple-element.13), channel_id=1, source_target_pairs={{0,1},{1,2},{2,3},{3,4},{4,5},{5,6},{6,7},{7,8},{8,9},{9,10},{10,1... | collective-permute-start | bytes 983048 | tf_op jit(solution)/shard_map/ppermute | solution.py:709
  28.9 32.9 %collective-permute-start.1 = (f32[5,2,32,256]{3,2,1,0:T(8,128)}, f32[5,2,32,256]{3,2,1,0:T(8,128)S(1)}, u32[]{:S(2)}, u32[]{:S(2)}) collective-permute-start(f32[5,2,32,256]{3,2,1,0:T(8,128)} %get-tuple-element.14), channel_id=1, source_target_pairs={{1,0},{2,1},{3,2},{4,3},{5,4},{6,5},{7,6},{8,7},{9,8},{10,9},{11,1... | collective-permute-start | bytes 983048 | tf_op jit(solution)/shard_map/ppermute | solution.py:712
  34.2 27.5 %copy-start = (f32[5,16,32,256]{3,2,1,0:T(8,128)S(1)}, f32[5,16,32,256]{3,2,1,0:T(8,128)}, u32[]{:S(2)}) copy-start(f32[5,16,32,256]{3,2,1,0:T(8,128)} %q_hbm.3) | copy-start | bytes 7864324
  34.2 27.5 %copy-start.1 = (f32[3,16,32,256]{3,2,1,0:T(8,128)S(1)}, f32[3,16,32,256]{3,2,1,0:T(8,128)}, u32[]{:S(2)}) copy-start(f32[3,16,32,256]{3,2,1,0:T(8,128)} %refs_4_.1) | copy-start | bytes 4718596
  34.3 27.5 %copy-start.4 = (f32[5,2,16,256]{3,2,1,0:T(8,128)S(1)}, f32[5,2,16,256]{3,2,1,0:T(8,128)}, u32[]{:S(2)}) copy-start(f32[5,2,16,256]{3,2,1,0:T(8,128)} %get-tuple-element.16.refs_0_) | copy-start | bytes 491524
  34.3 27.5 %copy-start.5 = (f32[5,2,16,256]{3,2,1,0:T(8,128)S(1)}, f32[5,2,16,256]{3,2,1,0:T(8,128)}, u32[]{:S(2)}) copy-start(f32[5,2,16,256]{3,2,1,0:T(8,128)} %get-tuple-element.15.refs_1_) | copy-start | bytes 491524
  34.3 27.5 %copy-start.6 = (f32[5,32,32]{2,1,0:T(8,128)S(1)}, f32[5,32,32]{2,1,0:T(8,128)}, u32[]{:S(2)}) copy-start(f32[5,32,32]{2,1,0:T(8,128)} %get-tuple-element.17.refs_2_) | copy-start | bytes 61444
  52.2 18.7 %collective-permute-start.5 = (f32[5,2,16,512]{3,2,1,0:T(8,128)S(1)}, f32[5,2,16,512]{3,2,1,0:T(8,128)S(1)}, u32[]{:S(2)}, u32[]{:S(2)}) collective-permute-start(f32[5,2,16,512]{3,2,1,0:T(8,128)S(1)} %get-tuple-element.20), channel_id=1, source_target_pairs={{0,16},{16,32},{32,48},{48,64},{64,80},{80,96},{96,112},{112,0},{1... | collective-permute-start | bytes 983048 | tf_op jit(solution)/shard_map/ppermute | solution.py:709
  52.5 18.4 %collective-permute-start.6 = (f32[5,2,16,512]{3,2,1,0:T(8,128)S(1)}, f32[5,2,16,512]{3,2,1,0:T(8,128)S(1)}, u32[]{:S(2)}, u32[]{:S(2)}) collective-permute-start(f32[5,2,16,512]{3,2,1,0:T(8,128)S(1)} %get-tuple-element.21), channel_id=1, source_target_pairs={{16,0},{32,16},{48,32},{64,48},{80,64},{96,80},{112,96},{0,112},{1... | collective-permute-start | bytes 983048 | tf_op jit(solution)/shard_map/ppermute | solution.py:712
  56.4 14.4 %collective-permute-start.7 = (f32[5,2,12,512]{3,2,1,0:T(8,128)S(1)}, f32[5,2,12,512]{3,2,1,0:T(8,128)S(1)}, u32[]{:S(2)}, u32[]{:S(2)}) collective-permute-start(f32[5,2,12,512]{3,2,1,0:T(8,128)S(1)} %get-tuple-element.22), channel_id=1, source_target_pairs={{0,1},{1,2},{2,3},{3,4},{4,5},{5,6},{6,7},{7,8},{8,9},{9,10},{10,1... | collective-permute-start | bytes 737288 | tf_op jit(solution)/shard_map/ppermute | solution.py:709
  56.4 14.5 %copy-start.2 = (f32[3,16,12,512]{3,1,2,0:T(8,128)S(1)}, f32[3,16,12,512]{3,1,2,0:T(8,128)}, u32[]{:S(2)}) copy-start(f32[3,16,12,512]{3,1,2,0:T(8,128)} %param.11) | copy-start | bytes 3538948
  56.4 14.4 %collective-permute-start.8 = (f32[5,2,12,512]{3,2,1,0:T(8,128)S(1)}, f32[5,2,12,512]{3,2,1,0:T(8,128)S(1)}, u32[]{:S(2)}, u32[]{:S(2)}) collective-permute-start(f32[5,2,12,512]{3,2,1,0:T(8,128)S(1)} %get-tuple-element.23), channel_id=1, source_target_pairs={{1,0},{2,1},{3,2},{4,3},{5,4},{6,5},{7,6},{8,7},{9,8},{10,9},{11,1... | collective-permute-start | bytes 737288 | tf_op jit(solution)/shard_map/ppermute | solution.py:712

commit v9 on v7

--- a/solution.py
+++ b/solution.py
@@ -79,16 +79,17 @@
     metric_rows,
 ):
     if cgrid:
-        own_lo, own_hi, wall_own, wall_far, metric_ref, out_ref, qe, prim, sub_edge, lane_edge, sems = refs
+        own_lo, own_hi, wall_own, wall_far, metric_ref, out_ref, qe, prim, sub_edge, lane_edge, mix, sems = refs
     else:
         own_lo = own_hi = None
-        mask_ref, metric_ref, out_ref, qe, prim, sub_edge, sems = refs
+        mask_ref, metric_ref, out_ref, qe, prim, sub_edge, mix, sems = refs
     planes, rows, lanes = qe.shape[1] - 4, qe.shape[2], qe.shape[3]
     step = pl.program_id(0)
     place, count = lax.axis_index("wrap"), lax.axis_size("wrap")
     at_start = place == 0
     at_end = place == count - 1
     major_m, sub_m, lane_m = components
+    width = mix.shape[1]
 
     def edge_fields(q1, q2, m, side):
         prims = primitives(q1)
@@ -147,8 +148,33 @@
                     parts.append(jnp.where(in_wake, far, sign * own))
                 ghosts.append(jnp.concatenate(parts, axis=0))
             second = [pltpu.roll(x, 127, 1) for x in ghosts]
-            for i, x in enumerate(edge_fields(ghosts, second, lane_m, -1)):
-                lane_edge[i] = x
+            fields = edge_fields(ghosts, second, lane_m, -1)
+            even = lax.broadcasted_iota(i32, (rows, 128), 1) % 2 == 0
+            for c in range(5):
+                lane_edge[c] = jnp.where(even, fields[c], -pltpu.roll(ghosts[c], 1, 1))
+            for i in range(4):
+                lane_edge[5 + i] = jnp.where(even, fields[10 + i], 0.0)
+
+        source = lax.broadcasted_iota(i32, (lanes, width), 0)
+        target = lax.broadcasted_iota(i32, (lanes, width), 1)
+        apart = source - target
+        apart = jnp.where(apart > lanes - 3, apart - lanes, apart)
+
+        def band(*pairs):
+            total = jnp.zeros((lanes, width), f32)
+            for distance, factor in pairs:
+                if cgrid:
+                    total += jnp.where(source == jnp.minimum(target + distance, lanes - 1), factor, 0.0)
+                else:
+                    total = jnp.where(apart == distance, factor, total)
+            return total.astype(bf16)
+
+        bands = [band((1, -1.0), (-1, 1.0))] * 2
+        bands += [band((1, 4.0), (-1, 4.0), (2, -1.0), (-2, -1.0))] * 2
+        bands += [band((1, 1.0), (-1, 1.0))] * 2
+        for i, x in enumerate(bands):
+            mix[i * lanes : (i + 1) * lanes, :] = x
+
         copies[0].wait()
         part(0).wait()
         part(1).wait()
@@ -180,7 +206,6 @@
     row_at = lax.broadcasted_iota(i32, (8, lanes), 0)
     lane_at = lax.broadcasted_iota(i32, (rows, 128), 1)
     row_first, row_last = row_at == 0, row_at == 7
-    lane_first, lane_last = lane_at == 0, lane_at == 127
 
     def one(b, _):
         k = step * step_planes + b
@@ -199,23 +224,6 @@
             moved += [pltpu.roll(x[r : r + 8], 1, 0) for r in range(0, rows, 8)]
             return jnp.concatenate(
                 [jnp.where(row_first, moved[r], moved[r + 1]) for r in range(rows // 8)], axis=0
-            )
-
-        def lane_next(x):
-            moved = [pltpu.roll(x[:, t : t + 128], 127, 1) for t in range(0, lanes, 128)]
-            moved.append(x[:, lanes - 128 :] if cgrid else moved[0])
-            return jnp.concatenate(
-                [jnp.where(lane_last, moved[t + 1], moved[t]) for t in range(lanes // 128)], axis=1
-            )
-
-        def lane_prior(x, i):
-            moved = [pltpu.roll(x[:, t : t + 128], 1, 1) for t in range(0, lanes, 128)]
-            if cgrid:
-                moved.insert(0, pltpu.roll(lane_edge[i], lax.rem(128 - 2 * k, 128), 1))
-            else:
-                moved.insert(0, moved[-1])
-            return jnp.concatenate(
-                [jnp.where(lane_first, moved[t], moved[t + 1]) for t in range(lanes // 128)], axis=1
             )
 
         gm = metric_ref[metric_rows[0], b]
@@ -226,16 +234,38 @@
         all2 = 2.0 * (gm2 + gs2 + gl2)
         all6 = 6.0 * (gm + gs + gl)
         mine = [prim[here, i] for i in range(5)]
+        q = [qe[c, k + 2] for c in range(5)]
+        lane_flux = flux(q, mine, lane_m)
+
+        def lane_mixed(groups, mixer, edge):
+            parts = [[part for x in group for part in split_two(x)] for group in groups]
+            lines = []
+            for t in range(0, lanes, width):
+                for row in parts:
+                    turned = [jnp.concatenate([x[:, t:], x[:, :t]], axis=1) if t else x for x in row]
+                    lines.append(jnp.concatenate(turned, axis=1))
+            mixed = jnp.dot(jnp.concatenate(lines, axis=0), mixer, preferred_element_type=f32)
+            results = []
+            for i in range(len(groups)):
+                at = [(i + n * len(groups)) * rows for n in range(lanes // width)]
+                x = jnp.concatenate([mixed[r : r + rows] for r in at], axis=1)
+                if cgrid:
+                    ghost = pltpu.roll(lane_edge[edge + i], lax.rem(128 - 2 * k, 128), 1)
+                    ghost = jnp.where(lane_at < 2, ghost, 0.0)
+                    x = jnp.concatenate([x[:, 0:128] + ghost, x[:, 128:]], axis=1)
+                results.append(x)
+            return results
+
+        lane_damped = lane_mixed([(lane_flux[c], q[c]) for c in range(5)], mix[0 : 4 * lanes, :], 0)
+        lane_curved = lane_mixed([(mine[i],) for i in (0, 1, 2, 4)], mix[4 * lanes :, :], 5)
         viscous = {}
         for i, c, e in ((0, 1, 10), (1, 2, 11), (2, 3, 12), (4, 4, 13)):
             x = mine[i]
             total = gm2 * (prim[above, i] + prim[below, i])
             total += gs2 * (sub_next(x, e) + sub_prior(x, e))
-            total += gl2 * (lane_next(x) + lane_prior(x, e))
+            total += gl2 * lane_curved[c - 1]
             viscous[c] = total - all2 * x
-        q = [qe[c, k + 2] for c in range(5)]
         sub_flux = flux(q, mine, sub_m)
-        lane_flux = flux(q, mine, lane_m)
         for c in range(5):
             x = q[c]
             four = 4.0 * x
@@ -247,9 +277,7 @@
             up = four - sub_flux[c] - sub_next(x, 5 + c)
             down = four + sub_flux[c] - sub_prior(x, 5 + c)
             total += gs * (sub_next(up, c) + sub_prior(down, c))
-            up = four - lane_flux[c] - lane_next(x)
-            down = four + lane_flux[c] - lane_prior(x, 5 + c)
-            total += gl * (lane_next(up) + lane_prior(down, c))
+            total += gl * lane_damped[c]
             total -= all6 * x
             if c:
                 total += viscous[c]
@@ -287,7 +315,8 @@
             pltpu.VMEM((3, 10, rows, lanes), f32),
             pltpu.VMEM((2, 14, planes, lanes), f32),
         ]
-        + [pltpu.VMEM((14, rows, 128), f32)] * cgrid
+        + [pltpu.VMEM((9, rows, 128), f32)] * cgrid
+        + [pltpu.VMEM((6 * lanes, 256), bf16)]
         + [pltpu.SemaphoreType.DMA((planes // step_planes + 2,))],
         compiler_params=params(),
         cost_estimate=pl.CostEstimate(
@@ -653,7 +682,7 @@
             pltpu.VMEM(state.shape, f32),
             pltpu.SemaphoreType.DMA((planes,)),
         ],
-        compiler_params=params(40 * 1024 * 1024),
+        compiler_params=params(49 * 1024 * 1024),
         cost_estimate=pl.CostEstimate(flops=24 * 10**9, bytes_accessed=6 * 10**6, transcendentals=0),
         name="fill",
     )(source, mask, state, slot)

time: 83.5 us -> 79.2 us (0.949)
  Pallas kernels: 51.9 us -> 49.1 us
  local copies, waits for them, and re-layouts: 1.57 us -> 0.04 us
    pallas_call x2, Pallas kernels: 20.3 us -> 17.1 us  [rate(): pl.pallas_call(functools.partial(rate_kernel, cgrid=cgrid, step_planes=st...]
    unnamed x18 -> x16, local copies, waits for them, and re-layouts: 1.57 us -> 0.04 us
  transfers between devices with their start and end apart: 10 -> 10, of which waited for: 0 -> 0; matrix products, arithmetic and copies ran while one was open for 0% -> 0% of each run, Pallas kernels for 35% -> 34%
where the time goes in v9:
time: 79.2 us; the launch traced here: 78.9 us
  Pallas kernels  49.1 us (62%)
  starting transfers between devices  28.9 us (36%)
  between operations  0.82 us (1%)
    pallas_call x1, Pallas kernels, fill(): pl.pallas_call(fill_kernel, grid=(planes,), in_specs=[plane, plane, IN_HB...  17.9 us
    pallas_call x2, Pallas kernels, rate(): pl.pallas_call(functools.partial(rate_kernel, cgrid=cgrid, step_planes=st...  17.1 us
    ppermute x4, starting transfers between devices, back(): return lax.ppermute(value, axis, [(j, i) for i, j in ring(axis)])  16.7 us
    pallas_call x1, Pallas kernels, donors(): pl.pallas_call(donor_kernel, grid=(1,), in_specs=[IN_VMEM, IN_VMEM, IN_HB...  14.2 us
    all_to_all x1, starting transfers between devices, body(): slot = lax.all_to_all(slot, 'wrap', split_axis=0, concat_axis=0, tiled=True)  5.92 us
    ppermute x1, starting transfers between devices, body(): lax.ppermute(wall, 'wrap', [(i, wrap_count - 1 - i if wrapped(i, wrap_cou...  3.89 us
    ppermute x4, starting transfers between devices, onward(): return lax.ppermute(value, axis, ring(axis))  2.42 us
  transfers between devices with their start and end apart: 10, of which 0 were waited for; matrix products, arithmetic and copies ran while one was open for 0% of the time, Pallas kernels for 34%

profile of v9, /device:TPU:0, one launch (start us, length us, event | category | flops | bytes accessed | tf_op | source)
XLA Modules:
  0.0 78.9 jit_solution(9802613137347559469)
XLA Ops:
  0.6 0.0 copy-start.3
  0.6 0.0 copy-start.7
  0.7 14.2 %donors.1 = (f32[8,5,1024]{2,1,0:T(8,128)}, f32[5,2,16,256]{3,2,1,0:T(8,128)}, f32[5,2,16,256]{3,2,1,0:T(8,128)}, f32[5,2,32,256]{3,2,1,0:T(8,128)}, f32[5,2,32,256]{3,2,1,0:T(8,128)}, /*index=5*/f32[5,32,32]{2,1,0:T(8,128)}) custom-call(s32[8,1024]{1,0:T(8,128)} %bitcast.15, f32[3,8,1024]{2,1,0:T(8,128)} %bitcast.14, f32[5,16,32,256]{3,2,1,0:T(8,128)} %q_hbm.3), custom_call_target="tpu_custom_call" | custom-call | tf_op jit(solution)/shard_map/donors/pallas_call | solution.py:567
  14.8 5.9 %all-to-all-start = ((f32[8,5,1024]{2,1,0:T(8,128)}), f32[8,5,1024]{2,1,0:T(8,128)S(1)}, u32[]{:S(2)}, u32[]{:S(2)}) async-start(f32[8,5,1024]{2,1,0:T(8,128)} %get-tuple-element.18), calls=%async_computation | async-start | bytes 524288 | tf_op jit(solution)/shard_map/all_to_all | solution.py:717
  20.7 2.0 %collective-permute-start.2 = (f32[5,2,16,256]{3,2,1,0:T(8,128)}, f32[5,2,16,256]{3,2,1,0:T(8,128)S(1)}, u32[]{:S(2)}, u32[]{:S(2)}) collective-permute-start(f32[5,2,16,256]{3,2,1,0:T(8,128)} %get-tuple-element.15.refs_1_), channel_id=1, source_target_pairs={{0,16},{16,32},{32,48},{48,64},{64,80},{80,96},{96,112},{112,0},{1... | collective-permute-start | bytes 491528 | tf_op jit(solution)/shard_map/ppermute | solution.py:701
  22.8 2.1 %collective-permute-start.3 = (f32[5,2,16,256]{3,2,1,0:T(8,128)}, f32[5,2,16,256]{3,2,1,0:T(8,128)S(1)}, u32[]{:S(2)}, u32[]{:S(2)}) collective-permute-start(f32[5,2,16,256]{3,2,1,0:T(8,128)} %get-tuple-element.16.refs_0_), channel_id=1, source_target_pairs={{16,0},{32,16},{48,32},{64,48},{80,64},{96,80},{112,96},{0,112},{1... | collective-permute-start | bytes 491528 | tf_op jit(solution)/shard_map/ppermute | solution.py:704
  24.9 3.9 %collective-permute-start.4 = (f32[5,32,32]{2,1,0:T(8,128)}, f32[5,32,32]{2,1,0:T(8,128)S(1)}, u32[]{:S(2)}, u32[]{:S(2)}) collective-permute-start(f32[5,32,32]{2,1,0:T(8,128)} %get-tuple-element.17.refs_2_), channel_id=1, source_target_pairs={{0,112},{16,96},{32,32},{48,48},{64,64},{80,80},{96,16},{112,0},{1... | collective-permute-start | bytes 61448 | tf_op jit(solution)/shard_map/ppermute | solution.py:709
  28.8 0.1 collective-permute-start
  28.9 5.3 %collective-permute-start.1 = (f32[5,2,32,256]{3,2,1,0:T(8,128)}, f32[5,2,32,256]{3,2,1,0:T(8,128)S(1)}, u32[]{:S(2)}, u32[]{:S(2)}) collective-permute-start(f32[5,2,32,256]{3,2,1,0:T(8,128)} %get-tuple-element.14), channel_id=1, source_target_pairs={{1,0},{2,1},{3,2},{4,3},{5,4},{6,5},{7,6},{8,7},{9,8},{10,9},{11,1... | collective-permute-start | bytes 983048 | tf_op jit(solution)/shard_map/ppermute | solution.py:704
  34.2 0.0 all-to-all-done.slot_ref
  34.2 0.0 copy-done.3
  34.2 0.0 copy-done.7
  34.2 0.0 copy-start
  34.2 0.0 copy-start.1
  34.3 17.9 %fill.1 = (f32[5,12,16,512]{3,2,1,0:T(8,128)S(1)}, f32[5,2,16,512]{3,2,1,0:T(8,128)S(1)}, f32[5,2,16,512]{3,2,1,0:T(8,128)S(1)}, f32[5,2,12,512]{3,2,1,0:T(8,128)S(1)}, f32[5,2,12,512]{3,2,1,0:T(8,128)S(1)}) custom-call(s32[12,16,512]{2,1,0:T(8,128)S(1)} %bitcast.12, s32[12,16,512]{2,1,0:T(8,128)S(1)} %bitcast.10, f32[5,12,16,512]{3,2,1,0:T(8,128)} %bitcast.16, ...), custom_call_target="tpu_custom_call" | custom-call | flops 24000000000 | bytes 6000000 | tf_op jit(solution)/shard_map/fill/pallas_call | solution.py:673
  52.2 0.0 collective-permute-done.4.refs_3_
  52.2 0.3 collective-permute-start.5
  52.5 0.0 collective-permute-done.2.sub_lo
  52.5 3.9 %collective-permute-start.6 = (f32[5,2,16,512]{3,2,1,0:T(8,128)S(1)}, f32[5,2,16,512]{3,2,1,0:T(8,128)S(1)}, u32[]{:S(2)}, u32[]{:S(2)}) collective-permute-start(f32[5,2,16,512]{3,2,1,0:T(8,128)S(1)} %get-tuple-element.21), channel_id=1, source_target_pairs={{16,0},{32,16},{48,32},{64,48},{80,64},{96,80},{112,96},{0,112},{1... | collective-permute-start | bytes 983048 | tf_op jit(solution)/shard_map/ppermute | solution.py:704
  56.4 0.0 collective-permute-done.3.sub_hi
  56.4 0.0 collective-permute-start.7
  56.4 0.0 collective-permute-done.major_lo
  56.4 0.0 copy-start.2
  56.4 5.3 %collective-permute-start.8 = (f32[5,2,12,512]{3,2,1,0:T(8,128)S(1)}, f32[5,2,12,512]{3,2,1,0:T(8,128)S(1)}, u32[]{:S(2)}, u32[]{:S(2)}) collective-permute-start(f32[5,2,12,512]{3,2,1,0:T(8,128)S(1)} %get-tuple-element.23), channel_id=1, source_target_pairs={{1,0},{2,1},{3,2},{4,3},{5,4},{6,5},{7,6},{8,7},{9,8},{10,9},{11,1... | collective-permute-start | bytes 737288 | tf_op jit(solution)/shard_map/ppermute | solution.py:704
  61.8 0.0 collective-permute-done.1.major_hi
  61.8 0.0 copy-done
  61.8 9.0 %cgrid_rate.1 = f32[5,16,32,256]{3,2,1,0:T(8,128)} custom-call(f32[5,16,32,256]{3,2,1,0:T(8,128)S(1)} %copy-done, f32[5,2,32,256]{3,2,1,0:T(8,128)S(1)} %collective-permute-done.major_lo, f32[5,2,32,256]{3,2,1,0:T(8,128)S(1)} %collective-permute-done.1.major_hi, f32[5,2,16,256]{3,2,1,0:T(8,128)S(1)} %collective-permute-done.2.sub_lo, ...), custom_call_target="tpu_custom_call" | custom-call | flops 39321600 | bytes 7864320 | tf_op jit(solution)/shard_map/cgrid_rate/pallas_call | solution.py:301
  70.8 0.0 collective-permute-done.7.sub_lo
  70.8 0.0 collective-permute-done.8.sub_hi
  70.9 0.0 collective-permute-done.5.major_lo
  70.9 0.0 collective-permute-done.6.major_hi
  70.9 8.1 %flap_rate.1 = f32[5,12,16,512]{3,2,1,0:T(8,128)} custom-call(f32[5,12,16,512]{3,2,1,0:T(8,128)S(1)} %get-tuple-element.19.q_hbm, f32[5,2,16,512]{3,2,1,0:T(8,128)S(1)} %collective-permute-done.5.major_lo, f32[5,2,16,512]{3,2,1,0:T(8,128)S(1)} %collective-permute-done.6.major_hi, f32[5,2,12,512]{3,2,1,0:T(8,128)S(1)} %collective-permute-done.7.sub_lo, ...), custom_call_target="tpu_custom_call" | custom-call | flops 29491200 | bytes 5898240 | tf_op jit(solution)/shard_map/flap_rate/pallas_call | solution.py:301
  (8 shorter events, 0.0 us)
Async XLA Ops:
  0.6 33.6 %copy-start.3 = (s32[16,12,512]{2,0,1:T(8,128)S(1)}, s32[16,12,512]{2,0,1:T(8,128)}, u32[]{:S(2)}) copy-start(s32[16,12,512]{2,0,1:T(8,128)} %param.12) | copy-start | bytes 1179652
  0.6 33.6 %copy-start.7 = (s32[16,12,512]{2,0,1:T(8,128)S(1)}, s32[16,12,512]{2,0,1:T(8,128)}, u32[]{:S(2)}) copy-start(s32[16,12,512]{2,0,1:T(8,128)} %param.13) | copy-start | bytes 1179652
  14.8 19.4 %all-to-all-start = ((f32[8,5,1024]{2,1,0:T(8,128)}), f32[8,5,1024]{2,1,0:T(8,128)S(1)}, u32[]{:S(2)}, u32[]{:S(2)}) async-start(f32[8,5,1024]{2,1,0:T(8,128)} %get-tuple-element.18), calls=%async_computation | async-start | bytes 524288 | tf_op jit(solution)/shard_map/all_to_all | solution.py:717
  20.7 31.8 %collective-permute-start.2 = (f32[5,2,16,256]{3,2,1,0:T(8,128)}, f32[5,2,16,256]{3,2,1,0:T(8,128)S(1)}, u32[]{:S(2)}, u32[]{:S(2)}) collective-permute-start(f32[5,2,16,256]{3,2,1,0:T(8,128)} %get-tuple-element.15.refs_1_), channel_id=1, source_target_pairs={{0,16},{16,32},{32,48},{48,64},{64,80},{80,96},{96,112},{112,0},{1... | collective-permute-start | bytes 491528 | tf_op jit(solution)/shard_map/ppermute | solution.py:701
  22.8 33.6 %collective-permute-start.3 = (f32[5,2,16,256]{3,2,1,0:T(8,128)}, f32[5,2,16,256]{3,2,1,0:T(8,128)S(1)}, u32[]{:S(2)}, u32[]{:S(2)}) collective-permute-start(f32[5,2,16,256]{3,2,1,0:T(8,128)} %get-tuple-element.16.refs_0_), channel_id=1, source_target_pairs={{16,0},{32,16},{48,32},{64,48},{80,64},{96,80},{112,96},{0,112},{1... | collective-permute-start | bytes 491528 | tf_op jit(solution)/shard_map/ppermute | solution.py:704
  24.9 27.3 %collective-permute-start.4 = (f32[5,32,32]{2,1,0:T(8,128)}, f32[5,32,32]{2,1,0:T(8,128)S(1)}, u32[]{:S(2)}, u32[]{:S(2)}) collective-permute-start(f32[5,32,32]{2,1,0:T(8,128)} %get-tuple-element.17.refs_2_), channel_id=1, source_target_pairs={{0,112},{16,96},{32,32},{48,48},{64,64},{80,80},{96,16},{112,0},{1... | collective-permute-start | bytes 61448 | tf_op jit(solution)/shard_map/ppermute | solution.py:709
  28.8 27.6 %collective-permute-start = (f32[5,2,32,256]{3,2,1,0:T(8,128)}, f32[5,2,32,256]{3,2,1,0:T(8,128)S(1)}, u32[]{:S(2)}, u32[]{:S(2)}) collective-permute-start(f32[5,2,32,256]{3,2,1,0:T(8,128)} %get-tuple-element.13), channel_id=1, source_target_pairs={{0,1},{1,2},{2,3},{3,4},{4,5},{5,6},{6,7},{7,8},{8,9},{9,10},{10,1... | collective-permute-start | bytes 983048 | tf_op jit(solution)/shard_map/ppermute | solution.py:701
  28.9 32.9 %collective-permute-start.1 = (f32[5,2,32,256]{3,2,1,0:T(8,128)}, f32[5,2,32,256]{3,2,1,0:T(8,128)S(1)}, u32[]{:S(2)}, u32[]{:S(2)}) collective-permute-start(f32[5,2,32,256]{3,2,1,0:T(8,128)} %get-tuple-element.14), channel_id=1, source_target_pairs={{1,0},{2,1},{3,2},{4,3},{5,4},{6,5},{7,6},{8,7},{9,8},{10,9},{11,1... | collective-permute-start | bytes 983048 | tf_op jit(solution)/shard_map/ppermute | solution.py:704
  34.2 27.5 %copy-start = (f32[5,16,32,256]{3,2,1,0:T(8,128)S(1)}, f32[5,16,32,256]{3,2,1,0:T(8,128)}, u32[]{:S(2)}) copy-start(f32[5,16,32,256]{3,2,1,0:T(8,128)} %q_hbm.3) | copy-start | bytes 7864324
  34.2 27.5 %copy-start.1 = (f32[3,16,32,256]{3,2,1,0:T(8,128)S(1)}, f32[3,16,32,256]{3,2,1,0:T(8,128)}, u32[]{:S(2)}) copy-start(f32[3,16,32,256]{3,2,1,0:T(8,128)} %refs_4_.1) | copy-start | bytes 4718596
  34.3 27.5 %copy-start.4 = (f32[5,2,16,256]{3,2,1,0:T(8,128)S(1)}, f32[5,2,16,256]{3,2,1,0:T(8,128)}, u32[]{:S(2)}) copy-start(f32[5,2,16,256]{3,2,1,0:T(8,128)} %get-tuple-element.16.refs_0_) | copy-start | bytes 491524
  34.3 27.5 %copy-start.5 = (f32[5,2,16,256]{3,2,1,0:T(8,128)S(1)}, f32[5,2,16,256]{3,2,1,0:T(8,128)}, u32[]{:S(2)}) copy-start(f32[5,2,16,256]{3,2,1,0:T(8,128)} %get-tuple-element.15.refs_1_) | copy-start | bytes 491524
  34.3 27.5 %copy-start.6 = (f32[5,32,32]{2,1,0:T(8,128)S(1)}, f32[5,32,32]{2,1,0:T(8,128)}, u32[]{:S(2)}) copy-start(f32[5,32,32]{2,1,0:T(8,128)} %get-tuple-element.17.refs_2_) | copy-start | bytes 61444
  52.2 18.7 %collective-permute-start.5 = (f32[5,2,16,512]{3,2,1,0:T(8,128)S(1)}, f32[5,2,16,512]{3,2,1,0:T(8,128)S(1)}, u32[]{:S(2)}, u32[]{:S(2)}) collective-permute-start(f32[5,2,16,512]{3,2,1,0:T(8,128)S(1)} %get-tuple-element.20), channel_id=1, source_target_pairs={{0,16},{16,32},{32,48},{48,64},{64,80},{80,96},{96,112},{112,0},{1... | collective-permute-start | bytes 983048 | tf_op jit(solution)/shard_map/ppermute | solution.py:701
  52.5 18.4 %collective-permute-start.6 = (f32[5,2,16,512]{3,2,1,0:T(8,128)S(1)}, f32[5,2,16,512]{3,2,1,0:T(8,128)S(1)}, u32[]{:S(2)}, u32[]{:S(2)}) collective-permute-start(f32[5,2,16,512]{3,2,1,0:T(8,128)S(1)} %get-tuple-element.21), channel_id=1, source_target_pairs={{16,0},{32,16},{48,32},{64,48},{80,64},{96,80},{112,96},{0,112},{1... | collective-permute-start | bytes 983048 | tf_op jit(solution)/shard_map/ppermute | solution.py:704
  56.4 14.4 %collective-permute-start.7 = (f32[5,2,12,512]{3,2,1,0:T(8,128)S(1)}, f32[5,2,12,512]{3,2,1,0:T(8,128)S(1)}, u32[]{:S(2)}, u32[]{:S(2)}) collective-permute-start(f32[5,2,12,512]{3,2,1,0:T(8,128)S(1)} %get-tuple-element.22), channel_id=1, source_target_pairs={{0,1},{1,2},{2,3},{3,4},{4,5},{5,6},{6,7},{7,8},{8,9},{9,10},{10,1... | collective-permute-start | bytes 737288 | tf_op jit(solution)/shard_map/ppermute | solution.py:701
  56.4 14.5 %copy-start.2 = (f32[3,16,12,512]{3,1,2,0:T(8,128)S(1)}, f32[3,16,12,512]{3,1,2,0:T(8,128)}, u32[]{:S(2)}) copy-start(f32[3,16,12,512]{3,1,2,0:T(8,128)} %param.11) | copy-start | bytes 3538948
  56.4 14.4 %collective-permute-start.8 = (f32[5,2,12,512]{3,2,1,0:T(8,128)S(1)}, f32[5,2,12,512]{3,2,1,0:T(8,128)S(1)}, u32[]{:S(2)}, u32[]{:S(2)}) collective-permute-start(f32[5,2,12,512]{3,2,1,0:T(8,128)S(1)} %get-tuple-element.23), channel_id=1, source_target_pairs={{1,0},{2,1},{3,2},{4,3},{5,4},{6,5},{7,6},{8,7},{9,8},{10,9},{11,1... | collective-permute-start | bytes 737288 | tf_op jit(solution)/shard_map/ppermute | solution.py:704

commit v10 on v9

--- a/solution.py
+++ b/solution.py
@@ -13,7 +13,7 @@
 VMEM_LIMIT = 40 * 1024 * 1024
 IN_HBM = pl.BlockSpec(memory_space=pltpu.HBM)
 IN_VMEM = pl.BlockSpec(memory_space=pltpu.VMEM)
-GROUP = 8
+GROUP = 16
 
 f32, bf16, i32 = jnp.float32, jnp.bfloat16, jnp.int32
 

time: 79.2 us -> 79 us (level)
  no operation moved by 1% of the time
where the time goes in v10:
time: 79 us; the launch traced here: 78.8 us
  Pallas kernels  48.8 us (62%)
  starting transfers between devices  28.9 us (37%)
  between operations  0.98 us (1%)
    pallas_call x1, Pallas kernels, fill(): pl.pallas_call(fill_kernel, grid=(planes,), in_specs=[plane, plane, IN_HB...  17.9 us
    pallas_call x2, Pallas kernels, rate(): pl.pallas_call(functools.partial(rate_kernel, cgrid=cgrid, step_planes=st...  17.1 us
    ppermute x4, starting transfers between devices, back(): return lax.ppermute(value, axis, [(j, i) for i, j in ring(axis)])  16.7 us
    pallas_call x1, Pallas kernels, donors(): pl.pallas_call(donor_kernel, grid=(1,), in_specs=[IN_VMEM, IN_VMEM, IN_HB...  13.8 us
    all_to_all x1, starting transfers between devices, body(): slot = lax.all_to_all(slot, 'wrap', split_axis=0, concat_axis=0, tiled=True)  5.92 us
    ppermute x1, starting transfers between devices, body(): lax.ppermute(wall, 'wrap', [(i, wrap_count - 1 - i if wrapped(i, wrap_cou...  3.89 us
    ppermute x4, starting transfers between devices, onward(): return lax.ppermute(value, axis, ring(axis))  2.42 us
  transfers between devices with their start and end apart: 10, of which 0 were waited for; matrix products, arithmetic and copies ran while one was open for 0% of the time, Pallas kernels for 34%

profile of v10, /device:TPU:0, one launch (start us, length us, event | category | flops | bytes accessed | tf_op | source)
XLA Modules:
  0.0 78.8 jit_solution(14511286697443533427)
XLA Ops:
  0.6 0.0 copy-start.3
  0.6 0.0 copy-start.7
  0.7 13.8 %donors.1 = (f32[8,5,1024]{2,1,0:T(8,128)}, f32[5,2,16,256]{3,2,1,0:T(8,128)}, f32[5,2,16,256]{3,2,1,0:T(8,128)}, f32[5,2,32,256]{3,2,1,0:T(8,128)}, f32[5,2,32,256]{3,2,1,0:T(8,128)}, /*index=5*/f32[5,32,32]{2,1,0:T(8,128)}) custom-call(s32[8,1024]{1,0:T(8,128)} %bitcast.15, f32[3,8,1024]{2,1,0:T(8,128)} %bitcast.14, f32[5,16,32,256]{3,2,1,0:T(8,128)} %q_hbm.3), custom_call_target="tpu_custom_call" | custom-call | tf_op jit(solution)/shard_map/donors/pallas_call | solution.py:567
  14.5 5.9 %all-to-all-start = ((f32[8,5,1024]{2,1,0:T(8,128)}), f32[8,5,1024]{2,1,0:T(8,128)S(1)}, u32[]{:S(2)}, u32[]{:S(2)}) async-start(f32[8,5,1024]{2,1,0:T(8,128)} %get-tuple-element.18), calls=%async_computation | async-start | bytes 524288 | tf_op jit(solution)/shard_map/all_to_all | solution.py:717
  20.4 2.0 %collective-permute-start.2 = (f32[5,2,16,256]{3,2,1,0:T(8,128)}, f32[5,2,16,256]{3,2,1,0:T(8,128)S(1)}, u32[]{:S(2)}, u32[]{:S(2)}) collective-permute-start(f32[5,2,16,256]{3,2,1,0:T(8,128)} %get-tuple-element.15.refs_1_), channel_id=1, source_target_pairs={{0,16},{16,32},{32,48},{48,64},{64,80},{80,96},{96,112},{112,0},{1... | collective-permute-start | bytes 491528 | tf_op jit(solution)/shard_map/ppermute | solution.py:701
  22.4 2.1 %collective-permute-start.3 = (f32[5,2,16,256]{3,2,1,0:T(8,128)}, f32[5,2,16,256]{3,2,1,0:T(8,128)S(1)}, u32[]{:S(2)}, u32[]{:S(2)}) collective-permute-start(f32[5,2,16,256]{3,2,1,0:T(8,128)} %get-tuple-element.16.refs_0_), channel_id=1, source_target_pairs={{16,0},{32,16},{48,32},{64,48},{80,64},{96,80},{112,96},{0,112},{1... | collective-permute-start | bytes 491528 | tf_op jit(solution)/shard_map/ppermute | solution.py:704
  24.5 3.9 %collective-permute-start.4 = (f32[5,32,32]{2,1,0:T(8,128)}, f32[5,32,32]{2,1,0:T(8,128)S(1)}, u32[]{:S(2)}, u32[]{:S(2)}) collective-permute-start(f32[5,32,32]{2,1,0:T(8,128)} %get-tuple-element.17.refs_2_), channel_id=1, source_target_pairs={{0,112},{16,96},{32,32},{48,48},{64,64},{80,80},{96,16},{112,0},{1... | collective-permute-start | bytes 61448 | tf_op jit(solution)/shard_map/ppermute | solution.py:709
  28.4 0.1 collective-permute-start
  28.5 5.3 %collective-permute-start.1 = (f32[5,2,32,256]{3,2,1,0:T(8,128)}, f32[5,2,32,256]{3,2,1,0:T(8,128)S(1)}, u32[]{:S(2)}, u32[]{:S(2)}) collective-permute-start(f32[5,2,32,256]{3,2,1,0:T(8,128)} %get-tuple-element.14), channel_id=1, source_target_pairs={{1,0},{2,1},{3,2},{4,3},{5,4},{6,5},{7,6},{8,7},{9,8},{10,9},{11,1... | collective-permute-start | bytes 983048 | tf_op jit(solution)/shard_map/ppermute | solution.py:704
  33.9 0.0 all-to-all-done.slot_ref
  33.9 0.0 copy-done.3
  33.9 0.0 copy-done.7
  33.9 0.0 copy-start
  33.9 0.0 copy-start.1
  33.9 0.0 copy-start.4
  33.9 17.9 %fill.1 = (f32[5,12,16,512]{3,2,1,0:T(8,128)S(1)}, f32[5,2,16,512]{3,2,1,0:T(8,128)S(1)}, f32[5,2,16,512]{3,2,1,0:T(8,128)S(1)}, f32[5,2,12,512]{3,2,1,0:T(8,128)S(1)}, f32[5,2,12,512]{3,2,1,0:T(8,128)S(1)}) custom-call(s32[12,16,512]{2,1,0:T(8,128)S(1)} %bitcast.12, s32[12,16,512]{2,1,0:T(8,128)S(1)} %bitcast.10, f32[5,12,16,512]{3,2,1,0:T(8,128)} %bitcast.16, ...), custom_call_target="tpu_custom_call" | custom-call | flops 24000000000 | bytes 6000000 | tf_op jit(solution)/shard_map/fill/pallas_call | solution.py:673
  51.8 0.0 collective-permute-done.4.refs_3_
  51.8 0.3 collective-permute-start.5
  52.1 0.0 collective-permute-done.2.sub_lo
  52.1 3.9 %collective-permute-start.6 = (f32[5,2,16,512]{3,2,1,0:T(8,128)S(1)}, f32[5,2,16,512]{3,2,1,0:T(8,128)S(1)}, u32[]{:S(2)}, u32[]{:S(2)}) collective-permute-start(f32[5,2,16,512]{3,2,1,0:T(8,128)S(1)} %get-tuple-element.21), channel_id=1, source_target_pairs={{16,0},{32,16},{48,32},{64,48},{80,64},{96,80},{112,96},{0,112},{1... | collective-permute-start | bytes 983048 | tf_op jit(solution)/shard_map/ppermute | solution.py:704
  56.0 0.0 collective-permute-done.3.sub_hi
  56.0 0.0 collective-permute-start.7
  56.0 0.0 collective-permute-done.major_lo
  56.0 0.0 copy-start.2
  56.1 5.3 %collective-permute-start.8 = (f32[5,2,12,512]{3,2,1,0:T(8,128)S(1)}, f32[5,2,12,512]{3,2,1,0:T(8,128)S(1)}, u32[]{:S(2)}, u32[]{:S(2)}) collective-permute-start(f32[5,2,12,512]{3,2,1,0:T(8,128)S(1)} %get-tuple-element.23), channel_id=1, source_target_pairs={{1,0},{2,1},{3,2},{4,3},{5,4},{6,5},{7,6},{8,7},{9,8},{10,9},{11,1... | collective-permute-start | bytes 737288 | tf_op jit(solution)/shard_map/ppermute | solution.py:704
  61.4 0.0 collective-permute-done.1.major_hi
  61.4 9.0 %cgrid_rate.1 = f32[5,16,32,256]{3,2,1,0:T(8,128)} custom-call(f32[5,16,32,256]{3,2,1,0:T(8,128)S(1)} %copy-done, f32[5,2,32,256]{3,2,1,0:T(8,128)S(1)} %collective-permute-done.major_lo, f32[5,2,32,256]{3,2,1,0:T(8,128)S(1)} %collective-permute-done.1.major_hi, f32[5,2,16,256]{3,2,1,0:T(8,128)S(1)} %collective-permute-done.2.sub_lo, ...), custom_call_target="tpu_custom_call" | custom-call | flops 39321600 | bytes 7864320 | tf_op jit(solution)/shard_map/cgrid_rate/pallas_call | solution.py:301
  70.5 0.0 collective-permute-done.7.sub_lo
  70.5 0.0 collective-permute-done.8.sub_hi
  70.5 0.0 collective-permute-done.5.major_lo
  70.5 0.0 collective-permute-done.6.major_hi
  70.5 8.1 %flap_rate.1 = f32[5,12,16,512]{3,2,1,0:T(8,128)} custom-call(f32[5,12,16,512]{3,2,1,0:T(8,128)S(1)} %get-tuple-element.19.q_hbm, f32[5,2,16,512]{3,2,1,0:T(8,128)S(1)} %collective-permute-done.5.major_lo, f32[5,2,16,512]{3,2,1,0:T(8,128)S(1)} %collective-permute-done.6.major_hi, f32[5,2,12,512]{3,2,1,0:T(8,128)S(1)} %collective-permute-done.7.sub_lo, ...), custom_call_target="tpu_custom_call" | custom-call | flops 29491200 | bytes 5898240 | tf_op jit(solution)/shard_map/flap_rate/pallas_call | solution.py:301
  (8 shorter events, 0.0 us)
Async XLA Ops:
  0.6 33.2 %copy-start.3 = (s32[16,12,512]{2,0,1:T(8,128)S(1)}, s32[16,12,512]{2,0,1:T(8,128)}, u32[]{:S(2)}) copy-start(s32[16,12,512]{2,0,1:T(8,128)} %param.12) | copy-start | bytes 1179652
  0.6 33.2 %copy-start.7 = (s32[16,12,512]{2,0,1:T(8,128)S(1)}, s32[16,12,512]{2,0,1:T(8,128)}, u32[]{:S(2)}) copy-start(s32[16,12,512]{2,0,1:T(8,128)} %param.13) | copy-start | bytes 1179652
  14.5 19.4 %all-to-all-start = ((f32[8,5,1024]{2,1,0:T(8,128)}), f32[8,5,1024]{2,1,0:T(8,128)S(1)}, u32[]{:S(2)}, u32[]{:S(2)}) async-start(f32[8,5,1024]{2,1,0:T(8,128)} %get-tuple-element.18), calls=%async_computation | async-start | bytes 524288 | tf_op jit(solution)/shard_map/all_to_all | solution.py:717
  20.4 31.8 %collective-permute-start.2 = (f32[5,2,16,256]{3,2,1,0:T(8,128)}, f32[5,2,16,256]{3,2,1,0:T(8,128)S(1)}, u32[]{:S(2)}, u32[]{:S(2)}) collective-permute-start(f32[5,2,16,256]{3,2,1,0:T(8,128)} %get-tuple-element.15.refs_1_), channel_id=1, source_target_pairs={{0,16},{16,32},{32,48},{48,64},{64,80},{80,96},{96,112},{112,0},{1... | collective-permute-start | bytes 491528 | tf_op jit(solution)/shard_map/ppermute | solution.py:701
  22.4 33.6 %collective-permute-start.3 = (f32[5,2,16,256]{3,2,1,0:T(8,128)}, f32[5,2,16,256]{3,2,1,0:T(8,128)S(1)}, u32[]{:S(2)}, u32[]{:S(2)}) collective-permute-start(f32[5,2,16,256]{3,2,1,0:T(8,128)} %get-tuple-element.16.refs_0_), channel_id=1, source_target_pairs={{16,0},{32,16},{48,32},{64,48},{80,64},{96,80},{112,96},{0,112},{1... | collective-permute-start | bytes 491528 | tf_op jit(solution)/shard_map/ppermute | solution.py:704
  24.5 27.3 %collective-permute-start.4 = (f32[5,32,32]{2,1,0:T(8,128)}, f32[5,32,32]{2,1,0:T(8,128)S(1)}, u32[]{:S(2)}, u32[]{:S(2)}) collective-permute-start(f32[5,32,32]{2,1,0:T(8,128)} %get-tuple-element.17.refs_2_), channel_id=1, source_target_pairs={{0,112},{16,96},{32,32},{48,48},{64,64},{80,80},{96,16},{112,0},{1... | collective-permute-start | bytes 61448 | tf_op jit(solution)/shard_map/ppermute | solution.py:709
  28.4 27.6 %collective-permute-start = (f32[5,2,32,256]{3,2,1,0:T(8,128)}, f32[5,2,32,256]{3,2,1,0:T(8,128)S(1)}, u32[]{:S(2)}, u32[]{:S(2)}) collective-permute-start(f32[5,2,32,256]{3,2,1,0:T(8,128)} %get-tuple-element.13), channel_id=1, source_target_pairs={{0,1},{1,2},{2,3},{3,4},{4,5},{5,6},{6,7},{7,8},{8,9},{9,10},{10,1... | collective-permute-start | bytes 983048 | tf_op jit(solution)/shard_map/ppermute | solution.py:701
  28.5 32.9 %collective-permute-start.1 = (f32[5,2,32,256]{3,2,1,0:T(8,128)}, f32[5,2,32,256]{3,2,1,0:T(8,128)S(1)}, u32[]{:S(2)}, u32[]{:S(2)}) collective-permute-start(f32[5,2,32,256]{3,2,1,0:T(8,128)} %get-tuple-element.14), channel_id=1, source_target_pairs={{1,0},{2,1},{3,2},{4,3},{5,4},{6,5},{7,6},{8,7},{9,8},{10,9},{11,1... | collective-permute-start | bytes 983048 | tf_op jit(solution)/shard_map/ppermute | solution.py:704
  33.9 27.5 %copy-start = (f32[5,16,32,256]{3,2,1,0:T(8,128)S(1)}, f32[5,16,32,256]{3,2,1,0:T(8,128)}, u32[]{:S(2)}) copy-start(f32[5,16,32,256]{3,2,1,0:T(8,128)} %q_hbm.3) | copy-start | bytes 7864324
  33.9 27.5 %copy-start.1 = (f32[3,16,32,256]{3,2,1,0:T(8,128)S(1)}, f32[3,16,32,256]{3,2,1,0:T(8,128)}, u32[]{:S(2)}) copy-start(f32[3,16,32,256]{3,2,1,0:T(8,128)} %refs_4_.1) | copy-start | bytes 4718596
  33.9 27.5 %copy-start.4 = (f32[5,2,16,256]{3,2,1,0:T(8,128)S(1)}, f32[5,2,16,256]{3,2,1,0:T(8,128)}, u32[]{:S(2)}) copy-start(f32[5,2,16,256]{3,2,1,0:T(8,128)} %get-tuple-element.16.refs_0_) | copy-start | bytes 491524
  33.9 27.5 %copy-start.5 = (f32[5,2,16,256]{3,2,1,0:T(8,128)S(1)}, f32[5,2,16,256]{3,2,1,0:T(8,128)}, u32[]{:S(2)}) copy-start(f32[5,2,16,256]{3,2,1,0:T(8,128)} %get-tuple-element.15.refs_1_) | copy-start | bytes 491524
  33.9 27.5 %copy-start.6 = (f32[5,32,32]{2,1,0:T(8,128)S(1)}, f32[5,32,32]{2,1,0:T(8,128)}, u32[]{:S(2)}) copy-start(f32[5,32,32]{2,1,0:T(8,128)} %get-tuple-element.17.refs_2_) | copy-start | bytes 61444
  51.8 18.7 %collective-permute-start.5 = (f32[5,2,16,512]{3,2,1,0:T(8,128)S(1)}, f32[5,2,16,512]{3,2,1,0:T(8,128)S(1)}, u32[]{:S(2)}, u32[]{:S(2)}) collective-permute-start(f32[5,2,16,512]{3,2,1,0:T(8,128)S(1)} %get-tuple-element.20), channel_id=1, source_target_pairs={{0,16},{16,32},{32,48},{48,64},{64,80},{80,96},{96,112},{112,0},{1... | collective-permute-start | bytes 983048 | tf_op jit(solution)/shard_map/ppermute | solution.py:701
  52.1 18.4 %collective-permute-start.6 = (f32[5,2,16,512]{3,2,1,0:T(8,128)S(1)}, f32[5,2,16,512]{3,2,1,0:T(8,128)S(1)}, u32[]{:S(2)}, u32[]{:S(2)}) collective-permute-start(f32[5,2,16,512]{3,2,1,0:T(8,128)S(1)} %get-tuple-element.21), channel_id=1, source_target_pairs={{16,0},{32,16},{48,32},{64,48},{80,64},{96,80},{112,96},{0,112},{1... | collective-permute-start | bytes 983048 | tf_op jit(solution)/shard_map/ppermute | solution.py:704
  56.0 14.4 %collective-permute-start.7 = (f32[5,2,12,512]{3,2,1,0:T(8,128)S(1)}, f32[5,2,12,512]{3,2,1,0:T(8,128)S(1)}, u32[]{:S(2)}, u32[]{:S(2)}) collective-permute-start(f32[5,2,12,512]{3,2,1,0:T(8,128)S(1)} %get-tuple-element.22), channel_id=1, source_target_pairs={{0,1},{1,2},{2,3},{3,4},{4,5},{5,6},{6,7},{7,8},{8,9},{9,10},{10,1... | collective-permute-start | bytes 737288 | tf_op jit(solution)/shard_map/ppermute | solution.py:701
  56.0 14.5 %copy-start.2 = (f32[3,16,12,512]{3,1,2,0:T(8,128)S(1)}, f32[3,16,12,512]{3,1,2,0:T(8,128)}, u32[]{:S(2)}) copy-start(f32[3,16,12,512]{3,1,2,0:T(8,128)} %param.11) | copy-start | bytes 3538948
  56.1 14.4 %collective-permute-start.8 = (f32[5,2,12,512]{3,2,1,0:T(8,128)S(1)}, f32[5,2,12,512]{3,2,1,0:T(8,128)S(1)}, u32[]{:S(2)}, u32[]{:S(2)}) collective-permute-start(f32[5,2,12,512]{3,2,1,0:T(8,128)S(1)} %get-tuple-element.23), channel_id=1, source_target_pairs={{1,0},{2,1},{3,2},{4,3},{5,4},{6,5},{7,6},{8,7},{9,8},{10,9},{11,1... | collective-permute-start | bytes 737288 | tf_op jit(solution)/shard_map/ppermute | solution.py:704

commit v11 on v10

--- a/solution.py
+++ b/solution.py
@@ -742,7 +742,7 @@
         turned(flap_metric),
         mask,
         cgrid=False,
-        step_planes=3,
+        step_planes=4,
         components=(2, 3, 1),
         metric_rows=(1, 0, 2),
     )

time: 79 us -> 78.9 us (level)
  no operation moved by 1% of the time
where the time goes in v11:
time: 78.9 us; the launch traced here: 78.6 us
  Pallas kernels  48.6 us (62%)
  starting transfers between devices  28.9 us (37%)
  between operations  0.98 us (1%)
    pallas_call x1, Pallas kernels, fill(): pl.pallas_call(fill_kernel, grid=(planes,), in_specs=[plane, plane, IN_HB...  17.9 us
    pallas_call x2, Pallas kernels, rate(): pl.pallas_call(functools.partial(rate_kernel, cgrid=cgrid, step_planes=st...  16.9 us
    ppermute x4, starting transfers between devices, back(): return lax.ppermute(value, axis, [(j, i) for i, j in ring(axis)])  16.7 us
    pallas_call x1, Pallas kernels, donors(): pl.pallas_call(donor_kernel, grid=(1,), in_specs=[IN_VMEM, IN_VMEM, IN_HB...  13.8 us
    all_to_all x1, starting transfers between devices, body(): slot = lax.all_to_all(slot, 'wrap', split_axis=0, concat_axis=0, tiled=True)  5.92 us
    ppermute x1, starting transfers between devices, body(): lax.ppermute(wall, 'wrap', [(i, wrap_count - 1 - i if wrapped(i, wrap_cou...  3.89 us
    ppermute x4, starting transfers between devices, onward(): return lax.ppermute(value, axis, ring(axis))  2.42 us
  transfers between devices with their start and end apart: 10, of which 0 were waited for; matrix products, arithmetic and copies ran while one was open for 0% of the time, Pallas kernels for 34%

profile of v11, /device:TPU:0, one launch (start us, length us, event | category | flops | bytes accessed | tf_op | source)
XLA Modules:
  0.0 78.6 jit_solution(456626687445009596)
XLA Ops:
  0.7 13.8 %donors.1 = (f32[8,5,1024]{2,1,0:T(8,128)}, f32[5,2,16,256]{3,2,1,0:T(8,128)}, f32[5,2,16,256]{3,2,1,0:T(8,128)}, f32[5,2,32,256]{3,2,1,0:T(8,128)}, f32[5,2,32,256]{3,2,1,0:T(8,128)}, /*index=5*/f32[5,32,32]{2,1,0:T(8,128)}) custom-call(s32[8,1024]{1,0:T(8,128)} %bitcast.15, f32[3,8,1024]{2,1,0:T(8,128)} %bitcast.14, f32[5,16,32,256]{3,2,1,0:T(8,128)} %q_hbm.3), custom_call_target="tpu_custom_call" | custom-call | tf_op jit(solution)/shard_map/donors/pallas_call | solution.py:567
  14.5 5.9 %all-to-all-start = ((f32[8,5,1024]{2,1,0:T(8,128)}), f32[8,5,1024]{2,1,0:T(8,128)S(1)}, u32[]{:S(2)}, u32[]{:S(2)}) async-start(f32[8,5,1024]{2,1,0:T(8,128)} %get-tuple-element.18), calls=%async_computation | async-start | bytes 524288 | tf_op jit(solution)/shard_map/all_to_all | solution.py:717
  20.4 2.0 %collective-permute-start.2 = (f32[5,2,16,256]{3,2,1,0:T(8,128)}, f32[5,2,16,256]{3,2,1,0:T(8,128)S(1)}, u32[]{:S(2)}, u32[]{:S(2)}) collective-permute-start(f32[5,2,16,256]{3,2,1,0:T(8,128)} %get-tuple-element.15.refs_1_), channel_id=1, source_target_pairs={{0,16},{16,32},{32,48},{48,64},{64,80},{80,96},{96,112},{112,0},{1... | collective-permute-start | bytes 491528 | tf_op jit(solution)/shard_map/ppermute | solution.py:701
  22.4 2.1 %collective-permute-start.3 = (f32[5,2,16,256]{3,2,1,0:T(8,128)}, f32[5,2,16,256]{3,2,1,0:T(8,128)S(1)}, u32[]{:S(2)}, u32[]{:S(2)}) collective-permute-start(f32[5,2,16,256]{3,2,1,0:T(8,128)} %get-tuple-element.16.refs_0_), channel_id=1, source_target_pairs={{16,0},{32,16},{48,32},{64,48},{80,64},{96,80},{112,96},{0,112},{1... | collective-permute-start | bytes 491528 | tf_op jit(solution)/shard_map/ppermute | solution.py:704
  24.5 3.9 %collective-permute-start.4 = (f32[5,32,32]{2,1,0:T(8,128)}, f32[5,32,32]{2,1,0:T(8,128)S(1)}, u32[]{:S(2)}, u32[]{:S(2)}) collective-permute-start(f32[5,32,32]{2,1,0:T(8,128)} %get-tuple-element.17.refs_2_), channel_id=1, source_target_pairs={{0,112},{16,96},{32,32},{48,48},{64,64},{80,80},{96,16},{112,0},{1... | collective-permute-start | bytes 61448 | tf_op jit(solution)/shard_map/ppermute | solution.py:709
  28.4 0.1 collective-permute-start
  28.5 5.3 %collective-permute-start.1 = (f32[5,2,32,256]{3,2,1,0:T(8,128)}, f32[5,2,32,256]{3,2,1,0:T(8,128)S(1)}, u32[]{:S(2)}, u32[]{:S(2)}) collective-permute-start(f32[5,2,32,256]{3,2,1,0:T(8,128)} %get-tuple-element.14), channel_id=1, source_target_pairs={{1,0},{2,1},{3,2},{4,3},{5,4},{6,5},{7,6},{8,7},{9,8},{10,9},{11,1... | collective-permute-start | bytes 983048 | tf_op jit(solution)/shard_map/ppermute | solution.py:704
  33.9 0.0 all-to-all-done.slot_ref
  33.9 0.0 copy-start
  33.9 0.0 copy-start.1
  33.9 0.0 copy-start.4
  33.9 0.0 copy-start.5
  33.9 0.0 copy-start.6
  33.9 17.9 %fill.1 = (f32[5,12,16,512]{3,2,1,0:T(8,128)S(1)}, f32[5,2,16,512]{3,2,1,0:T(8,128)S(1)}, f32[5,2,16,512]{3,2,1,0:T(8,128)S(1)}, f32[5,2,12,512]{3,2,1,0:T(8,128)S(1)}, f32[5,2,12,512]{3,2,1,0:T(8,128)S(1)}) custom-call(s32[12,16,512]{2,1,0:T(8,128)S(1)} %bitcast.12, s32[12,16,512]{2,1,0:T(8,128)S(1)} %bitcast.10, f32[5,12,16,512]{3,2,1,0:T(8,128)} %bitcast.16, ...), custom_call_target="tpu_custom_call" | custom-call | flops 24000000000 | bytes 6000000 | tf_op jit(solution)/shard_map/fill/pallas_call | solution.py:673
  51.8 0.0 collective-permute-done.4.refs_3_
  51.8 0.3 collective-permute-start.5
  52.1 0.0 collective-permute-done.2.sub_lo
  52.1 3.9 %collective-permute-start.6 = (f32[5,2,16,512]{3,2,1,0:T(8,128)S(1)}, f32[5,2,16,512]{3,2,1,0:T(8,128)S(1)}, u32[]{:S(2)}, u32[]{:S(2)}) collective-permute-start(f32[5,2,16,512]{3,2,1,0:T(8,128)S(1)} %get-tuple-element.21), channel_id=1, source_target_pairs={{16,0},{32,16},{48,32},{64,48},{80,64},{96,80},{112,96},{0,112},{1... | collective-permute-start | bytes 983048 | tf_op jit(solution)/shard_map/ppermute | solution.py:704
  56.0 0.0 collective-permute-done.3.sub_hi
  56.0 0.0 collective-permute-start.7
  56.0 0.0 collective-permute-done.major_lo
  56.0 0.0 copy-start.2
  56.1 5.3 %collective-permute-start.8 = (f32[5,2,12,512]{3,2,1,0:T(8,128)S(1)}, f32[5,2,12,512]{3,2,1,0:T(8,128)S(1)}, u32[]{:S(2)}, u32[]{:S(2)}) collective-permute-start(f32[5,2,12,512]{3,2,1,0:T(8,128)S(1)} %get-tuple-element.23), channel_id=1, source_target_pairs={{1,0},{2,1},{3,2},{4,3},{5,4},{6,5},{7,6},{8,7},{9,8},{10,9},{11,1... | collective-permute-start | bytes 737288 | tf_op jit(solution)/shard_map/ppermute | solution.py:704
  61.4 0.0 collective-permute-done.1.major_hi
  61.4 0.0 copy-done
  61.4 9.0 %cgrid_rate.1 = f32[5,16,32,256]{3,2,1,0:T(8,128)} custom-call(f32[5,16,32,256]{3,2,1,0:T(8,128)S(1)} %copy-done, f32[5,2,32,256]{3,2,1,0:T(8,128)S(1)} %collective-permute-done.major_lo, f32[5,2,32,256]{3,2,1,0:T(8,128)S(1)} %collective-permute-done.1.major_hi, f32[5,2,16,256]{3,2,1,0:T(8,128)S(1)} %collective-permute-done.2.sub_lo, ...), custom_call_target="tpu_custom_call" | custom-call | flops 39321600 | bytes 7864320 | tf_op jit(solution)/shard_map/cgrid_rate/pallas_call | solution.py:301
  70.5 0.0 collective-permute-done.7.sub_lo
  70.5 0.0 collective-permute-done.8.sub_hi
  70.5 0.0 collective-permute-done.5.major_lo
  70.5 0.0 collective-permute-done.6.major_hi
  70.5 0.0 copy-done.2
  70.5 7.9 %flap_rate.1 = f32[5,12,16,512]{3,2,1,0:T(8,128)} custom-call(f32[5,12,16,512]{3,2,1,0:T(8,128)S(1)} %get-tuple-element.19.q_hbm, f32[5,2,16,512]{3,2,1,0:T(8,128)S(1)} %collective-permute-done.5.major_lo, f32[5,2,16,512]{3,2,1,0:T(8,128)S(1)} %collective-permute-done.6.major_hi, f32[5,2,12,512]{3,2,1,0:T(8,128)S(1)} %collective-permute-done.7.sub_lo, ...), custom_call_target="tpu_custom_call" | custom-call | flops 29491200 | bytes 5898240 | tf_op jit(solution)/shard_map/flap_rate/pallas_call | solution.py:301
  (8 shorter events, 0.0 us)
Async XLA Ops:
  0.6 33.2 %copy-start.3 = (s32[16,12,512]{2,0,1:T(8,128)S(1)}, s32[16,12,512]{2,0,1:T(8,128)}, u32[]{:S(2)}) copy-start(s32[16,12,512]{2,0,1:T(8,128)} %param.12) | copy-start | bytes 1179652
  0.6 33.2 %copy-start.7 = (s32[16,12,512]{2,0,1:T(8,128)S(1)}, s32[16,12,512]{2,0,1:T(8,128)}, u32[]{:S(2)}) copy-start(s32[16,12,512]{2,0,1:T(8,128)} %param.13) | copy-start | bytes 1179652
  14.5 19.4 %all-to-all-start = ((f32[8,5,1024]{2,1,0:T(8,128)}), f32[8,5,1024]{2,1,0:T(8,128)S(1)}, u32[]{:S(2)}, u32[]{:S(2)}) async-start(f32[8,5,1024]{2,1,0:T(8,128)} %get-tuple-element.18), calls=%async_computation | async-start | bytes 524288 | tf_op jit(solution)/shard_map/all_to_all | solution.py:717
  20.4 31.8 %collective-permute-start.2 = (f32[5,2,16,256]{3,2,1,0:T(8,128)}, f32[5,2,16,256]{3,2,1,0:T(8,128)S(1)}, u32[]{:S(2)}, u32[]{:S(2)}) collective-permute-start(f32[5,2,16,256]{3,2,1,0:T(8,128)} %get-tuple-element.15.refs_1_), channel_id=1, source_target_pairs={{0,16},{16,32},{32,48},{48,64},{64,80},{80,96},{96,112},{112,0},{1... | collective-permute-start | bytes 491528 | tf_op jit(solution)/shard_map/ppermute | solution.py:701
  22.4 33.6 %collective-permute-start.3 = (f32[5,2,16,256]{3,2,1,0:T(8,128)}, f32[5,2,16,256]{3,2,1,0:T(8,128)S(1)}, u32[]{:S(2)}, u32[]{:S(2)}) collective-permute-start(f32[5,2,16,256]{3,2,1,0:T(8,128)} %get-tuple-element.16.refs_0_), channel_id=1, source_target_pairs={{16,0},{32,16},{48,32},{64,48},{80,64},{96,80},{112,96},{0,112},{1... | collective-permute-start | bytes 491528 | tf_op jit(solution)/shard_map/ppermute | solution.py:704
  24.5 27.3 %collective-permute-start.4 = (f32[5,32,32]{2,1,0:T(8,128)}, f32[5,32,32]{2,1,0:T(8,128)S(1)}, u32[]{:S(2)}, u32[]{:S(2)}) collective-permute-start(f32[5,32,32]{2,1,0:T(8,128)} %get-tuple-element.17.refs_2_), channel_id=1, source_target_pairs={{0,112},{16,96},{32,32},{48,48},{64,64},{80,80},{96,16},{112,0},{1... | collective-permute-start | bytes 61448 | tf_op jit(solution)/shard_map/ppermute | solution.py:709
  28.4 27.6 %collective-permute-start = (f32[5,2,32,256]{3,2,1,0:T(8,128)}, f32[5,2,32,256]{3,2,1,0:T(8,128)S(1)}, u32[]{:S(2)}, u32[]{:S(2)}) collective-permute-start(f32[5,2,32,256]{3,2,1,0:T(8,128)} %get-tuple-element.13), channel_id=1, source_target_pairs={{0,1},{1,2},{2,3},{3,4},{4,5},{5,6},{6,7},{7,8},{8,9},{9,10},{10,1... | collective-permute-start | bytes 983048 | tf_op jit(solution)/shard_map/ppermute | solution.py:701
  28.5 32.9 %collective-permute-start.1 = (f32[5,2,32,256]{3,2,1,0:T(8,128)}, f32[5,2,32,256]{3,2,1,0:T(8,128)S(1)}, u32[]{:S(2)}, u32[]{:S(2)}) collective-permute-start(f32[5,2,32,256]{3,2,1,0:T(8,128)} %get-tuple-element.14), channel_id=1, source_target_pairs={{1,0},{2,1},{3,2},{4,3},{5,4},{6,5},{7,6},{8,7},{9,8},{10,9},{11,1... | collective-permute-start | bytes 983048 | tf_op jit(solution)/shard_map/ppermute | solution.py:704
  33.9 27.5 %copy-start = (f32[5,16,32,256]{3,2,1,0:T(8,128)S(1)}, f32[5,16,32,256]{3,2,1,0:T(8,128)}, u32[]{:S(2)}) copy-start(f32[5,16,32,256]{3,2,1,0:T(8,128)} %q_hbm.3) | copy-start | bytes 7864324
  33.9 27.5 %copy-start.1 = (f32[3,16,32,256]{3,2,1,0:T(8,128)S(1)}, f32[3,16,32,256]{3,2,1,0:T(8,128)}, u32[]{:S(2)}) copy-start(f32[3,16,32,256]{3,2,1,0:T(8,128)} %refs_4_.1) | copy-start | bytes 4718596
  33.9 27.5 %copy-start.4 = (f32[5,2,16,256]{3,2,1,0:T(8,128)S(1)}, f32[5,2,16,256]{3,2,1,0:T(8,128)}, u32[]{:S(2)}) copy-start(f32[5,2,16,256]{3,2,1,0:T(8,128)} %get-tuple-element.16.refs_0_) | copy-start | bytes 491524
  33.9 27.5 %copy-start.5 = (f32[5,2,16,256]{3,2,1,0:T(8,128)S(1)}, f32[5,2,16,256]{3,2,1,0:T(8,128)}, u32[]{:S(2)}) copy-start(f32[5,2,16,256]{3,2,1,0:T(8,128)} %get-tuple-element.15.refs_1_) | copy-start | bytes 491524
  33.9 27.5 %copy-start.6 = (f32[5,32,32]{2,1,0:T(8,128)S(1)}, f32[5,32,32]{2,1,0:T(8,128)}, u32[]{:S(2)}) copy-start(f32[5,32,32]{2,1,0:T(8,128)} %get-tuple-element.17.refs_2_) | copy-start | bytes 61444
  51.8 18.7 %collective-permute-start.5 = (f32[5,2,16,512]{3,2,1,0:T(8,128)S(1)}, f32[5,2,16,512]{3,2,1,0:T(8,128)S(1)}, u32[]{:S(2)}, u32[]{:S(2)}) collective-permute-start(f32[5,2,16,512]{3,2,1,0:T(8,128)S(1)} %get-tuple-element.20), channel_id=1, source_target_pairs={{0,16},{16,32},{32,48},{48,64},{64,80},{80,96},{96,112},{112,0},{1... | collective-permute-start | bytes 983048 | tf_op jit(solution)/shard_map/ppermute | solution.py:701
  52.1 18.4 %collective-permute-start.6 = (f32[5,2,16,512]{3,2,1,0:T(8,128)S(1)}, f32[5,2,16,512]{3,2,1,0:T(8,128)S(1)}, u32[]{:S(2)}, u32[]{:S(2)}) collective-permute-start(f32[5,2,16,512]{3,2,1,0:T(8,128)S(1)} %get-tuple-element.21), channel_id=1, source_target_pairs={{16,0},{32,16},{48,32},{64,48},{80,64},{96,80},{112,96},{0,112},{1... | collective-permute-start | bytes 983048 | tf_op jit(solution)/shard_map/ppermute | solution.py:704
  56.0 14.4 %collective-permute-start.7 = (f32[5,2,12,512]{3,2,1,0:T(8,128)S(1)}, f32[5,2,12,512]{3,2,1,0:T(8,128)S(1)}, u32[]{:S(2)}, u32[]{:S(2)}) collective-permute-start(f32[5,2,12,512]{3,2,1,0:T(8,128)S(1)} %get-tuple-element.22), channel_id=1, source_target_pairs={{0,1},{1,2},{2,3},{3,4},{4,5},{5,6},{6,7},{7,8},{8,9},{9,10},{10,1... | collective-permute-start | bytes 737288 | tf_op jit(solution)/shard_map/ppermute | solution.py:701
  56.0 14.5 %copy-start.2 = (f32[3,16,12,512]{3,1,2,0:T(8,128)S(1)}, f32[3,16,12,512]{3,1,2,0:T(8,128)}, u32[]{:S(2)}) copy-start(f32[3,16,12,512]{3,1,2,0:T(8,128)} %param.11) | copy-start | bytes 3538948
  56.1 14.4 %collective-permute-start.8 = (f32[5,2,12,512]{3,2,1,0:T(8,128)S(1)}, f32[5,2,12,512]{3,2,1,0:T(8,128)S(1)}, u32[]{:S(2)}, u32[]{:S(2)}) collective-permute-start(f32[5,2,12,512]{3,2,1,0:T(8,128)S(1)} %get-tuple-element.23), channel_id=1, source_target_pairs={{1,0},{2,1},{3,2},{4,3},{5,4},{6,5},{7,6},{8,7},{9,8},{10,9},{11,1... | collective-permute-start | bytes 737288 | tf_op jit(solution)/shard_map/ppermute | solution.py:704
